TPU v7x, 32 devices: a whole 2x2x4 slice. The times are simulated.
32 devices in a mesh: dp: 4 (over z), ctx: 4 (over x, core), tp: 2 (over y).
Axes of the slice: x: 2, y: 2, z: 4, core: 2. Of those that a mesh axis runs over, the one named last changes fastest.
Arguments:
- inputs: bfloat16 [16, 1024, 2048], P('dp', 'ctx'), may hold values from -6 to 6
- span_order: int32 [16, 8], P('dp'), may hold values from 0 to 7, each once within a row
- first_gain: bfloat16 [2048], P(('dp', 'ctx')), may hold values from 0.099609375 to 1.8984375
- query_proj: bfloat16 [2048, 2048], P(('dp', 'ctx'), 'tp'), may hold values from -0.125 to 0.125
- key_matrix: bfloat16 [2048, 1024], P(('dp', 'ctx'), 'tp'), may hold values from -0.125 to 0.125
- value_matrix: bfloat16 [2048, 1024], P(('dp', 'ctx'), 'tp'), may hold values from -0.125 to 0.125
- query_norm: bfloat16 [128], P(('dp', 'ctx')), may hold values from 0.5 to 2
- key_norm: bfloat16 [128], P(('dp', 'ctx')), may hold values from 0.5 to 2
- output_proj: bfloat16 [2048, 2048], P('tp', ('dp', 'ctx')), may hold values from -1 to 1
- second_gain: bfloat16 [2048], P(('dp', 'ctx')), may hold values from 0.099609375 to 1.8984375
- gate_proj: bfloat16 [2048, 6144], P(('dp', 'ctx'), 'tp'), may hold values from -0.125 to 0.125
- up_proj: bfloat16 [2048, 6144], P(('dp', 'ctx'), 'tp'), may hold values from -0.125 to 0.125
- down_proj: bfloat16 [6144, 2048], P('tp', ('dp', 'ctx')), may hold values from -0.078125 to 0.078125
- cotangent: bfloat16 [16, 1024, 2048], P('dp', 'ctx'), may hold values from -6 to 6
Outputs:
- outputs: bfloat16 [16, 1024, 2048], P('dp', 'ctx')
- input_grad: bfloat16 [16, 1024, 2048], P('dp', 'ctx')
- grad_first: float32 [2048], P(('dp', 'ctx'))
- grad_query: float32 [2048, 2048], P(('dp', 'ctx'), 'tp')
- grad_key: float32 [2048, 1024], P(('dp', 'ctx'), 'tp')
- grad_value: float32 [2048, 1024], P(('dp', 'ctx'), 'tp')
- grad_querynorm: float32 [128], P(('dp', 'ctx'))
- grad_keynorm: float32 [128], P(('dp', 'ctx'))
- grad_output: float32 [2048, 2048], P('tp', ('dp', 'ctx'))
- grad_second: float32 [2048], P(('dp', 'ctx'))
- grad_gate: float32 [2048, 6144], P(('dp', 'ctx'), 'tp')
- grad_upproj: float32 [2048, 6144], P(('dp', 'ctx'), 'tp')
- grad_down: float32 [6144, 2048], P('tp', ('dp', 'ctx'))
Inputs may be any that keep to these rules, and one draw needn't show every extreme that they name: Each row of span_order is a permutation of the 8 spans of a sequence, each of 128 tokens.
All inputs are finite; a program needn't handle non-finite values.
Results may differ from a plain program's by a relative error of at most 0.04.
Values may be sent and summed in bfloat16 or wider, within the bound.
No kernel may reach another device: no remote copies, remote signals or barrier semaphores. Data moves between devices by JAX's collectives and lax.ppermute only.
A program may use at most 320 MiB of HBM per device.

v0:
```python
import jax
import jax.numpy as jnp
from jax import lax
from jax.sharding import PartitionSpec as P

QUERY_HEADS = 16
KEY_HEADS = 8
HEAD_DIM = 128


EPSILON = 1e-06
ROPE_BASE = 1000000.0
MASKED = -1e30


def norm_forward(values, gain):
    inverse = lax.rsqrt(jnp.mean(values * values, axis=-1, keepdims=True) + EPSILON)
    normalized = values * inverse
    return (normalized * gain, normalized, inverse)


def norm_backward(grad_out, gain, normalized, inverse):
    grad_normed = grad_out * gain
    grad_values = inverse * (
        grad_normed - normalized * jnp.mean(grad_normed * normalized, axis=-1, keepdims=True)
    )
    return (grad_values, grad_out * normalized)


def rotary_tables(positions):
    half_dim = HEAD_DIM // 2
    frequency = ROPE_BASE ** (-(jnp.arange(half_dim, dtype=jnp.float32) * (2.0 / HEAD_DIM)))
    angles = positions.astype(jnp.float32)[:, None] * frequency[None, :]
    return (jnp.cos(angles)[:, None, :], jnp.sin(angles)[:, None, :])


def rotate(values, cosine_table, sine_table):
    half_dim = values.shape[-1] // 2
    lower_half = values[..., :half_dim]
    upper_half = values[..., half_dim:]
    return jnp.concatenate(
        [
            lower_half * cosine_table - upper_half * sine_table,
            upper_half * cosine_table + lower_half * sine_table,
        ],
        axis=-1,
    )


def shards(
    inputs,
    span_order,
    first_gain,
    query_proj,
    key_matrix,
    value_matrix,
    query_norm,
    key_norm,
    output_proj,
    second_gain,
    gate_proj,
    up_proj,
    down_proj,
    cotangent,
):
    seq_count, local_len, model_width = inputs.shape
    span_len = local_len // 2
    total_len = local_len * lax.axis_size("ctx")
    heads_per_group = QUERY_HEADS // KEY_HEADS
    score_scale = HEAD_DIM ** (-0.5)
    ctx_index = lax.axis_index("ctx")
    whole_places = (
        span_order[:, :, None] * span_len + jnp.arange(span_len, dtype=jnp.int32)[None, None, :]
    ).reshape(seq_count, total_len)
    local_places = lax.dynamic_slice_in_dim(whole_places, ctx_index * local_len, local_len, 1)
    gathered = (
        lax.all_gather(first_gain, ("dp", "ctx"), axis=0, tiled=True),
        lax.all_gather(query_proj, ("dp", "ctx"), axis=0, tiled=True),
        lax.all_gather(key_matrix, ("dp", "ctx"), axis=0, tiled=True),
        lax.all_gather(value_matrix, ("dp", "ctx"), axis=0, tiled=True),
        lax.all_gather(query_norm, ("dp", "ctx"), axis=0, tiled=True),
        lax.all_gather(key_norm, ("dp", "ctx"), axis=0, tiled=True),
        lax.all_gather(output_proj, ("dp", "ctx"), axis=1, tiled=True),
        lax.all_gather(second_gain, ("dp", "ctx"), axis=0, tiled=True),
        lax.all_gather(gate_proj, ("dp", "ctx"), axis=0, tiled=True),
        lax.all_gather(up_proj, ("dp", "ctx"), axis=0, tiled=True),
        lax.all_gather(down_proj, ("dp", "ctx"), axis=1, tiled=True),
    )
    (
        gain_first,
        full_query,
        full_key,
        full_value,
        gain_query,
        gain_key,
        full_output,
        gain_second,
        full_gate,
        full_upward,
        full_down,
    ) = gathered
    gain_first = gain_first.astype(jnp.float32)
    gain_query = gain_query.astype(jnp.float32)
    gain_key = gain_key.astype(jnp.float32)
    gain_second = gain_second.astype(jnp.float32)
    rows_count = seq_count * local_len
    token_rows = inputs.reshape(rows_count, model_width).astype(jnp.float32)
    normed_one, unit_one, inverse_one = norm_forward(token_rows, gain_first)
    feed_one = normed_one.astype(jnp.bfloat16)
    kv_heads = full_key.shape[1] // HEAD_DIM
    cosine_table, sine_table = rotary_tables(local_places.reshape(-1))
    query_raw = jnp.dot(feed_one, full_query, preferred_element_type=jnp.float32).reshape(
        rows_count, -1, HEAD_DIM
    )
    key_raw = jnp.dot(feed_one, full_key, preferred_element_type=jnp.float32).reshape(
        rows_count, -1, HEAD_DIM
    )
    value_bf = jnp.dot(feed_one, full_value, preferred_element_type=jnp.float32).astype(
        jnp.bfloat16
    )
    value_bf = value_bf.reshape(seq_count, local_len, kv_heads, HEAD_DIM)
    query_scaled, query_unit, query_inverse = norm_forward(query_raw, gain_query)
    key_scaled, key_unit, key_inverse = norm_forward(key_raw, gain_key)
    query_rot = rotate(query_scaled, cosine_table, sine_table).astype(jnp.bfloat16)
    query_rot = query_rot.reshape(seq_count, local_len, kv_heads, heads_per_group, HEAD_DIM)
    key_rot = rotate(key_scaled, cosine_table, sine_table).astype(jnp.bfloat16)
    key_rot = key_rot.reshape(seq_count, local_len, kv_heads, HEAD_DIM)

    def masked_scores(key_piece):
        scores = (
            jnp.einsum(
                "sqkgd,spkd->skgqp", query_rot, key_piece, preferred_element_type=jnp.float32
            )
            * score_scale
        )
        allowed = local_places[:, None, None, :, None] >= whole_places[:, None, None, None, :]
        return jnp.where(allowed, scores, MASKED)

    running_max = jnp.full((seq_count, kv_heads, heads_per_group, local_len), MASKED, jnp.float32)
    key_piece = lax.all_gather(key_rot, "ctx", axis=1, tiled=True)
    value_piece = lax.all_gather(value_bf, "ctx", axis=1, tiled=True)
    scores = masked_scores(key_piece)
    new_max = jnp.maximum(running_max, jnp.max(scores, axis=-1))
    exponent = jnp.exp(scores - new_max[..., None])
    running_sum = jnp.sum(exponent, axis=-1)
    running_acc = jnp.einsum(
        "skgqp,spkd->skgqd",
        exponent.astype(jnp.bfloat16),
        value_piece,
        preferred_element_type=jnp.float32,
    )
    attended = running_acc / running_sum[..., None]
    log_total = new_max + jnp.log(running_sum)
    attended_bf = (
        jnp.transpose(attended, (0, 3, 1, 2, 4)).reshape(rows_count, -1).astype(jnp.bfloat16)
    )
    attn_part = jnp.dot(attended_bf, full_output, preferred_element_type=jnp.float32)
    middle = token_rows + lax.psum(attn_part.astype(jnp.bfloat16), "tp").astype(jnp.float32)
    normed_two, unit_two, inverse_two = norm_forward(middle, gain_second)
    feed_two = normed_two.astype(jnp.bfloat16)
    gate_act = jnp.dot(feed_two, full_gate, preferred_element_type=jnp.float32)
    upward = jnp.dot(feed_two, full_upward, preferred_element_type=jnp.float32)
    gate_sigmoid = jax.nn.sigmoid(gate_act)
    hidden = (gate_act * gate_sigmoid * upward).astype(jnp.bfloat16)
    down_part = jnp.dot(hidden, full_down, preferred_element_type=jnp.float32)
    mlp_out = lax.psum(down_part.astype(jnp.bfloat16), "tp").astype(jnp.float32)
    outputs = (middle + mlp_out).astype(jnp.bfloat16).reshape(inputs.shape)
    regathered = (
        lax.all_gather(first_gain, ("dp", "ctx"), axis=0, tiled=True),
        lax.all_gather(query_proj, ("dp", "ctx"), axis=0, tiled=True),
        lax.all_gather(key_matrix, ("dp", "ctx"), axis=0, tiled=True),
        lax.all_gather(value_matrix, ("dp", "ctx"), axis=0, tiled=True),
        lax.all_gather(query_norm, ("dp", "ctx"), axis=0, tiled=True),
        lax.all_gather(key_norm, ("dp", "ctx"), axis=0, tiled=True),
        lax.all_gather(output_proj, ("dp", "ctx"), axis=1, tiled=True),
        lax.all_gather(second_gain, ("dp", "ctx"), axis=0, tiled=True),
        lax.all_gather(gate_proj, ("dp", "ctx"), axis=0, tiled=True),
        lax.all_gather(up_proj, ("dp", "ctx"), axis=0, tiled=True),
        lax.all_gather(down_proj, ("dp", "ctx"), axis=1, tiled=True),
    )
    (
        spare_first,
        back_query,
        back_key,
        back_value,
        spare_query,
        spare_key,
        back_output,
        spare_second,
        back_gate,
        back_upward,
        back_down,
    ) = regathered
    cot_rows = cotangent.reshape(rows_count, model_width)
    grad_hidden = jnp.einsum("nd,fd->nf", cot_rows, back_down, preferred_element_type=jnp.float32)
    grad_down = jnp.einsum("nf,nd->fd", hidden, cot_rows, preferred_element_type=jnp.float32)
    silu_slope = gate_sigmoid * (1.0 + gate_act * (1.0 - gate_sigmoid))
    gate_back = (grad_hidden * upward * silu_slope).astype(jnp.bfloat16)
    up_back = (grad_hidden * gate_act * gate_sigmoid).astype(jnp.bfloat16)
    grad_gate = jnp.einsum("nd,nf->df", feed_two, gate_back, preferred_element_type=jnp.float32)
    grad_upproj = jnp.einsum("nd,nf->df", feed_two, up_back, preferred_element_type=jnp.float32)
    back_two = jnp.einsum(
        "nf,df->nd", gate_back, back_gate, preferred_element_type=jnp.float32
    ) + jnp.einsum("nf,df->nd", up_back, back_upward, preferred_element_type=jnp.float32)
    back_two = lax.psum(back_two.astype(jnp.bfloat16), "tp").astype(jnp.float32)
    grad_middle_norm, second_terms = norm_backward(back_two, gain_second, unit_two, inverse_two)
    grad_second = jnp.sum(second_terms, axis=0)
    grad_middle = cot_rows.astype(jnp.float32) + grad_middle_norm
    middle_low = grad_middle.astype(jnp.bfloat16)
    grad_output = jnp.einsum(
        "nc,nd->cd", attended_bf, middle_low, preferred_element_type=jnp.float32
    )
    grad_attended = jnp.einsum(
        "nd,cd->nc", middle_low, back_output, preferred_element_type=jnp.float32
    ).astype(jnp.bfloat16)
    grad_att = grad_attended.reshape(seq_count, local_len, kv_heads, heads_per_group, HEAD_DIM)
    row_delta = jnp.sum(
        jnp.transpose(grad_att, (0, 2, 3, 1, 4)).astype(jnp.float32) * attended, axis=-1
    )
    key_piece = lax.all_gather(key_rot, "ctx", axis=1, tiled=True)
    value_piece = lax.all_gather(value_bf, "ctx", axis=1, tiled=True)
    scores = masked_scores(key_piece)
    probability = jnp.exp(scores - log_total[..., None])
    grad_prob = jnp.einsum(
        "sqkgd,spkd->skgqp", grad_att, value_piece, preferred_element_type=jnp.float32
    )
    grad_scores = (probability * (grad_prob - row_delta[..., None])).astype(jnp.bfloat16)
    grad_query_acc = (
        jnp.einsum("skgqp,spkd->sqkgd", grad_scores, key_piece, preferred_element_type=jnp.float32)
        * score_scale
    )
    key_term = (
        jnp.einsum("skgqp,sqkgd->spkd", grad_scores, query_rot, preferred_element_type=jnp.float32)
        * score_scale
    )
    value_term = jnp.einsum(
        "skgqp,sqkgd->spkd",
        probability.astype(jnp.bfloat16),
        grad_att,
        preferred_element_type=jnp.float32,
    )
    key_full = key_term
    value_full = value_term
    grad_qrot, key_full, value_full = (grad_query_acc, key_full, value_full)
    grad_krot, grad_vfull = (
        lax.psum_scatter(
            key_full.astype(jnp.bfloat16), "ctx", scatter_dimension=1, tiled=True
        ).astype(jnp.float32),
        lax.psum_scatter(
            value_full.astype(jnp.bfloat16), "ctx", scatter_dimension=1, tiled=True
        ).astype(jnp.float32),
    )
    query_turned = rotate(grad_qrot.reshape(rows_count, -1, HEAD_DIM), cosine_table, -sine_table)
    query_grad_raw, query_terms = norm_backward(query_turned, gain_query, query_unit, query_inverse)
    query_back = query_grad_raw.astype(jnp.bfloat16).reshape(rows_count, -1)
    key_turned = rotate(grad_krot.reshape(rows_count, -1, HEAD_DIM), cosine_table, -sine_table)
    key_grad_raw, key_terms = norm_backward(key_turned, gain_key, key_unit, key_inverse)
    key_back = key_grad_raw.astype(jnp.bfloat16).reshape(rows_count, -1)
    value_back = grad_vfull.astype(jnp.bfloat16).reshape(rows_count, -1)
    grad_query = jnp.einsum("nd,nc->dc", feed_one, query_back, preferred_element_type=jnp.float32)
    grad_key = jnp.einsum("nd,nc->dc", feed_one, key_back, preferred_element_type=jnp.float32)
    grad_value = jnp.einsum("nd,nc->dc", feed_one, value_back, preferred_element_type=jnp.float32)
    back_one = (
        jnp.einsum("nc,dc->nd", query_back, back_query, preferred_element_type=jnp.float32)
        + jnp.einsum("nc,dc->nd", key_back, back_key, preferred_element_type=jnp.float32)
        + jnp.einsum("nc,dc->nd", value_back, back_value, preferred_element_type=jnp.float32)
    )
    back_one, query_gain_sum, key_gain_sum = (
        lax.psum(back_one.astype(jnp.bfloat16), "tp").astype(jnp.float32),
        lax.psum(jnp.sum(query_terms, axis=(0, 1)).astype(jnp.bfloat16), "tp").astype(jnp.float32),
        lax.psum(jnp.sum(key_terms, axis=(0, 1)).astype(jnp.bfloat16), "tp").astype(jnp.float32),
    )
    grad_input_norm, first_terms = norm_backward(back_one, gain_first, unit_one, inverse_one)
    grad_first = jnp.sum(first_terms, axis=0)
    input_grad = (grad_middle + grad_input_norm).astype(jnp.bfloat16).reshape(inputs.shape)
    results = (
        lax.psum_scatter(
            grad_first.astype(jnp.bfloat16), ("dp", "ctx"), scatter_dimension=0, tiled=True
        ).astype(jnp.float32),
        lax.psum_scatter(
            grad_query.astype(jnp.bfloat16), ("dp", "ctx"), scatter_dimension=0, tiled=True
        ).astype(jnp.float32),
        lax.psum_scatter(
            grad_key.astype(jnp.bfloat16), ("dp", "ctx"), scatter_dimension=0, tiled=True
        ).astype(jnp.float32),
        lax.psum_scatter(
            grad_value.astype(jnp.bfloat16), ("dp", "ctx"), scatter_dimension=0, tiled=True
        ).astype(jnp.float32),
        lax.psum_scatter(
            query_gain_sum.astype(jnp.bfloat16), ("dp", "ctx"), scatter_dimension=0, tiled=True
        ).astype(jnp.float32),
        lax.psum_scatter(
            key_gain_sum.astype(jnp.bfloat16), ("dp", "ctx"), scatter_dimension=0, tiled=True
        ).astype(jnp.float32),
        lax.psum_scatter(
            grad_output.astype(jnp.bfloat16), ("dp", "ctx"), scatter_dimension=1, tiled=True
        ).astype(jnp.float32),
        lax.psum_scatter(
            grad_second.astype(jnp.bfloat16), ("dp", "ctx"), scatter_dimension=0, tiled=True
        ).astype(jnp.float32),
        lax.psum_scatter(
            grad_gate.astype(jnp.bfloat16), ("dp", "ctx"), scatter_dimension=0, tiled=True
        ).astype(jnp.float32),
        lax.psum_scatter(
            grad_upproj.astype(jnp.bfloat16), ("dp", "ctx"), scatter_dimension=0, tiled=True
        ).astype(jnp.float32),
        lax.psum_scatter(
            grad_down.astype(jnp.bfloat16), ("dp", "ctx"), scatter_dimension=1, tiled=True
        ).astype(jnp.float32),
    )
    return (
        outputs,
        input_grad,
        results[0],
        results[1],
        results[2],
        results[3],
        results[4],
        results[5],
        results[6],
        results[7],
        results[8],
        results[9],
        results[10],
    )


def solution(mesh):
    in_specs = (
        P("dp", "ctx", None),
        P("dp", None),
        P(("dp", "ctx")),
        P(("dp", "ctx"), "tp"),
        P(("dp", "ctx"), "tp"),
        P(("dp", "ctx"), "tp"),
        P(("dp", "ctx")),
        P(("dp", "ctx")),
        P("tp", ("dp", "ctx")),
        P(("dp", "ctx")),
        P(("dp", "ctx"), "tp"),
        P(("dp", "ctx"), "tp"),
        P("tp", ("dp", "ctx")),
        P("dp", "ctx", None),
    )
    out_specs = (
        P("dp", "ctx", None),
        P("dp", "ctx", None),
        P(("dp", "ctx")),
        P(("dp", "ctx"), "tp"),
        P(("dp", "ctx"), "tp"),
        P(("dp", "ctx"), "tp"),
        P(("dp", "ctx")),
        P(("dp", "ctx")),
        P("tp", ("dp", "ctx")),
        P(("dp", "ctx")),
        P(("dp", "ctx"), "tp"),
        P(("dp", "ctx"), "tp"),
        P("tp", ("dp", "ctx")),
    )
    return jax.shard_map(shards, mesh=mesh, in_specs=in_specs, out_specs=out_specs, check_vma=False)
```

profile of v0, /device:TPU:0, one launch (start us, length us, event | category | flops | bytes accessed | tf_op | source)
XLA Modules:
  0.0 1939.3 jit_solution(3205209632538053472)
XLA Ops:
  9.5 23.1 %all-gather = bf16[16,1,128]{2,1,0:T(2,128)(2,1)S(1)} all-gather(bf16[1,1,128]{2,1,0:T(2,128)(2,1)} %bitcast.239), channel_id=1, replica_groups=mesh['dp'=4,'ctx'=4,'tp'=2] {'dp','ctx'}, dimensions={0}, use_global_device_ids=true | all-gather | bytes 4352 | tf_op jit(solution)/shard_map/all_gather | solution.py:77
  36.3 30.1 %all-reduce.7 = (bf16[128]{0:T(256)(128)(2,1)S(1)}, bf16[128]{0:T(256)(128)(2,1)S(1)}) all-reduce(bf16[128]{0:T(256)(128)(2,1)S(1)} %dynamic-update-slice, bf16[128]{0:T(256)(128)(2,1)S(1)} %dynamic-update-slice.1), channel_id=1, replica_groups=mesh['dp'=4,'ctx'=4,'tp'=2] {'dp','ctx'}, use_global_device_ids=true, to_apply=%add | all-reduce | flops 256 | bytes 1024
  105.3 42.9 %all-gather.16.cloned.1.call-done = bf16[2048,1024]{1,0:T(8,128)(2,1)} async-done(((bf16[128,1024]{1,0:T(8,128)(2,1)}), bf16[2048,1024]{1,0:T(8,128)(2,1)}) %all-gather.16.cloned.1.call-update) | async-done | bytes 4194320 | tf_op jit(solution)/shard_map/all_gather | solution.py:78
  183.3 17.6 fusion.5
  219.7 18.3 fusion.45
  245.5 29.5 %all-gather.22.cloned.1.call-done = bf16[1024,2048]{1,0:T(8,128)(2,1)} async-done(((bf16[1024,128]{1,0:T(8,128)(2,1)}), bf16[1024,2048]{1,0:T(8,128)(2,1)}) %all-gather.22.cloned.1.call-update) | async-done | bytes 4194320 | tf_op jit(solution)/shard_map/all_gather | solution.py:83
  286.5 18.6 all-gather.1
  305.1 85.5 %all-reduce.14.cloned.1.call-done = bf16[1024,2048]{1,0:T(8,128)(2,1)} async-done(((bf16[1024,2048]{1,0:T(8,128)(2,1)}), bf16[1024,2048]{1,0:T(8,128)(2,1)}) %all-reduce.14.cloned.1.call-update) | async-done | bytes 4194320 | tf_op jit(solution)/shard_map/psum | solution.py:158
  400.7 93.2 %all-gather.24.cloned.1.call-done = bf16[2048,3072]{1,0:T(8,128)(2,1)} async-done(((bf16[128,3072]{1,0:T(8,128)(2,1)}), bf16[2048,3072]{1,0:T(8,128)(2,1)}) %all-gather.24.cloned.1.call-update) | async-done | bytes 12582928 | tf_op jit(solution)/shard_map/all_gather | solution.py:85
  493.9 18.9 fusion.69
  512.9 82.6 %all-gather.26.cloned.1.call-done = bf16[2048,3072]{1,0:T(8,128)(2,1)} async-done(((bf16[128,3072]{1,0:T(8,128)(2,1)}), bf16[2048,3072]{1,0:T(8,128)(2,1)}) %all-gather.26.cloned.1.call-update) | async-done | bytes 12582928 | tf_op jit(solution)/shard_map/all_gather | solution.py:86
  595.4 19.2 fusion.70
  614.6 85.2 %all-gather.28.cloned.1.call-done = bf16[3072,2048]{1,0:T(8,128)(2,1)} async-done(((bf16[3072,128]{1,0:T(8,128)(2,1)}), bf16[3072,2048]{1,0:T(8,128)(2,1)}) %all-gather.28.cloned.1.call-update) | async-done | bytes 12582928 | tf_op jit(solution)/shard_map/all_gather | solution.py:87
  699.8 28.8 %multiply_convert_fusion = (bf16[1024,3072]{1,0:T(8,128)(2,1)}, bf16[1024,3072]{1,0:T(8,128)(2,1)}, bf16[1024,3072]{1,0:T(8,128)(2,1)}) fusion(f32[1024,3072]{1,0:T(8,128)} %fusion.69, f32[1024,3072]{1,0:T(8,128)} %fusion.70, bf16[1024,2048]{1,0:T(8,128)(2,1)} %bitcast.215, bf16[3072,2048]{1,0:T(8,128)(2,1)} %all-gather.28.cloned.1.call-done), kind=kOutput, calls=%fused_computation.17 | convolution fusion | flops 12935233536 | bytes 60817408 | tf_op jit(solution)/shard_map/nd,fd->nf/dot_general | solution.py:195
  728.6 19.1 fusion.71
  747.7 19.1 add_convert_fusion.1
  767.6 105.4 %all-reduce.16.cloned.1.call-done = bf16[1024,2048]{1,0:T(8,128)(2,1)} async-done(((bf16[1024,2048]{1,0:T(8,128)(2,1)}), bf16[1024,2048]{1,0:T(8,128)(2,1)}) %all-reduce.16.cloned.1.call-update) | async-done | bytes 4194320 | tf_op jit(solution)/shard_map/psum | solution.py:205
  904.1 17.2 fusion.37
  924.9 22.7 %fusion.1 = bf16[4,4,2,256,1024]{3,4,2,1,0:T(8,128)(2,1)} fusion(f32[4,4,1024,256,2]{3,2,4,1,0:T(8,128)} %get-tuple-element.58, f32[4,4,2,256]{3,2,1,0:T(2,128)S(1)} %fusion.44, f32[4,4,2,256]{3,2,1,0:T(2,128)S(1)} %log_add_fusion, pred[4,256,1024]{1,2,0:T(8,128)(4,1)S(1)} %copy-done.14, bf16[4,256,4,2,128]{1,4,3,2,0:T(8,128)(2,1)} %copy-done.15, ...), kind=kOutput, calls=%fused_computation.2 | convolution fusion | flops 2197815296 | bytes 57737216 | tf_op jit(solution)/shard_map/sqkgd,spkd->skgqp/dot_general | solution.py:224
  1029.7 19.7 %convolution_convert_fusion = bf16[3072,2048]{1,0:T(8,128)(2,1)} fusion(bf16[1024,3072]{1,0:T(8,128)(2,1)} %get-tuple-element.35, bf16[1024,2048]{1,0:T(8,128)(2,1)} %bitcast.216), kind=kOutput, calls=%fused_computation.21 | convolution fusion | flops 12891193344 | bytes 23068672 | tf_op jit(solution)/shard_map/nf,nd->fd/dot_general | solution.py:196
  1049.4 16.7 copy.103
  1066.4 19.5 %convolution_convert_fusion.2 = bf16[2048,3072]{1,0:T(8,128)(2,1)} fusion(bf16[1024,2048]{1,0:T(8,128)(2,1)} %multiply_convert_fusion.3, bf16[1024,3072]{1,0:T(8,128)(2,1)} %get-tuple-element.34), kind=kOutput, calls=%fused_computation.23 | convolution fusion | flops 12891193344 | bytes 23068672 | tf_op jit(solution)/shard_map/nd,nf->df/dot_general | solution.py:200
  1085.9 19.6 %convolution_convert_fusion.3 = bf16[1024,2048]{1,0:T(8,128)(2,1)} fusion(bf16[1024,3072]{1,0:T(8,128)(2,1)} %get-tuple-element.35, bf16[3072,2048]{1,0:T(8,128)(2,1)} %all-gather.28.cloned.1.call-done), kind=kOutput, calls=%fused_computation.78 | convolution fusion | flops 12886999040 | bytes 23068672 | tf_op jit(solution)/shard_map/dot_general | solution.py:165
  1118.7 19.7 %convolution_convert_fusion.1 = bf16[2048,3072]{1,0:T(8,128)(2,1)} fusion(bf16[1024,2048]{1,0:T(8,128)(2,1)} %multiply_convert_fusion.3, bf16[1024,3072]{1,0:T(8,128)(2,1)} %get-tuple-element.33), kind=kOutput, calls=%fused_computation.22 | convolution fusion | flops 12891193344 | bytes 23068672 | tf_op jit(solution)/shard_map/nd,nf->df/dot_general | solution.py:201
  1141.8 23.6 %reduce-scatter.18.cloned.1.call-done = bf16[128,1024]{1,0:T(8,128)(2,1)} async-done(((bf16[2048,1024]{1,0:T(8,128)(2,1)}), bf16[128,1024]{1,0:T(8,128)(2,1)}) %reduce-scatter.18.cloned.1.call-update) | async-done | bytes 262160 | tf_op jit(solution)/shard_map/reduce_scatter | solution.py:280
  1167.2 62.5 %reduce-scatter.22.cloned.1.call-done = bf16[128,512]{1,0:T(8,128)(2,1)} async-done(((bf16[2048,512]{1,0:T(8,128)(2,1)}), bf16[128,512]{1,0:T(8,128)(2,1)}) %reduce-scatter.22.cloned.1.call-update) | async-done | bytes 131088 | tf_op jit(solution)/shard_map/reduce_scatter | solution.py:286
  1231.3 63.0 %reduce-scatter.20.cloned.1.call-done = bf16[128,512]{1,0:T(8,128)(2,1)} async-done(((bf16[2048,512]{1,0:T(8,128)(2,1)}), bf16[128,512]{1,0:T(8,128)(2,1)}) %reduce-scatter.20.cloned.1.call-update) | async-done | bytes 131088 | tf_op jit(solution)/shard_map/reduce_scatter | solution.py:283
  1295.9 135.9 %reduce-scatter.30.cloned.1.call-done = bf16[128,3072]{1,0:T(8,128)(2,1)} async-done(((bf16[2048,3072]{1,0:T(8,128)(2,1)}), bf16[128,3072]{1,0:T(8,128)(2,1)}) %reduce-scatter.30.cloned.1.call-update) | async-done | bytes 786448
  1434.6 135.1 %reduce-scatter.24.cloned.1.call-done = bf16[128,3072]{1,0:T(8,128)(2,1)} async-done(((bf16[2048,3072]{1,0:T(8,128)(2,1)}), bf16[128,3072]{1,0:T(8,128)(2,1)}) %reduce-scatter.24.cloned.1.call-update) | async-done | bytes 786448 | tf_op jit(solution)/shard_map/reduce_scatter | solution.py:301
  1572.1 198.2 %all-reduce.18.cloned.1.call-done = (bf16[1024,2048]{1,0:T(8,128)(2,1)}, bf16[1024,2048]{1,0:T(8,128)(2,1)}) async-done(((bf16[1024,2048]{1,0:T(8,128)(2,1)}, bf16[1024,2048]{1,0:T(8,128)(2,1)}), (bf16[1024,2048]{1,0:T(8,128)(2,1)}, bf16[1024,2048]{1,0:T(8,128)(2,1)})) %all-reduce.18.cloned.1.call-update) | async-done | bytes 8388624 | tf_op jit(solution)/shard_map/psum | solution.py:166
  1775.4 34.2 %all-reduce.6 = (bf16[2048]{0:T(1024)(128)(2,1)S(1)}, bf16[128]{0:T(256)(128)(2,1)S(1)}, bf16[128]{0:T(256)(128)(2,1)S(1)}, bf16[2048]{0:T(1024)(128)(2,1)S(1)}) all-reduce(bf16[2048]{0:T(1024)(128)(2,1)S(1)} %get-tuple-element.17, bf16[128]{0:T(256)(128)(2,1)S(1)} %copy-done.47, ...), channel_id=4, replica_groups=mesh['dp'=4,'ctx'=4,'tp'=2] {'dp','ctx'}, use_global_device_ids=true, to_apply=%region_18.19.clone | all-reduce | flops 4352 | bytes 17408
  1809.7 99.7 %reduce-scatter.26.cloned.1.call-done = bf16[128,3072]{1,0:T(8,128)(2,1)} async-done(((bf16[2048,3072]{1,0:T(8,128)(2,1)}), bf16[128,3072]{1,0:T(8,128)(2,1)}) %reduce-scatter.26.cloned.1.call-update) | async-done | bytes 786448 | tf_op jit(solution)/shard_map/reduce_scatter | solution.py:304
  (255 shorter events, 297.2 us)
Async XLA Ops:
  7.2 68.5 %all-gather.12.cloned.1.call-start = ((), (), s32[]{:S(2)}) async-start(), calls=%async_computation.9 | async-start | bytes 2228224 | tf_op jit(solution)/shard_map/all_gather | solution.py:79
  7.9 88.8 %all-gather.18.cloned.1.call-start = ((), (), s32[]{:S(2)}) async-start(), calls=%async_computation.12 | async-start | bytes 2228224 | tf_op jit(solution)/shard_map/all_gather | solution.py:80
  8.7 139.6 %all-gather.16.cloned.1.call-start = ((), (), s32[]{:S(2)}) async-start(), calls=%async_computation.11 | async-start | bytes 4456448 | tf_op jit(solution)/shard_map/all_gather | solution.py:78
  9.4 173.9 %all-gather.14.cloned.1.call-start = ((), (), s32[]{:S(2)}) async-start(), calls=%async_computation.10 | async-start | bytes 5242880 | tf_op jit(solution)/shard_map/all_gather | solution.py:140
  32.6 56.7 %copy-start.34 = (f32[16,1,128]{2,1,0:T(1,128)}, f32[16,1,128]{2,1,0:T(1,128)S(1)}, u32[]{:S(2)}) copy-start(f32[16,1,128]{2,1,0:T(1,128)S(1)} %convert_element_type.285) | copy-start | bytes 24580
  72.6 92.1 %copy-start.16 = (f32[1024,64]{0,1:T(8,128)}, f32[1024,64]{0,1:T(8,128)S(1)}, u32[]{:S(2)}) copy-start(f32[1024,64]{0,1:T(8,128)S(1)} %get-tuple-element.48) | copy-start | bytes 786436
  89.3 130.5 %all-gather.20.cloned.1.call-start = ((), (), s32[]{:S(2)}) async-start(), calls=%async_computation.13 | async-start | bytes 5242880 | tf_op jit(solution)/shard_map/all_gather | solution.py:141
  103.6 171.4 %all-gather.22.cloned.1.call-start = ((), (), s32[]{:S(2)}) async-start(), calls=%async_computation.14 | async-start | bytes 4456448 | tf_op jit(solution)/shard_map/all_gather | solution.py:83
  104.2 286.4 %all-reduce.14.cloned.1.call-start = ((), (), s32[]{:S(2)}) async-start(), calls=%async_computation.15 | async-start | bytes 8388608 | tf_op jit(solution)/shard_map/psum | solution.py:158
  104.5 58.5 %copy-start.45 = (f32[128]{0:T(128)}, f32[128]{0:T(128)S(1)}, u32[]{:S(2)}) copy-start(f32[128]{0:T(128)S(1)} %convert_element_type.227) | copy-start | bytes 1540
  105.3 114.4 %copy-start.13 = (pred[4,256,1024]{1,2,0:T(8,128)(4,1)}, pred[4,256,1024]{1,2,0:T(8,128)(4,1)S(1)}, u32[]{:S(2)}) copy-start(pred[4,256,1024]{1,2,0:T(8,128)(4,1)S(1)} %broadcast_compare_fusion) | copy-start | bytes 3145732
  171.4 29.5 %copy-start.8 = (bf16[4,256,4,2,64]{4,1,3,2,0:T(8,128)(2,1)}, bf16[4,256,4,2,64]{4,1,3,2,0:T(8,128)(2,1)S(1)}, u32[]{:S(2)}) copy-start(bf16[4,256,4,2,64]{4,1,3,2,0:T(8,128)(2,1)S(1)} %copy.69) | copy-start | bytes 3145732
  215.2 22.8 %copy-start.30 = (f32[4,4,2,256]{3,2,1,0:T(2,128)}, f32[4,4,2,256]{3,2,1,0:T(2,128)S(1)}, u32[]{:S(2)}) copy-start(f32[4,4,2,256]{3,2,1,0:T(2,128)S(1)} %fusion.2) | copy-start | bytes 98308
  284.4 209.5 %all-gather.24.cloned.1.call-start = ((), (), s32[]{:S(2)}) async-start(), calls=%async_computation.16 | async-start | bytes 13369344 | tf_op jit(solution)/shard_map/all_gather | solution.py:85
  285.1 310.3 %all-gather.26.cloned.1.call-start = ((), (), s32[]{:S(2)}) async-start(), calls=%async_computation.17 | async-start | bytes 13369344 | tf_op jit(solution)/shard_map/all_gather | solution.py:86
  285.9 413.9 %all-gather.28.cloned.1.call-start = ((), (), s32[]{:S(2)}) async-start(), calls=%async_computation.18 | async-start | bytes 13369344 | tf_op jit(solution)/shard_map/all_gather | solution.py:87
  286.5 586.6 %all-reduce.16.cloned.1.call-start = ((), (), s32[]{:S(2)}) async-start(), calls=%async_computation.19 | async-start | bytes 8388608 | tf_op jit(solution)/shard_map/psum | solution.py:205
  305.1 90.5 %copy-start.36 = (f32[16,1,128]{2,1,0:T(1,128)}, f32[16,1,128]{2,1,0:T(1,128)S(1)}, u32[]{:S(2)}) copy-start(f32[16,1,128]{2,1,0:T(1,128)S(1)} %convert_element_type.286) | copy-start | bytes 24580
  766.8 106.2 %copy-start.37 = (f32[16,1,128]{2,1,0:T(1,128)S(1)}, f32[16,1,128]{2,1,0:T(1,128)}, u32[]{:S(2)}) copy-start(f32[16,1,128]{2,1,0:T(1,128)} %copy-done.36) | copy-start | bytes 24580
  766.8 106.2 %copy-start.39 = (f32[1024]{0:T(1024)S(1)}, f32[1024]{0:T(1024)}, u32[]{:S(2)}) copy-start(f32[1024]{0:T(1024)} %copy-done.38) | copy-start | bytes 12292
  766.8 245.8 %reduce-scatter.16.cloned.1.call-start = ((), (), s32[]{:S(2)}) async-start(), calls=%async_computation.21 | async-start | bytes 5242880 | tf_op jit(solution)/shard_map/reduce_scatter | solution.py:249
  921.4 98.8 %reduce-scatter.14.cloned.1.call-start = ((), (), s32[]{:S(2)}) async-start(), calls=%async_computation.20 | async-start | bytes 5242880 | tf_op jit(solution)/shard_map/reduce_scatter | solution.py:246
  958.8 181.0 %reduce-scatter.28.cloned.1.call-start = ((), (), s32[]{:S(2)}) async-start(), calls=%async_computation.27 | async-start | bytes 4456448
  976.4 189.0 %reduce-scatter.18.cloned.1.call-start = ((), (), s32[]{:S(2)}) async-start(), calls=%async_computation.22 | async-start | bytes 4456448 | tf_op jit(solution)/shard_map/reduce_scatter | solution.py:280
  1012.0 217.6 %reduce-scatter.22.cloned.1.call-start = ((), (), s32[]{:S(2)}) async-start(), calls=%async_computation.24 | async-start | bytes 2228224 | tf_op jit(solution)/shard_map/reduce_scatter | solution.py:286
  1020.2 274.1 %reduce-scatter.20.cloned.1.call-start = ((), (), s32[]{:S(2)}) async-start(), calls=%async_computation.23 | async-start | bytes 2228224 | tf_op jit(solution)/shard_map/reduce_scatter | solution.py:283
  1029.7 402.2 %reduce-scatter.30.cloned.1.call-start = ((), (), s32[]{:S(2)}) async-start(), calls=%async_computation.28 | async-start | bytes 13369344
  1066.1 503.6 %reduce-scatter.24.cloned.1.call-start = ((), (), s32[]{:S(2)}) async-start(), calls=%async_computation.25 | async-start | bytes 13369344 | tf_op jit(solution)/shard_map/reduce_scatter | solution.py:301
  1085.9 684.5 %all-reduce.18.cloned.1.call-start = ((), (), s32[]{:S(2)}) async-start(), calls=%async_computation.29 | async-start | bytes 16777216 | tf_op jit(solution)/shard_map/psum | solution.py:166
  1118.7 790.7 %reduce-scatter.26.cloned.1.call-start = ((), (), s32[]{:S(2)}) async-start(), calls=%async_computation.26 | async-start | bytes 13369344 | tf_op jit(solution)/shard_map/reduce_scatter | solution.py:304
  1140.9 629.4 %copy-start.35 = (f32[16,1,128]{2,1,0:T(1,128)S(1)}, f32[16,1,128]{2,1,0:T(1,128)}, u32[]{:S(2)}) copy-start(f32[16,1,128]{2,1,0:T(1,128)} %copy-done.34) | copy-start | bytes 24580
  1141.0 629.4 %copy-start.41 = (f32[1,2,4,128]{3,1,2,0:T(2,128)S(1)}, f32[1,2,4,128]{3,1,2,0:T(2,128)}, u32[]{:S(2)}) copy-start(f32[1,2,4,128]{3,1,2,0:T(2,128)} %copy-done.40) | copy-start | bytes 12292
  (41 other events, 263.7 us)
Sparse Core Ops, SparseCore 0:
  10.2 44.1 all-gather.11
  56.6 40.1 all-gather.17
  98.9 49.3 all-gather.15
  150.3 32.9 all-gather.13
  184.7 35.0 all-gather.19
  221.7 53.2 all-gather.21
  284.5 106.0 all-reduce.13
  393.1 100.7 all-gather.23
  496.5 98.9 all-gather.25
  597.7 102.1 all-gather.27
  767.0 106.0 all-reduce.15
  921.5 44.4 reduce-scatter.15
  968.7 44.4 reduce-scatter.13
  1017.0 72.3 reduce-scatter.27
  1093.6 71.7 reduce-scatter.17
  1169.0 60.6 reduce-scatter.21
  1233.7 60.5 reduce-scatter.19
  1298.2 133.5 reduce-scatter.29
  1435.9 133.7 reduce-scatter.23
  1572.6 197.6 all-reduce.17
  1774.4 134.9 reduce-scatter.25
where the time goes:
time: 1950 us; the launch traced here: 1940 us
  waiting for transfers between devices  1260 us (65%)
  matrix products  352 us (18%)
  blocking collectives  111 us (6%)
  other arithmetic  104 us (5%)
  local copies, waits for them, and re-layouts  93.9 us (5%)
    psum x1, waiting for transfers between devices, shards(): mlp_out = lax.psum(down_part.astype(jnp.bfloat16), 'tp').astype(jnp.float32)  198 us
    unnamed x23, waiting for transfers between devices  141 us
    reduce_scatter x1, waiting for transfers between devices, shards(): lax.psum_scatter(grad_gate.astype(jnp.bfloat16), ('dp', 'ctx'), scatter_d...  135 us
    psum x1, waiting for transfers between devices, shards(): back_two = lax.psum(back_two.astype(jnp.bfloat16), 'tp').astype(jnp.float32)  105 us
    reduce_scatter x1, waiting for transfers between devices, shards(): lax.psum_scatter(grad_upproj.astype(jnp.bfloat16), ('dp', 'ctx'), scatter...  99.7 us
    all_gather x1, waiting for transfers between devices, shards(): lax.all_gather(gate_proj, ('dp', 'ctx'), axis=0, tiled=True)  93.2 us
    psum x1, waiting for transfers between devices, shards(): lax.psum(attn_part.astype(jnp.bfloat16), 'tp').astype(jnp.float32)  85.5 us
    all_gather x1, waiting for transfers between devices, shards(): lax.all_gather(down_proj, ('dp', 'ctx'), axis=1, tiled=True)  85.2 us
  transfers between devices with their start and end apart: 21, of which 17 were waited for; matrix products, arithmetic and copies ran while one was open for 21% of the time, Pallas kernels for 0%

commit v1 on v0

v1 whole, which is shorter than its diff:
```python
import functools

import jax
import jax.numpy as jnp
from jax import lax
from jax.experimental import pallas as pl
from jax.experimental.pallas import tpu as pltpu
from jax.sharding import PartitionSpec as P

HEAD_DIM = 128
GROUP = 2 * HEAD_DIM
BLOCK = 128
EPSILON = 1e-06
ROPE_BASE = 1000000.0
MASKED = -1e30
VMEM_LIMIT = 56 * 1024 * 1024
F32 = jnp.float32
BF16 = jnp.bfloat16

CORE_SWAP = [(0, 1), (1, 0), (2, 3), (3, 2)]
X_SWAP = [(0, 2), (2, 0), (1, 3), (3, 1)]
TP_SWAP = [(0, 1), (1, 0)]


def nn(left, right):
    return lax.dot_general(left, right, (((1,), (0,)), ((), ())), preferred_element_type=F32)


def nt(left, right):
    return lax.dot_general(left, right, (((1,), (1,)), ((), ())), preferred_element_type=F32)


def tn(left, right):
    return lax.dot_general(left, right, (((0,), (0,)), ((), ())), preferred_element_type=F32)


def unit_norm(values):
    inverse = lax.rsqrt(jnp.mean(values * values, axis=-1, keepdims=True) + EPSILON)
    return values * inverse, inverse


def swap_halves(values):
    return pltpu.roll(values, HEAD_DIM // 2, 1)


def call(kernel, grid, ins, outs, scratch=(), scalars=(), alias=None, after=(), name=None, cost=None):
    any_space = pl.BlockSpec(memory_space=pl.ANY)
    specs = [any_space if b is None else pl.BlockSpec(b, m) for _, b, m in ins]
    n_in, n_after, n_scalar = len(ins), len(after), len(scalars)

    def body(*refs):
        keep = refs[: n_scalar + n_in] + refs[n_scalar + n_in + n_after :]
        kernel(*keep)

    return pl.pallas_call(
        body,
        grid_spec=pltpu.PrefetchScalarGridSpec(
            num_scalar_prefetch=n_scalar,
            grid=grid,
            in_specs=specs + [any_space] * n_after,
            out_specs=[pl.BlockSpec(b, m) for _, _, b, m in outs],
            scratch_shapes=list(scratch),
        ),
        out_shape=[jax.ShapeDtypeStruct(s, d) for s, d, _, _ in outs],
        input_output_aliases={n_scalar + i: o for o, i in (alias or {}).items()},
        compiler_params=pltpu.CompilerParams(
            dimension_semantics=("arbitrary",) * len(grid), vmem_limit_bytes=VMEM_LIMIT
        ),
        cost_estimate=None
        if cost is None
        else pl.CostEstimate(flops=cost[0], bytes_accessed=cost[1], transcendentals=0),
        name=name,
    )(*scalars, *[a for a, _, _ in ins], *after)


def project_kernel(x_ref, w_ref, cos_ref, sin_ref, gain_ref, out_ref, raw_ref, *, groups, rows):
    is_query = pl.program_id(0) < groups
    gain = jnp.where(is_query, gain_ref[0:1, :], gain_ref[1:2, :])
    for at in range(0, x_ref.shape[0], rows):
        part = pl.ds(at, rows)
        raw = nn(x_ref[part, :], w_ref[...])
        raw_ref[part, :] = raw
        cosine, sine = cos_ref[part, :], sin_ref[part, :]
        for head in range(2):
            values = raw[:, head * HEAD_DIM : (head + 1) * HEAD_DIM]
            scaled = unit_norm(values)[0] * gain
            turned = scaled * cosine + swap_halves(scaled) * sine
            if head == 1:
                turned = jnp.where(is_query, turned, values)
            out_ref[part, head * HEAD_DIM : (head + 1) * HEAD_DIM] = turned.astype(BF16)


def project(x, weights, cosine, sine, gains, groups):
    tokens, width = x.shape
    whole = lambda j: (0, 0)
    column = lambda j: (0, j)
    columns = 2 * groups * GROUP
    return call(
        functools.partial(project_kernel, groups=groups, rows=min(256, tokens)),
        (2 * groups,),
        [
            (x, (tokens, width), whole),
            (weights, (width, GROUP), column),
            (cosine, (tokens, HEAD_DIM), whole),
            (sine, (tokens, HEAD_DIM), whole),
            (gains, (2, HEAD_DIM), whole),
        ],
        [
            ((tokens, columns), BF16, (tokens, GROUP), column),
            ((tokens, columns), F32, (tokens, GROUP), column),
        ],
        name="project",
        cost=(2 * tokens * width * columns, 2 * width * columns + 6 * tokens * columns),
    )


def span_places(orders_ref, seq, piece, span, shape, dim):
    index = lax.broadcasted_iota(jnp.int32, shape, dim)
    first, second = orders_ref[seq, 2 * piece], orders_ref[seq, 2 * piece + 1]
    return jnp.where(index < span, first * span + index, second * span + index - span)


def stacked_heads(block):
    return jnp.concatenate([block[:, 0:HEAD_DIM], block[:, HEAD_DIM:GROUP]], axis=0)


def masked_exponents(orders_ref, seq, query, pieces, span):
    rows, keys = query.shape[0], pieces[0].shape[0]
    scale = HEAD_DIM**-0.5
    places = span_places(orders_ref, seq, 0, span, (rows // 2, 1), 0)
    places = jnp.concatenate([places, places], axis=0)
    scores = []
    for at, piece in enumerate(pieces):
        key_places = span_places(orders_ref, seq, at, span, (1, keys), 1)
        product = nt(query, piece[:, 0:HEAD_DIM]) * scale
        scores.append(jnp.where(key_places <= places, product, MASKED))
    peak = functools.reduce(jnp.maximum, [jnp.max(s, axis=1, keepdims=True) for s in scores])
    exponents = [jnp.exp(s - peak) for s in scores]
    total = functools.reduce(jnp.add, [jnp.sum(e, axis=1, keepdims=True) for e in exponents])
    return exponents, 1.0 / total


def attend_kernel(orders_ref, q_ref, own_ref, core_ref, x_ref, diag_ref, *rest, first, span):
    out_ref = rest[-1]
    seq = pl.program_id(0) + first
    query = stacked_heads(q_ref[...])
    pieces = [own_ref[...], core_ref[...], x_ref[...], diag_ref[...]]
    exponents, inverse = masked_exponents(orders_ref, seq, query, pieces, span)
    total = functools.reduce(
        jnp.add, [nn(e.astype(BF16), p[:, HEAD_DIM:GROUP]) for e, p in zip(exponents, pieces)]
    )
    result = (total * inverse).astype(BF16)
    local = q_ref.shape[0]
    out_ref[:, 0:HEAD_DIM] = result[0:local]
    out_ref[:, HEAD_DIM:GROUP] = result[local:]


def attend(orders, qkv, others, first, count, local, into, after=()):
    columns = qkv.shape[1] // 2
    groups = columns // GROUP
    block = (local, GROUP)
    at_query = lambda s, g, o: (s + first, g)
    at_own = lambda s, g, o: (s + first, g + groups)
    at_half = lambda s, g, o: (s, g)
    ins = [(qkv, block, at_query), (qkv, block, at_own)] + [(k, block, at_half) for k in others]
    if into is not None:
        ins.append((into, None, None))
    return call(
        functools.partial(attend_kernel, first=first, span=local // 2),
        (count, groups),
        ins,
        [((qkv.shape[0], columns), BF16, block, at_query)],
        scalars=(orders,),
        alias=None if into is None else {0: len(ins) - 1},
        after=after,
        name="attend",
        cost=(32 * count * local * local * columns, 12 * count * local * columns),
    )[0]


def turn_back(grad, raw, cosine, sine, gain):
    turned = grad * cosine - swap_halves(grad) * sine
    unit, inverse = unit_norm(raw)
    grad_normed = turned * gain
    mean = jnp.mean(grad_normed * unit, axis=-1, keepdims=True)
    terms = jnp.sum((turned * unit).reshape(-1, 8, HEAD_DIM), axis=0)
    return (inverse * (grad_normed - unit * mean)).astype(BF16), terms


def clear_at_start(ref, dims):
    start = functools.reduce(jnp.logical_and, [pl.program_id(d) == 0 for d in range(dims)])

    @pl.when(start)
    def _():
        ref[...] = jnp.zeros_like(ref)


def attend_back_kernel(
    orders_ref, q_ref, own_ref, core_ref, x_ref, diag_ref, grad_ref, raw_ref, cos_ref, sin_ref, gain_ref,
    *rest, first, span
):
    q_back_ref, own_out, core_out, x_out, diag_out, gain_out = rest[-6:]
    seq = pl.program_id(0) + first
    scale = HEAD_DIM**-0.5
    query = stacked_heads(q_ref[...])
    grad = stacked_heads(grad_ref[...])
    pieces = [own_ref[...], core_ref[...], x_ref[...], diag_ref[...]]
    exponents, inverse = masked_exponents(orders_ref, seq, query, pieces, span)
    probability = [e * inverse for e in exponents]
    grad_prob = [nt(grad, p[:, HEAD_DIM:GROUP]) for p in pieces]
    delta = functools.reduce(
        jnp.add, [jnp.sum(p * g, axis=1, keepdims=True) for p, g in zip(probability, grad_prob)]
    )
    grad_scores = [(p * (g - delta)).astype(BF16) for p, g in zip(probability, grad_prob)]
    grad_query = functools.reduce(
        jnp.add, [nn(s, p[:, 0:HEAD_DIM]) for s, p in zip(grad_scores, pieces)]
    )
    for out, scores, prob in zip((own_out, core_out, x_out, diag_out), grad_scores, probability):
        out[:, 0:HEAD_DIM] = (tn(scores, query) * scale).astype(BF16)
        out[:, HEAD_DIM:GROUP] = tn(prob.astype(BF16), grad).astype(BF16)

    clear_at_start(gain_out, 2)
    local = q_ref.shape[0]
    for head in range(2):
        columns = pl.ds(head * HEAD_DIM, HEAD_DIM)
        result, terms = turn_back(
            grad_query[head * local : (head + 1) * local] * scale,
            raw_ref[:, columns],
            cos_ref[...],
            sin_ref[...],
            gain_ref[0:1, :],
        )
        q_back_ref[:, columns] = result
        gain_out[...] += terms


def attend_back(orders, qkv, others, grad, raw, cosine, sine, gains, first, count, local, into, after=()):
    columns = qkv.shape[1] // 2
    groups = columns // GROUP
    block = (local, GROUP)
    at_query = lambda s, g, o: (s + first, g)
    at_own = lambda s, g, o: (s + first, g + groups)
    at_half = lambda s, g, o: (s, g)
    at_table = lambda s, g, o: (s + first, 0)
    fixed = lambda s, g, o: (0, 0)
    ins = [(qkv, block, at_query), (qkv, block, at_own)] + [(k, block, at_half) for k in others]
    ins += [(grad, block, at_half), (raw, block, at_query)]
    ins += [(cosine, (local, HEAD_DIM), at_table), (sine, (local, HEAD_DIM), at_table)]
    ins += [(gains, (2, HEAD_DIM), fixed)]
    if into is not None:
        ins.append((into, None, None))
    piece = ((count * local, columns), BF16, block, at_half)
    return call(
        functools.partial(attend_back_kernel, first=first, span=local // 2),
        (count, groups),
        ins,
        [((qkv.shape[0], columns), BF16, block, at_query)]
        + [piece] * 4
        + [((8, HEAD_DIM), F32, (8, HEAD_DIM), fixed)],
        scalars=(orders,),
        alias=None if into is None else {0: len(ins) - 1},
        after=after,
        name="attend_back",
        cost=(80 * count * local * local * columns, 26 * count * local * columns),
    )


def key_back_kernel(mine_ref, core_ref, x_ref, raw_ref, cos_ref, sin_ref, gain_ref, *rest):
    out_ref, gain_out = rest[-2:]
    clear_at_start(gain_out, 2)
    grad = mine_ref[...].astype(F32) + core_ref[...].astype(F32) + x_ref[...].astype(F32)
    result, terms = turn_back(
        grad[:, 0:HEAD_DIM], raw_ref[:, 0:HEAD_DIM], cos_ref[...], sin_ref[...], gain_ref[1:2, :]
    )
    out_ref[:, 0:HEAD_DIM] = result
    out_ref[:, HEAD_DIM:GROUP] = grad[:, HEAD_DIM:GROUP].astype(BF16)
    gain_out[...] += terms


def key_back(mine, core, x, raw, cosine, sine, gains, first, count, local, into, after=()):
    columns = mine.shape[1]
    groups = columns // GROUP
    block = (local, GROUP)
    at_half = lambda s, g: (s, g)
    at_table = lambda s, g: (s + first, 0)
    fixed = lambda s, g: (0, 0)
    ins = [(mine, block, at_half), (core, block, at_half), (x, block, at_half)]
    ins += [(raw, block, lambda s, g: (s + first, g + groups))]
    ins += [(cosine, (local, HEAD_DIM), at_table), (sine, (local, HEAD_DIM), at_table)]
    ins += [(gains, (2, HEAD_DIM), fixed)]
    if into is not None:
        ins.append((into, None, None))
    return call(
        key_back_kernel,
        (count, groups),
        ins,
        [
            ((raw.shape[0], columns), BF16, block, lambda s, g: (s + first, g)),
            ((8, HEAD_DIM), F32, (8, HEAD_DIM), fixed),
        ],
        alias=None if into is None else {0: len(ins) - 1},
        after=after,
        name="key_back",
        cost=(20 * count * local * columns, 12 * count * local * columns),
    )


def feed_kernel(x_ref, c_ref, g_ref, u_ref, d_ref, *rest, rows):
    hidden_ref, gate_ref, up_ref = rest[-3:]
    for at in range(0, x_ref.shape[0], rows):
        part = pl.ds(at, rows)
        gate = nn(x_ref[part, :], g_ref[...])
        upward = nn(x_ref[part, :], u_ref[...])
        grad = nn(c_ref[part, :], d_ref[...])
        sigmoid = jax.nn.sigmoid(gate)
        silu = gate * sigmoid
        hidden_ref[part, :] = (silu * upward).astype(BF16)
        slope = sigmoid + silu * (1.0 - sigmoid)
        gate_ref[part, :] = (grad * upward * slope).astype(BF16)
        up_ref[part, :] = (grad * silu).astype(BF16)


def feed(x, c, weights, units, tile, first, count, into, after=()):
    tokens, width = x.shape
    tiles = units // tile
    whole = lambda j: (0, 0)
    ins = [(x, (tokens, width), whole), (c, (tokens, width), whole)]
    for at in range(3):
        ins.append((weights, (width, tile), lambda j, at=at: (0, at * tiles + first + j)))
    alias = None
    if into is not None:
        alias = {o: len(ins) + o for o in range(3)}
        ins += [(array, None, None) for array in into]
    return call(
        functools.partial(feed_kernel, rows=min(256, tokens)),
        (count,),
        ins,
        [((tokens, units), BF16, (tokens, tile), lambda j: (0, first + j))] * 3,
        alias=alias,
        after=after,
        name="feed",
        cost=(6 * tokens * width * count * tile, 6 * (width + tokens) * count * tile + 4 * tokens * width),
    )


def nt_kernel(*refs, count):
    w_ref, out_ref = refs[count], refs[-1]
    total, at = None, 0
    for ref in refs[:count]:
        depth = ref.shape[1]
        product = nt(ref[...], w_ref[:, at : at + depth])
        total, at = product if total is None else total + product, at + depth
    out_ref[...] = total.astype(out_ref.dtype)


def nt_product(lefts, weights, first_column, row, rows, after=()):
    width = weights.shape[0]
    depth = sum(left.shape[1] for left in lefts)
    tile = min(256, width)
    fixed = lambda j: (row // rows, 0)
    ins = [(left, (rows, left.shape[1]), fixed) for left in lefts]
    ins.append((weights, (tile, depth), lambda j: (j, first_column // depth)))
    return call(
        functools.partial(nt_kernel, count=len(lefts)),
        (width // tile,),
        ins,
        [((rows, width), BF16, (rows, tile), lambda j: (0, j))],
        after=after,
        name="nt_product",
        cost=(2 * rows * width * depth, 2 * (rows + width) * depth + 2 * rows * width),
    )[0]


def nn_kernel(x_ref, w_ref, out_ref):
    out_ref[...] = nn(x_ref[...], w_ref[...]).astype(out_ref.dtype)


def nn_product(left, weights, first_column, columns, row, rows, after=()):
    width = weights.shape[0]
    tile = min(256, columns)
    return call(
        nn_kernel,
        (columns // tile,),
        [
            (left, (rows, width), lambda j: (row // rows, 0)),
            (weights, (width, tile), lambda j: (0, first_column // tile + j)),
        ],
        [((rows, columns), BF16, (rows, tile), lambda j: (0, j))],
        after=after,
        name="nn_product",
        cost=(2 * rows * width * columns, 2 * (rows + columns) * width + 2 * rows * columns),
    )[0]


def turn_kernel(order_ref, in_ref, out_ref):
    out_ref[...] = in_ref[...].T


def turned_blocks(order, left, after=()):
    tokens, width = left.shape
    return call(
        turn_kernel,
        (width // BLOCK,),
        [(left, (tokens, BLOCK), lambda j, o: (0, o[j]))],
        [((width, tokens), BF16, (BLOCK, tokens), lambda j, o: (j, 0))],
        scalars=(order,),
        after=after,
        name="turned_blocks",
        cost=(0, 4 * tokens * width),
    )[0]


def grad_kernel(left_ref, right_ref, *outs):
    right, at = right_ref[...], 0
    for out in outs:
        rows = out.shape[0]
        out[...] = nn(left_ref[at : at + rows, :], right).astype(BF16)
        at += rows


def grad_product(left, right, cuts, first, columns, after=()):
    width, tokens = left.shape
    tile = min(512, columns)
    return call(
        grad_kernel,
        (columns // tile,),
        [
            (left, (width, tokens), lambda j: (0, 0)),
            (right, (tokens, tile), lambda j: (0, first // tile + j)),
        ],
        [((cut, columns), BF16, (cut, tile), lambda j: (0, j)) for cut in cuts],
        after=after,
        name="grad_product",
        cost=(2 * tokens * width * columns, 2 * (width + columns) * tokens + 2 * width * columns),
    )


def join_kernel(x_ref, own_ref, other_ref, gain_ref, *rest):
    middle_ref, normed_ref = rest[-2:]
    middle = x_ref[...].astype(F32) + (own_ref[...].astype(F32) + other_ref[...].astype(F32))
    middle_ref[...] = middle
    normed_ref[...] = (unit_norm(middle)[0] * gain_ref[...]).astype(BF16)


def join(x, own, other, gain, row, into, after=()):
    tokens, width = x.shape
    rows = own.shape[0]
    tile = min(128, rows)
    block = (tile, width)
    at_whole = lambda j: (row // tile + j, 0)
    at_half = lambda j: (j, 0)
    ins = [(x, block, at_whole), (own, block, at_half), (other, block, at_half)]
    ins += [(gain, (1, width), lambda j: (0, 0))]
    alias = None
    if into is not None:
        alias = {o: len(ins) + o for o in range(2)}
        ins += [(array, None, None) for array in into]
    return call(
        join_kernel,
        (rows // tile,),
        ins,
        [((tokens, width), F32, block, at_whole), ((tokens, width), BF16, block, at_whole)],
        alias=alias,
        after=after,
        name="join",
        cost=(10 * rows * width, 12 * rows * width),
    )


def norm_back_kernel(v_ref, base_ref, own_ref, other_ref, gain_ref, *rest, outs):
    out_refs, terms_ref = rest[-outs - 1 : -1], rest[-1]
    clear_at_start(terms_ref, 1)
    own = own_ref[...].astype(F32)
    unit, inverse = unit_norm(v_ref[...].astype(F32))
    grad_normed = (own + other_ref[...].astype(F32)) * gain_ref[...]
    mean = jnp.mean(grad_normed * unit, axis=-1, keepdims=True)
    result = base_ref[...].astype(F32) + inverse * (grad_normed - unit * mean)
    for ref in out_refs:
        ref[...] = result.astype(ref.dtype)
    terms_ref[...] += jnp.sum((own * unit).reshape(-1, 8, own.shape[1]), axis=0)


def norm_back(values, base, own, other, gain, row, types, into, after=()):
    tokens, width = values.shape
    rows = own.shape[0]
    tile = min(128, rows)
    block = (tile, width)
    at_whole = lambda j: (row // tile + j, 0)
    at_half = lambda j: (j, 0)
    fixed = lambda j: (0, 0)
    ins = [(values, block, at_whole), (base, block, at_whole)]
    ins += [(own, block, at_half), (other, block, at_half), (gain, (1, width), fixed)]
    alias = None
    if into is not None:
        alias = {o: len(ins) + o for o in range(len(types))}
        ins += [(array, None, None) for array in into]
    return call(
        functools.partial(norm_back_kernel, outs=len(types)),
        (rows // tile,),
        ins,
        [((tokens, width), kind, block, at_whole) for kind in types]
        + [((8, width), F32, (8, width), fixed)],
        alias=alias,
        after=after,
        name="norm_back",
        cost=(20 * rows * width, 16 * rows * width),
    )


def pair_heads(left, right):
    heads = left.shape[1] // HEAD_DIM
    cut = lambda array, at: array[:, at * HEAD_DIM : (at + 1) * HEAD_DIM]
    return jnp.concatenate([cut(a, at) for at in range(heads) for a in (left, right)], axis=1)


def split_heads(both, which):
    cuts = range(which, both.shape[1] // HEAD_DIM, 2)
    return jnp.concatenate([both[:, at * HEAD_DIM : (at + 1) * HEAD_DIM] for at in cuts], axis=1)


def behind(value, *others):
    return lax.optimization_barrier((value,) + others)[0]


def shards(
    inputs,
    span_order,
    first_gain,
    query_proj,
    key_matrix,
    value_matrix,
    query_norm,
    key_norm,
    output_proj,
    second_gain,
    gate_proj,
    up_proj,
    down_proj,
    cotangent,
):
    seqs, local, width = inputs.shape
    tokens = seqs * local
    span = local // 2
    shard = query_proj.shape[0]
    head_shard = query_norm.shape[0]
    q_cols, kv_cols = query_proj.shape[1], 2 * key_matrix.shape[1]
    groups = q_cols // GROUP
    units = gate_proj.shape[1]
    tile = 256
    tiles = units // tile
    dp_size, tp_size = lax.axis_size("dp"), lax.axis_size("tp")
    ctx = lax.axis_index("ctx")
    x_at, core_at = ctx // 2, ctx % 2
    share = lax.axis_index("dp") * 4 + ctx
    half_rows = tokens // 2
    half_seqs = seqs // 2

    def tp_start(part):
        if tp_size == 2:
            return part, lax.ppermute(part, "tp", TP_SWAP)
        return lax.psum(part, "tp"), jnp.zeros_like(part)

    core_swap = lambda value: lax.ppermute(value, "ctx", CORE_SWAP)
    x_swap = lambda value: lax.ppermute(value, "ctx", X_SWAP)

    heads = jnp.zeros((shard - head_shard,), BF16)
    small = [first_gain, second_gain]
    small += [jnp.concatenate([gain, heads]) for gain in (query_norm, key_norm)]
    small = jnp.pad(jnp.stack(small, axis=1), ((0, 0), (0, BLOCK - len(small))))
    attention_shard = jnp.concatenate(
        [query_proj, pair_heads(key_matrix, value_matrix), output_proj.T, small], axis=1
    )
    feed_shard = jnp.concatenate([gate_proj, up_proj, down_proj.T], axis=1)
    weights = lax.all_gather(attention_shard, ("dp", "ctx"), axis=0, tiled=True)
    feed_shard = behind(feed_shard, weights)
    feed_weights = lax.all_gather(feed_shard, ("dp", "ctx"), axis=0, tiled=True)
    small = weights[:, q_cols * 2 + kv_cols :].astype(F32)
    gain_first = small[:, 0].reshape(1, width)
    gain_second = small[:, 1].reshape(1, width)
    head_gains = small.reshape(-1, shard, BLOCK)[:, 0:head_shard, 2:4]
    head_gains = head_gains.reshape(HEAD_DIM, 2).T

    pairs = span_order.reshape(seqs, 4, 2)
    relative = jnp.stack([ctx, ctx ^ 1, ctx ^ 2, ctx ^ 3])
    orders = jnp.take(pairs, relative, axis=1).reshape(seqs, 8)
    places = (
        orders[:, 0:2, None] * span + jnp.arange(span, dtype=jnp.int32)[None, None, :]
    ).reshape(tokens)
    half_dim = HEAD_DIM // 2
    frequency = ROPE_BASE ** (-(jnp.arange(half_dim, dtype=F32) * (2.0 / HEAD_DIM)))
    angles = places.astype(F32)[:, None] * frequency[None, :]
    cosine, sine = jnp.cos(angles), jnp.sin(angles)
    cosine = jnp.concatenate([cosine, cosine], axis=1)
    sine = jnp.concatenate([-sine, sine], axis=1)

    dps = jnp.arange(dp_size, dtype=jnp.int32)
    other_first = jnp.stack([1 - x_at, x_at])
    cores = jnp.stack([1 - core_at, core_at])
    by_x = cores[:, None, None] + 2 * other_first[None, :, None] + 4 * dps[None, None, :]
    by_x = by_x.reshape(-1).astype(jnp.int32)
    by_dp = cores[:, None, None] + 4 * dps[None, :, None] + 2 * other_first[None, None, :]
    by_dp = by_dp.reshape(-1).astype(jnp.int32)
    cut = width // 4

    def scatter(value):
        return lax.psum_scatter(value, "dp", scatter_dimension=0, tiled=True)

    def add(*values):
        return functools.reduce(jnp.add, [v.astype(F32) for v in values]).astype(BF16)

    input_rows = inputs.reshape(tokens, width)
    cot_rows = cotangent.reshape(tokens, width)
    unit_one = unit_norm(input_rows.astype(F32))[0]
    cot_turned = turned_blocks(by_x, cot_rows)
    feed_one = (unit_one * gain_first).astype(BF16)
    qkv, raw = project(feed_one, weights, cosine, sine, head_gains, groups)

    kv = [qkv[h * half_rows : (h + 1) * half_rows, q_cols:] for h in range(2)]
    across_a = x_swap(kv[0])
    beside_a = core_swap(kv[0])
    one_turned = turned_blocks(by_dp, feed_one, after=(qkv,))
    across_b = x_swap(behind(kv[1], across_a))
    others = [(beside_a, across_a, core_swap(across_a))]
    others += [(core_swap(kv[1]), across_b, core_swap(across_b))]
    attended, joined, started = None, None, []
    for h in range(2):
        attended = attend(orders, qkv, others[h], h * half_seqs, half_seqs, local, attended)
        part = nt_product([attended], weights, q_cols + kv_cols, h * half_rows, half_rows)
        started.append(tp_start(part))
    for h in range(2):
        joined = join(input_rows, *started[h], gain_second, h * half_rows, joined)
    middle, feed_two = joined

    count_a = (tiles + 1) // 2
    run_feed = lambda first, count, into, after: feed(
        feed_two, cot_rows, feed_weights, units, tile, first, count, into, after
    )
    acts = run_feed(0, count_a, None, ())
    columns_a = count_a * tile

    x_cuts = (2 * cut, cut, cut)
    down_a = grad_product(cot_turned, acts[0], x_cuts, 0, columns_a)
    down_a_core = core_swap(down_a[0])
    two_turned = turned_blocks(by_x, feed_two, after=(down_a[0],))
    down_a_x = add(down_a[1], behind(down_a_core, two_turned)[0:cut])
    down_a_from = x_swap(down_a_x)
    acts = run_feed(count_a, tiles - count_a, acts, (down_a_x,))
    hidden, gate_back, up_back = acts

    back = []
    part = nt_product([gate_back, up_back], feed_weights, 0, 0, half_rows)
    back.append(tp_start(part))
    down_b = grad_product(
        cot_turned, hidden, x_cuts, columns_a, units - columns_a, after=(part,)
    )
    down_b_core = core_swap(down_b[0])
    part = nt_product(
        [gate_back, up_back], feed_weights, 0, half_rows, half_rows, after=(down_b[0],)
    )
    back.append(tp_start(behind(part, back[0][1])))
    down_b_x = add(down_b[1], behind(down_b_core, part)[0:cut])
    down_b_from = x_swap(behind(down_b_x, down_a_from))

    gate = grad_product(two_turned, gate_back, x_cuts, 0, units, after=(down_b_x,))
    gate_core = core_swap(gate[0])
    up = grad_product(two_turned, up_back, x_cuts, 0, units, after=(gate[0],))
    up_core = core_swap(up[0])
    gate_x = add(gate[1], behind(gate_core, up[0])[0:cut])
    gate_from = x_swap(behind(gate_x, down_b_from))
    down_a_out = scatter(add(down_a[2], down_a_core[cut:], behind(down_a_from, gate_x)))

    grads, q_back, k_back, pieces = None, None, None, []
    terms = {"second": 0.0, "query": 0.0, "key": 0.0, "first": 0.0}
    latest = gate_x
    for h in range(2):
        row = h * half_rows
        *grads, second = norm_back(
            middle, cot_rows, *back[h], gain_second, row, (F32, BF16), grads, after=(latest,)
        )
        terms["second"] = terms["second"] + jnp.sum(second, axis=0)
        grad_attended = nn_product(grads[1], weights, q_cols + kv_cols, q_cols, row, half_rows)
        q_back, to_own, to_core, to_x, to_diag, query = attend_back(
            orders, qkv, others[h], grad_attended, raw, cosine, sine, head_gains,
            h * half_seqs, half_seqs, local, q_back,
        )
        terms["query"] = terms["query"] + jnp.sum(query, axis=0)
        from_diag = core_swap(to_diag)
        from_core = core_swap(to_core)
        if h == 0:
            up_x = add(up[1], behind(up_core, to_own)[0:cut])
            latest = up_x
        pieces.append((to_own, from_core, add(to_x, from_diag)))
    grad_middle, middle_low = grads

    from_x_a = x_swap(behind(pieces[0][2], gate_from))
    from_x_b = x_swap(behind(pieces[1][2], from_x_a))
    up_from = x_swap(behind(up_x, from_x_b))
    down_b_out = scatter(add(down_b[2], down_b_core[cut:], behind(down_b_from, q_back)))

    z_cuts = (2 * cut, 2 * cut)

    def scatter_first(left, right, after):
        to_core, kept = grad_product(left, right, z_cuts, 0, right.shape[1], after=after)
        from_core = core_swap(to_core)
        return kept, from_core

    query_parts = scatter_first(one_turned, q_back, ())
    low_turned = turned_blocks(by_dp, middle_low, after=(query_parts[0],))
    query_out = scatter(add(query_parts[0], behind(query_parts[1], low_turned)))
    output_parts = scatter_first(low_turned, attended, (query_out,) if False else ())
    out_part = nt_product([hidden], feed_weights, 2 * units, 0, tokens, after=(output_parts[0],))
    out_started = tp_start(behind(out_part, back[1][1]))
    output_out = scatter(add(output_parts[0], behind(output_parts[1], out_part)))

    one = []
    for h in range(2):
        from_x = (from_x_a, from_x_b)[h]
        k_back, key = key_back(
            pieces[h][0], pieces[h][1], from_x, raw, cosine, sine, head_gains,
            h * half_seqs, half_seqs, local, k_back, after=(out_part,),
        )
        terms["key"] = terms["key"] + jnp.sum(key, axis=0)
        part = nt_product([q_back, k_back], weights, 0, h * half_rows, half_rows)
        one.append(tp_start(behind(part, out_started[1])))
    key_parts = scatter_first(one_turned, k_back, ())
    key_out = scatter(add(*key_parts))
    gate_out = scatter(add(gate[2], gate_core[cut:], gate_from))
    up_out = scatter(add(up[2], up_core[cut:], up_from))

    finish = lambda value: add(value[shard:], x_swap(value[0:shard])).astype(F32)
    grad_query, grad_output, grad_kv = finish(query_out), finish(output_out), finish(key_out)

    result = None
    for h in range(2):
        *result, first = norm_back(
            input_rows, grad_middle, *one[h], gain_first, h * half_rows, (BF16,), result
        )
        terms["first"] = terms["first"] + jnp.sum(first, axis=0)

    if tp_size != 2:
        terms["first"], terms["second"] = terms["first"] / tp_size, terms["second"] / tp_size
    totals = jnp.concatenate([terms[name] for name in ("first", "second", "query", "key")])
    totals = lax.psum(totals, ("dp", "ctx", "tp"))
    cut_total = lambda start, size: lax.dynamic_slice(totals, (start + share * size,), (size,))

    outputs = middle + (out_started[0].astype(F32) + out_started[1].astype(F32))
    grad_down = jnp.concatenate([down_a_out, down_b_out], axis=1)
    return (
        outputs.astype(BF16).reshape(inputs.shape),
        result[0].reshape(inputs.shape),
        cut_total(0, shard),
        grad_query,
        split_heads(grad_kv, 0),
        split_heads(grad_kv, 1),
        cut_total(2 * width, head_shard),
        cut_total(2 * width + HEAD_DIM, head_shard),
        grad_output.T,
        cut_total(width, shard),
        gate_out.astype(F32),
        up_out.astype(F32),
        grad_down.astype(F32).T,
    )


def solution(mesh):
    rows = P(("dp", "ctx"))
    columns = P(("dp", "ctx"), "tp")
    turned = P("tp", ("dp", "ctx"))
    tokens = P("dp", "ctx", None)
    in_specs = (
        (tokens, P("dp", None), rows, columns, columns, columns, rows, rows, turned, rows)
        + (columns, columns, turned, tokens)
    )
    out_specs = (
        (tokens, tokens, rows, columns, columns, columns, rows, rows, turned, rows)
        + (columns, columns, turned)
    )
    return jax.shard_map(shards, mesh=mesh, in_specs=in_specs, out_specs=out_specs, check_vma=False)
```

time: 1950 us -> 1160 us (0.59)
  waiting for transfers between devices: 1260 us -> 505 us
  Pallas kernels: 0 us -> 445 us
  matrix products: 352 us -> 0 us
  blocking collectives: 111 us -> 37.6 us
  local copies, waits for them, and re-layouts: 93.9 us -> 37.2 us
  other arithmetic: 104 us -> 82.7 us
  starting transfers between devices: 1.91 us -> 22.5 us
    pallas_call x0 -> x35, Pallas kernels: none -> 445 us  [call(): pl.pallas_call(body, grid_spec=pltpu.PrefetchScalarGridSpec(num_scalar_pr...]
    ppermute x0 -> x33, waiting for transfers between devices: none -> 401 us  [the longest x11 245 us: shards(): x_swap = lambda value: lax.ppermute(value, 'ctx', X_SWAP)]
    psum x3 -> x0, waiting for transfers between devices: 389 us -> none  [the longest x1 198 us: shards(): mlp_out = lax.psum(down_part.astype(jnp.bfloat16), 'tp').astype(jnp.float32)]
    reduce_scatter x7, waiting for transfers between devices: 384 us -> 0.07 us  [scatter(): return lax.psum_scatter(value, 'dp', scatter_dimension=0, tiled=True)]
    dot_general x27 -> x0, matrix products: 352 us -> none  [the longest x1 28.8 us: shards(): jnp.einsum('nd,fd->nf', cot_rows, back_down, preferred_element_type=jnp.f...]
    all_gather x9 -> x2, waiting for transfers between devices: 345 us -> 104 us  [the longest x1 104 us: shards(): weights = lax.all_gather(attention_shard, ('dp', 'ctx'), axis=0, tiled=True)]
    unnamed x23 -> x9, waiting for transfers between devices: 141 us -> 0.15 us
    unnamed x2 -> x0, blocking collectives: 64.3 us -> none
  transfers between devices with their start and end apart: 21 -> 42, of which waited for: 17 -> 15; matrix products, arithmetic and copies ran while one was open for 21% -> 8% of each run, Pallas kernels for 0% -> 29%
where the time goes in v1:
time: 1160 us; the launch traced here: 1150 us
  waiting for transfers between devices  505 us (44%)
  Pallas kernels  445 us (38%)
  other arithmetic  82.7 us (7%)
  blocking collectives  37.6 us (3%)
  local copies, waits for them, and re-layouts  37.2 us (3%)
  starting transfers between devices  22.5 us (2%)
  between operations  14.9 us (1%)
    pallas_call x35, Pallas kernels, call(): pl.pallas_call(body, grid_spec=pltpu.PrefetchScalarGridSpec(num_scalar_pr...  445 us
    ppermute x11, waiting for transfers between devices, shards(): x_swap = lambda value: lax.ppermute(value, 'ctx', X_SWAP)  245 us
    ppermute x7, waiting for transfers between devices, tp_start(): return (part, lax.ppermute(part, 'tp', TP_SWAP))  145 us
    all_gather x1, waiting for transfers between devices, shards(): weights = lax.all_gather(attention_shard, ('dp', 'ctx'), axis=0, tiled=True)  104 us
    convert_element_type x13, other arithmetic, add(): functools.reduce(jnp.add, [v.astype(F32) for v in values]).astype(BF16)  45 us
    psum x1, blocking collectives, shards(): totals = lax.psum(totals, ('dp', 'ctx', 'tp'))  37.6 us
    unnamed x118, local copies, waits for them, and re-layouts  26.4 us
  transfers between devices with their start and end apart: 42, of which 15 were waited for; matrix products, arithmetic and copies ran while one was open for 8% of the time, Pallas kernels for 29%

profile of v1, /device:TPU:0, one launch (start us, length us, event | category | flops | bytes accessed | tf_op | source)
XLA Modules:
  0.0 1145.6 jit_solution(16864920355270706187)
XLA Ops:
  21.1 103.8 %all-gather.3.cloned.1.call-done.refs_1_.refs_2_ = bf16[2048,3200]{1,0:T(8,128)(2,1)} async-done(((bf16[128,3200]{1,0:T(8,128)(2,1)}), bf16[2048,3200]{1,0:T(8,128)(2,1)}) %all-gather.3.cloned.1.call-update) | async-done | bytes 13107216 | tf_op jit(solution)/shard_map/all_gather | solution.py:574
  140.9 16.6 %project.1 = (bf16[1024,2048]{1,0:T(8,128)(2,1)}, f32[1024,2048]{1,0:T(8,128)}) custom-call(bf16[1024,2048]{1,0:T(8,128)(2,1)} %multiply_convert_fusion.refs_0_.refs_1_, bf16[2048,3200]{1,0:T(8,128)(2,1)} %all-gather.3.cloned.1.call-done.refs_1_.refs_2_, f32[1024,128]{1,0:T(8,128)} %get-tuple-element.223.refs_2_.refs_8_.refs_4_, ...), custom_call_target="tpu_custom_call" | custom-call | flops 8589934592 | bytes 20971520 | tf_op jit(solution)/shard_map/project/pallas_call | solution.py:55
  160.1 47.5 %collective-permute-done.1.refs_4_ = bf16[512,1024]{1,0:T(8,128)(2,1)S(1)} collective-permute-done((bf16[512,1024]{1,0:T(8,128)(2,1)S(1)}, bf16[512,1024]{1,0:T(8,128)(2,1)S(1)}, u32[]{:S(2)}, u32[]{:S(2)}) %collective-permute-start.1) | collective-permute-done | bytes 1048608 | tf_op jit(solution)/shard_map/ppermute | solution.py:564
  208.8 46.8 %collective-permute-done.2.refs_4_ = bf16[512,1024]{1,0:T(8,128)(2,1)S(1)} collective-permute-done((bf16[512,1024]{1,0:T(8,128)(2,1)S(1)}, bf16[512,1024]{1,0:T(8,128)(2,1)S(1)}, u32[]{:S(2)}, u32[]{:S(2)}) %collective-permute-start.2) | collective-permute-done | bytes 1048608 | tf_op jit(solution)/shard_map/ppermute | solution.py:564
  257.7 14.0 %attend.2.refs_6_.refs_0_ = bf16[1024,1024]{1,0:T(8,128)(2,1)} custom-call(s32[4,8]{1,0:T(4,128)} %copy-done.33, bf16[1024,2048]{1,0:T(8,128)(2,1)} %get-tuple-element.88.refs_1_.refs_2_, bf16[1024,2048]{1,0:T(8,128)(2,1)} %get-tuple-element.88.refs_1_.refs_2_, bf16[512,1024]{1,0:T(8,128)(2,1)} %copy-done.49, bf16[512,1024]{1,0:T(8,128)(2,1)} %copy-done.48, ...), custom_call_target="tpu_custom_call" | custom-call | flops 4294967296 | bytes 6291456 | tf_op jit(solution)/shard_map/attend/pallas_call | solution.py:55
  283.4 14.0 %attend.3.refs_0_.refs_1_ = bf16[1024,1024]{1,0:T(8,128)(2,1)} custom-call(s32[4,8]{1,0:T(4,128)} %copy-done.33, bf16[1024,2048]{1,0:T(8,128)(2,1)} %get-tuple-element.88.refs_1_.refs_2_, bf16[1024,2048]{1,0:T(8,128)(2,1)} %get-tuple-element.88.refs_1_.refs_2_, bf16[512,1024]{1,0:T(8,128)(2,1)} %copy-done.46, ...), custom_call_target="tpu_custom_call", output_to_operand_aliasing={{}: (6, {})} | custom-call | flops 4294967296 | bytes 6291456 | tf_op jit(solution)/shard_map/attend/pallas_call | solution.py:55
  307.7 11.6 %turned_blocks.4.refs_0_ = bf16[2048,1024]{1,0:T(8,128)(2,1)} custom-call(s32[16]{0:T(128)} %add.256.refs_0_, bf16[1024,2048]{1,0:T(8,128)(2,1)} %bitcast.50), custom_call_target="tpu_custom_call" | custom-call | bytes 8388608 | tf_op jit(solution)/shard_map/turned_blocks/pallas_call | solution.py:55
  336.5 36.7 %collective-permute-done.6.refs_2_ = bf16[512,2048]{1,0:T(8,128)(2,1)} collective-permute-done((bf16[512,2048]{1,0:T(8,128)(2,1)}, bf16[512,2048]{1,0:T(8,128)(2,1)}, u32[]{:S(2)}, u32[]{:S(2)}) %collective-permute-start.6) | collective-permute-done | bytes 2097184 | tf_op jit(solution)/shard_map/ppermute | solution.py:560
  379.4 27.1 %feed.2 = (bf16[1024,3072]{1,0:T(8,128)(2,1)}, bf16[1024,3072]{1,0:T(8,128)(2,1)}, bf16[1024,3072]{1,0:T(8,128)(2,1)}) custom-call(bf16[1024,2048]{1,0:T(8,128)(2,1)} %get-tuple-element.93.refs_0_.refs_1_, bf16[1024,2048]{1,0:T(8,128)(2,1)} %bitcast.51, bf16[2048,9216]{1,0:T(8,128)(2,1)} %all-gather.5.cloned.1.call-done.refs_2_.refs_3_.refs_4_.refs_1_, ...), custom_call_target="tpu_custom_call" | custom-call | flops 19327352832 | bytes 36700160 | tf_op jit(solution)/shard_map/feed/pallas_call | solution.py:55
  416.9 11.7 %turned_blocks.5.refs_0_ = bf16[2048,1024]{1,0:T(8,128)(2,1)} custom-call(s32[16]{0:T(128)} %add.256.refs_0_, bf16[1024,2048]{1,0:T(8,128)(2,1)} %get-tuple-element.93.refs_0_.refs_1_, bf16[1024,1536]{1,0:T(8,128)(2,1)} %get-tuple-element.99.refs_2_), custom_call_target="tpu_custom_call" | custom-call | bytes 8388608 | tf_op jit(solution)/shard_map/turned_blocks/pallas_call | solution.py:55
  430.4 27.5 %feed.3 = (bf16[1024,3072]{1,0:T(8,128)(2,1)}, bf16[1024,3072]{1,0:T(8,128)(2,1)}, bf16[1024,3072]{1,0:T(8,128)(2,1)}) custom-call(bf16[1024,2048]{1,0:T(8,128)(2,1)} %get-tuple-element.93.refs_0_.refs_1_, bf16[1024,2048]{1,0:T(8,128)(2,1)} %bitcast.52, ...), custom_call_target="tpu_custom_call", output_to_operand_aliasing={{0}: (5, {}), {1}: (6, {}), {2}: (7, {})} | custom-call | flops 19327352832 | bytes 36700160 | tf_op jit(solution)/shard_map/feed/pallas_call | solution.py:55
  457.9 19.7 %nt_product.9.refs_2_ = bf16[512,2048]{1,0:T(8,128)(2,1)} custom-call(bf16[1024,3072]{1,0:T(8,128)(2,1)} %get-tuple-element.102.refs_0_.refs_1_, bf16[1024,3072]{1,0:T(8,128)(2,1)} %get-tuple-element.103.refs_1_, bf16[2048,9216]{1,0:T(8,128)(2,1)} %all-gather.5.cloned.1.call-done.refs_2_.refs_3_.refs_4_.refs_1_), custom_call_target="tpu_custom_call" | custom-call | flops 12884901888 | bytes 33554432 | tf_op jit(solution)/shard_map/nt_product/pallas_call | solution.py:55
  477.6 10.4 grad_product.8
  488.4 19.8 %nt_product.10.refs_2_ = bf16[512,2048]{1,0:T(8,128)(2,1)} custom-call(bf16[1024,3072]{1,0:T(8,128)(2,1)} %get-tuple-element.102.refs_0_.refs_1_, bf16[1024,3072]{1,0:T(8,128)(2,1)} %get-tuple-element.103.refs_1_, bf16[2048,9216]{1,0:T(8,128)(2,1)} %all-gather.5.cloned.1.call-done.refs_2_.refs_3_.refs_4_.refs_1_, bf16[1024,1536]{1,0:T(8,128)(2,1)} %get-tuple-element.104.refs_3_), custom_call_target="tpu_custom_call" | custom-call | flops 12884901888 | bytes 33554432 | tf_op jit(solution)/shard_map/nt_product/pallas_call | solution.py:55
  510.0 17.4 %grad_product.9 = (bf16[1024,3072]{1,0:T(8,128)(2,1)}, bf16[512,3072]{1,0:T(8,128)(2,1)}, bf16[512,3072]{1,0:T(8,128)(2,1)}) custom-call(bf16[2048,1024]{1,0:T(8,128)(2,1)} %turned_blocks.5.refs_0_, bf16[1024,3072]{1,0:T(8,128)(2,1)} %get-tuple-element.102.refs_0_.refs_1_, bf16[512,1536]{1,0:T(8,128)(2,1)} %add_convert_fusion.10.refs_2_), custom_call_target="tpu_custom_call" | custom-call | flops 12884901888 | bytes 23068672 | tf_op jit(solution)/shard_map/grad_product/pallas_call | solution.py:55
  527.7 17.6 %grad_product.10 = (bf16[1024,3072]{1,0:T(8,128)(2,1)}, bf16[512,3072]{1,0:T(8,128)(2,1)}, bf16[512,3072]{1,0:T(8,128)(2,1)}) custom-call(bf16[2048,1024]{1,0:T(8,128)(2,1)} %turned_blocks.5.refs_0_, bf16[1024,3072]{1,0:T(8,128)(2,1)} %get-tuple-element.103.refs_1_, bf16[1024,3072]{1,0:T(8,128)(2,1)} %get-tuple-element.109.refs_2_), custom_call_target="tpu_custom_call" | custom-call | flops 12884901888 | bytes 23068672 | tf_op jit(solution)/shard_map/grad_product/pallas_call | solution.py:55
  548.5 11.9 %turned_blocks.6.refs_0_ = bf16[2048,1024]{1,0:T(8,128)(2,1)} custom-call(s32[16]{0:T(128)} %add.264.refs_0_, bf16[1024,2048]{1,0:T(8,128)(2,1)} %multiply_convert_fusion.refs_0_.refs_1_, bf16[1024,2048]{1,0:T(8,128)(2,1)} %get-tuple-element.88.refs_1_.refs_2_), custom_call_target="tpu_custom_call" | custom-call | bytes 8388608 | tf_op jit(solution)/shard_map/turned_blocks/pallas_call | solution.py:55
  560.5 33.0 %collective-permute-done.9.refs_3_ = bf16[512,2048]{1,0:T(8,128)(2,1)} collective-permute-done((bf16[512,2048]{1,0:T(8,128)(2,1)S(1)}, bf16[512,2048]{1,0:T(8,128)(2,1)}, u32[]{:S(2)}, u32[]{:S(2)}) %collective-permute-start.9) | collective-permute-done | bytes 2097184 | tf_op jit(solution)/shard_map/ppermute | solution.py:560
  617.9 25.8 %attend_back.2 = (bf16[1024,1024]{1,0:T(8,128)(2,1)}, bf16[512,1024]{1,0:T(8,128)(2,1)}, bf16[512,1024]{1,0:T(8,128)(2,1)}, bf16[512,1024]{1,0:T(8,128)(2,1)}, b...) custom-call(s32[4,8]{1,0:T(4,128)} %copy-done.33, bf16[1024,2048]{1,0:T(8,128)(2,1)} %get-tuple-element.88.refs_1_.refs_2_, ...), custom_call_target="tpu_custom_call" | custom-call | flops 10737418240 | bytes 13631488 | tf_op jit(solution)/shard_map/attend_back/pallas_call | solution.py:55
  664.1 26.4 %attend_back.3 = (bf16[1024,1024]{1,0:T(8,128)(2,1)}, bf16[512,1024]{1,0:T(8,128)(2,1)}, bf16[512,1024]{1,0:T(8,128)(2,1)}, bf16[512,1024]{1,0:T(8,128)(2,1)}, b...) custom-call(s32[4,8]{1,0:T(4,128)} %copy-done.33, ...), custom_call_target="tpu_custom_call", output_to_operand_aliasing={{0}: (11, {})} | custom-call | flops 10737418240 | bytes 13631488 | tf_op jit(solution)/shard_map/attend_back/pallas_call | solution.py:55
  702.2 11.5 %turned_blocks.7.refs_0_ = bf16[2048,1024]{1,0:T(8,128)(2,1)} custom-call(s32[16]{0:T(128)} %add.264.refs_0_, bf16[1024,2048]{1,0:T(8,128)(2,1)} %get-tuple-element.118.refs_0_.refs_1_, bf16[1024,1024]{1,0:T(8,128)(2,1)} %get-tuple-element.121.refs_2_), custom_call_target="tpu_custom_call" | custom-call | bytes 8388608 | tf_op jit(solution)/shard_map/turned_blocks/pallas_call | solution.py:55
  722.0 18.9 %nt_product.11.refs_7_.refs_8_ = bf16[1024,2048]{1,0:T(8,128)(2,1)} custom-call(bf16[1024,3072]{1,0:T(8,128)(2,1)} %get-tuple-element.101.refs_1_.refs_0_, bf16[2048,9216]{1,0:T(8,128)(2,1)} %all-gather.5.cloned.1.call-done.refs_2_.refs_3_.refs_4_.refs_1_, bf16[1024,1024]{1,0:T(8,128)(2,1)} %get-tuple-element.122.refs_2_), custom_call_target="tpu_custom_call" | custom-call | flops 12884901888 | bytes 23068672 | tf_op jit(solution)/shard_map/nt_product/pallas_call | solution.py:55
  754.9 59.1 %collective-permute-done.20 = bf16[512,3072]{1,0:T(8,128)(2,1)S(1)} collective-permute-done((bf16[512,3072]{1,0:T(8,128)(2,1)S(1)}, bf16[512,3072]{1,0:T(8,128)(2,1)S(1)}, u32[]{:S(2)}, u32[]{:S(2)}) %collective-permute-start.20) | collective-permute-done | bytes 3145760 | tf_op jit(solution)/shard_map/ppermute | solution.py:564
  821.6 19.0 %collective-permute-done.21.refs_2_ = bf16[512,1024]{1,0:T(8,128)(2,1)S(1)} collective-permute-done((bf16[512,1024]{1,0:T(8,128)(2,1)}, bf16[512,1024]{1,0:T(8,128)(2,1)S(1)}, u32[]{:S(2)}, u32[]{:S(2)}) %collective-permute-start.21) | collective-permute-done | bytes 1048608 | tf_op jit(solution)/shard_map/ppermute | solution.py:564
  849.2 10.6 nt_product.13.refs_2_
  900.1 68.1 %collective-permute-done.32 = bf16[512,3072]{1,0:T(8,128)(2,1)S(1)} collective-permute-done((bf16[512,3072]{1,0:T(8,128)(2,1)S(1)}, bf16[512,3072]{1,0:T(8,128)(2,1)S(1)}, u32[]{:S(2)}, u32[]{:S(2)}) %collective-permute-start.32) | collective-permute-done | bytes 3145760 | tf_op jit(solution)/shard_map/ppermute | solution.py:564
  974.6 17.5 %collective-permute-done.14 = bf16[1024,2048]{1,0:T(8,128)(2,1)} collective-permute-done((bf16[1024,2048]{1,0:T(8,128)(2,1)}, bf16[1024,2048]{1,0:T(8,128)(2,1)}, u32[]{:S(2)}, u32[]{:S(2)}) %collective-permute-start.14) | collective-permute-done | bytes 4194336 | tf_op jit(solution)/shard_map/ppermute | solution.py:560
  992.8 10.6 nt_product.12.refs_2_
  1014.5 10.6 add_convert_fusion
  1025.2 15.7 %collective-permute-done.25.refs_3_ = bf16[512,2048]{1,0:T(8,128)(2,1)} collective-permute-done((bf16[512,2048]{1,0:T(8,128)(2,1)S(1)}, bf16[512,2048]{1,0:T(8,128)(2,1)}, u32[]{:S(2)}, u32[]{:S(2)}) %collective-permute-start.25) | collective-permute-done | bytes 2097184 | tf_op jit(solution)/shard_map/ppermute | solution.py:560
  1050.8 32.9 %collective-permute-done.24.refs_3_ = bf16[512,2048]{1,0:T(8,128)(2,1)} collective-permute-done((bf16[512,2048]{1,0:T(8,128)(2,1)}, bf16[512,2048]{1,0:T(8,128)(2,1)}, u32[]{:S(2)}, u32[]{:S(2)}) %collective-permute-start.24) | collective-permute-done | bytes 2097184 | tf_op jit(solution)/shard_map/ppermute | solution.py:560
  1093.4 37.6 %psum.7 = f32[4352]{0:T(1024)S(1)} all-reduce(f32[4352]{0:T(1024)S(1)} %pad_maximum_fusion.5), channel_id=1, replica_groups=mesh['dp'=4,'ctx'=4,'tp'=2] {'dp','ctx','tp'}, use_global_device_ids=true, to_apply=%region_9.10 | all-reduce | flops 4352 | bytes 34816 | tf_op jit(solution)/shard_map/psum | solution.py:743
  (290 shorter events, 279.2 us)
Async XLA Ops:
  7.2 117.7 %all-gather.3.cloned.1.call-start = ((), (), s32[]{:S(2)}) async-start(), calls=%async_computation.7 | async-start | bytes 13926400 | tf_op jit(solution)/shard_map/all_gather | solution.py:574
  18.0 361.4 %all-gather.5.cloned.1.call-start = ((), (), s32[]{:S(2)}) async-start(), calls=%async_computation.8 | async-start | bytes 40108032 | tf_op jit(solution)/shard_map/all_gather | solution.py:576
  124.9 880.0 %reduce-scatter.18.cloned.1.call-start = ((), (), s32[]{:S(2)}) async-start(), calls=%async_computation.14 | async-start | bytes 1966080 | tf_op jit(solution)/shard_map/reduce_scatter | solution.py:606
  159.3 48.3 %collective-permute-start.1 = (bf16[512,1024]{1,0:T(8,128)(2,1)S(1)}, bf16[512,1024]{1,0:T(8,128)(2,1)S(1)}, u32[]{:S(2)}, u32[]{:S(2)}) collective-permute-start(bf16[512,1024]{1,0:T(8,128)(2,1)S(1)} %get-tuple-element.204), channel_id=1, source_target_pairs={{0,4},{4,0},{2,6},{6,2},{1,5},{5,1},{3,7},{7,3},{8,12},{12,8},{10,... | collective-permute-start | bytes 3145736 | tf_op jit(solution)/shard_map/ppermute | solution.py:564
  207.6 48.0 %collective-permute-start.2 = (bf16[512,1024]{1,0:T(8,128)(2,1)S(1)}, bf16[512,1024]{1,0:T(8,128)(2,1)S(1)}, u32[]{:S(2)}, u32[]{:S(2)}) collective-permute-start(bf16[512,1024]{1,0:T(8,128)(2,1)S(1)} %get-tuple-element.89), channel_id=1, source_target_pairs={{0,4},{4,0},{2,6},{6,2},{1,5},{5,1},{3,7},{7,3},{8,12},{12,8},{10,... | collective-permute-start | bytes 3145736 | tf_op jit(solution)/shard_map/ppermute | solution.py:564
  208.3 47.4 %collective-permute-start.4 = (bf16[512,1024]{1,0:T(8,128)(2,1)S(1)}, bf16[512,1024]{1,0:T(8,128)(2,1)S(1)}, u32[]{:S(2)}, u32[]{:S(2)}) collective-permute-start(bf16[512,1024]{1,0:T(8,128)(2,1)S(1)} %get-tuple-element.204), channel_id=1, source_target_pairs={{0,2},{2,0},{4,6},{6,4},{1,3},{3,1},{5,7},{7,5},{8,10},{10,8},{12,... | collective-permute-start | bytes 3145736 | tf_op jit(solution)/shard_map/ppermute | solution.py:563
  208.3 47.4 %collective-permute-start.5 = (bf16[512,1024]{1,0:T(8,128)(2,1)S(1)}, bf16[512,1024]{1,0:T(8,128)(2,1)S(1)}, u32[]{:S(2)}, u32[]{:S(2)}) collective-permute-start(bf16[512,1024]{1,0:T(8,128)(2,1)S(1)} %collective-permute-done.1.refs_4_), channel_id=1, source_target_pairs={{0,2},{2,0},{4,6},{6,4},{1,3},{3,1},{5,7},{7,5},{8,10},{10,8},{12,... | collective-permute-start | bytes 3145736 | tf_op jit(solution)/shard_map/ppermute | solution.py:563
  208.8 72.7 %collective-permute-start = (bf16[512,1024]{1,0:T(8,128)(2,1)S(1)}, bf16[512,1024]{1,0:T(8,128)(2,1)S(1)}, u32[]{:S(2)}, u32[]{:S(2)}) collective-permute-start(bf16[512,1024]{1,0:T(8,128)(2,1)S(1)} %get-tuple-element.89), channel_id=1, source_target_pairs={{0,2},{2,0},{4,6},{6,4},{1,3},{3,1},{5,7},{7,5},{8,10},{10,8},{12,... | collective-permute-start | bytes 3145736 | tf_op jit(solution)/shard_map/ppermute | solution.py:563
  280.0 48.6 %collective-permute-start.7 = (bf16[512,2048]{1,0:T(8,128)(2,1)}, bf16[512,2048]{1,0:T(8,128)(2,1)S(1)}, u32[]{:S(2)}, u32[]{:S(2)}) collective-permute-start(bf16[512,2048]{1,0:T(8,128)(2,1)} %nt_product.8.refs_1_), channel_id=1, source_target_pairs={{0,1},{1,0},{2,3},{3,2},{4,5},{5,4},{6,7},{7,6},{8,9},{9,8},{10,11... | collective-permute-start | bytes 6291464 | tf_op jit(solution)/shard_map/ppermute | solution.py:560
  305.7 67.5 %collective-permute-start.6 = (bf16[512,2048]{1,0:T(8,128)(2,1)}, bf16[512,2048]{1,0:T(8,128)(2,1)}, u32[]{:S(2)}, u32[]{:S(2)}) collective-permute-start(bf16[512,2048]{1,0:T(8,128)(2,1)} %nt_product.7.refs_1_), channel_id=1, source_target_pairs={{0,1},{1,0},{2,3},{3,2},{4,5},{5,4},{6,7},{7,6},{8,9},{9,8},{10,11... | collective-permute-start | bytes 6291464 | tf_op jit(solution)/shard_map/ppermute | solution.py:560
  527.5 68.0 %collective-permute-start.12 = (bf16[1024,3072]{1,0:T(8,128)(2,1)}, bf16[1024,3072]{1,0:T(8,128)(2,1)}, u32[]{:S(2)}, u32[]{:S(2)}) collective-permute-start(bf16[1024,3072]{1,0:T(8,128)(2,1)} %get-tuple-element.109.refs_2_), channel_id=1, source_target_pairs={{0,2},{2,0},{4,6},{6,4},{1,3},{3,1},{5,7},{7,5},{8,10},{10,8},{12,... | collective-permute-start | bytes 18874376 | tf_op jit(solution)/shard_map/ppermute | solution.py:563
  545.3 98.5 %collective-permute-start.13 = (bf16[1024,3072]{1,0:T(8,128)(2,1)}, bf16[1024,3072]{1,0:T(8,128)(2,1)}, u32[]{:S(2)}, u32[]{:S(2)}) collective-permute-start(bf16[1024,3072]{1,0:T(8,128)(2,1)} %get-tuple-element.110), channel_id=1, source_target_pairs={{0,2},{2,0},{4,6},{6,4},{1,3},{3,1},{5,7},{7,5},{8,10},{10,8},{12,... | collective-permute-start | bytes 18874376 | tf_op jit(solution)/shard_map/ppermute | solution.py:563
  545.7 47.7 %collective-permute-start.9 = (bf16[512,2048]{1,0:T(8,128)(2,1)S(1)}, bf16[512,2048]{1,0:T(8,128)(2,1)}, u32[]{:S(2)}, u32[]{:S(2)}) collective-permute-start(bf16[512,2048]{1,0:T(8,128)(2,1)S(1)} %copy-done.2), channel_id=1, source_target_pairs={{0,1},{1,0},{2,3},{3,2},{4,5},{5,4},{6,7},{7,6},{8,9},{9,8},{10,11... | collective-permute-start | bytes 6291464 | tf_op jit(solution)/shard_map/ppermute | solution.py:560
  547.2 47.7 %collective-permute-start.18 = (bf16[512,1536]{1,0:T(8,128)(2,1)}, bf16[512,1536]{1,0:T(8,128)(2,1)}, u32[]{:S(2)}, u32[]{:S(2)}) collective-permute-start(bf16[512,1536]{1,0:T(8,128)(2,1)} %add_convert_fusion.11.refs_8_), channel_id=1, source_target_pairs={{0,4},{4,0},{2,6},{6,2},{1,5},{5,1},{3,7},{7,3},{8,12},{12,8},{10,... | collective-permute-start | bytes 4718600 | tf_op jit(solution)/shard_map/ppermute | solution.py:564
  593.4 55.0 %collective-permute-start.10 = (bf16[512,2048]{1,0:T(8,128)(2,1)}, bf16[512,2048]{1,0:T(8,128)(2,1)S(1)}, u32[]{:S(2)}, u32[]{:S(2)}) collective-permute-start(bf16[512,2048]{1,0:T(8,128)(2,1)} %nt_product.10.refs_2_), channel_id=1, source_target_pairs={{0,1},{1,0},{2,3},{3,2},{4,5},{5,4},{6,7},{7,6},{8,9},{9,8},{10,11... | collective-permute-start | bytes 6291464 | tf_op jit(solution)/shard_map/ppermute | solution.py:560
  594.9 95.6 %collective-permute-start.19 = (bf16[512,1536]{1,0:T(8,128)(2,1)}, bf16[512,1536]{1,0:T(8,128)(2,1)}, u32[]{:S(2)}, u32[]{:S(2)}) collective-permute-start(bf16[512,1536]{1,0:T(8,128)(2,1)} %add_convert_fusion.10.refs_2_), channel_id=1, source_target_pairs={{0,4},{4,0},{2,6},{6,2},{1,5},{5,1},{3,7},{7,3},{8,12},{12,8},{10,... | collective-permute-start | bytes 4718600 | tf_op jit(solution)/shard_map/ppermute | solution.py:564
  603.5 401.5 %reduce-scatter.20.cloned.1.call-start = ((), (), s32[]{:S(2)}) async-start(), calls=%async_computation.15 | async-start | bytes 1966080 | tf_op jit(solution)/shard_map/reduce_scatter | solution.py:606
  693.7 316.7 %reduce-scatter.12.cloned.1.call-start = ((), (), s32[]{:S(2)}) async-start(), calls=%async_computation.11 | async-start | bytes 2621440 | tf_op jit(solution)/shard_map/reduce_scatter | solution.py:606
  743.3 268.6 %reduce-scatter.8.cloned.1.call-start = ((), (), s32[]{:S(2)}) async-start(), calls=%async_computation.9 | async-start | bytes 2621440 | tf_op jit(solution)/shard_map/reduce_scatter | solution.py:606
  743.4 70.6 %collective-permute-start.20 = (bf16[512,3072]{1,0:T(8,128)(2,1)S(1)}, bf16[512,3072]{1,0:T(8,128)(2,1)S(1)}, u32[]{:S(2)}, u32[]{:S(2)}) collective-permute-start(bf16[512,3072]{1,0:T(8,128)(2,1)S(1)} %copy-done.1), channel_id=1, source_target_pairs={{0,4},{4,0},{2,6},{6,2},{1,5},{5,1},{3,7},{7,3},{8,12},{12,8},{10,... | collective-permute-start | bytes 9437192 | tf_op jit(solution)/shard_map/ppermute | solution.py:564
  744.9 72.7 %collective-permute-start.26 = (bf16[1024,1024]{1,0:T(8,128)(2,1)}, bf16[1024,1024]{1,0:T(8,128)(2,1)S(1)}, u32[]{:S(2)}, u32[]{:S(2)}) collective-permute-start(bf16[1024,1024]{1,0:T(8,128)(2,1)} %get-tuple-element.150), channel_id=1, source_target_pairs={{0,2},{2,0},{4,6},{6,4},{1,3},{3,1},{5,7},{7,5},{8,10},{10,8},{12,... | collective-permute-start | bytes 6291464 | tf_op jit(solution)/shard_map/ppermute | solution.py:563
  745.4 74.5 %collective-permute-start.16 = (bf16[512,1024]{1,0:T(8,128)(2,1)}, bf16[512,1024]{1,0:T(8,128)(2,1)}, u32[]{:S(2)}, u32[]{:S(2)}) collective-permute-start(bf16[512,1024]{1,0:T(8,128)(2,1)} %get-tuple-element.128), channel_id=1, source_target_pairs={{0,2},{2,0},{4,6},{6,4},{1,3},{3,1},{5,7},{7,5},{8,10},{10,8},{12,... | collective-permute-start | bytes 3145736 | tf_op jit(solution)/shard_map/ppermute | solution.py:563
  817.1 42.8 %collective-permute-start.15 = (bf16[512,1024]{1,0:T(8,128)(2,1)}, bf16[512,1024]{1,0:T(8,128)(2,1)S(1)}, u32[]{:S(2)}, u32[]{:S(2)}) collective-permute-start(bf16[512,1024]{1,0:T(8,128)(2,1)} %get-tuple-element.126), channel_id=1, source_target_pairs={{0,2},{2,0},{4,6},{6,4},{1,3},{3,1},{5,7},{7,5},{8,10},{10,8},{12,... | collective-permute-start | bytes 3145736 | tf_op jit(solution)/shard_map/ppermute | solution.py:563
  819.9 271.8 %reduce-scatter.10.cloned.1.call-start = ((), (), s32[]{:S(2)}) async-start(), calls=%async_computation.10 | async-start | bytes 2621440 | tf_op jit(solution)/shard_map/reduce_scatter | solution.py:606
  889.5 242.7 %reduce-scatter.14.cloned.1.call-start = ((), (), s32[]{:S(2)}) async-start(), calls=%async_computation.12 | async-start | bytes 3932160 | tf_op jit(solution)/shard_map/reduce_scatter | solution.py:606
  896.2 240.0 %reduce-scatter.16.cloned.1.call-start = ((), (), s32[]{:S(2)}) async-start(), calls=%async_computation.13 | async-start | bytes 3932160 | tf_op jit(solution)/shard_map/reduce_scatter | solution.py:606
  898.0 70.1 %collective-permute-start.32 = (bf16[512,3072]{1,0:T(8,128)(2,1)S(1)}, bf16[512,3072]{1,0:T(8,128)(2,1)S(1)}, u32[]{:S(2)}, u32[]{:S(2)}) collective-permute-start(bf16[512,3072]{1,0:T(8,128)(2,1)S(1)} %copy-done), channel_id=1, source_target_pairs={{0,4},{4,0},{2,6},{6,2},{1,5},{5,1},{3,7},{7,3},{8,12},{12,8},{10,... | collective-permute-start | bytes 9437192 | tf_op jit(solution)/shard_map/ppermute | solution.py:564
  899.5 92.6 %collective-permute-start.14 = (bf16[1024,2048]{1,0:T(8,128)(2,1)}, bf16[1024,2048]{1,0:T(8,128)(2,1)}, u32[]{:S(2)}, u32[]{:S(2)}) collective-permute-start(bf16[1024,2048]{1,0:T(8,128)(2,1)} %nt_product.11.refs_7_.refs_8_), channel_id=1, source_target_pairs={{0,1},{1,0},{2,3},{3,2},{4,5},{5,4},{6,7},{7,6},{8,9},{9,8},{10,11... | collective-permute-start | bytes 12582920 | tf_op jit(solution)/shard_map/ppermute | solution.py:560
  992.1 48.7 %collective-permute-start.25 = (bf16[512,2048]{1,0:T(8,128)(2,1)S(1)}, bf16[512,2048]{1,0:T(8,128)(2,1)}, u32[]{:S(2)}, u32[]{:S(2)}) collective-permute-start(bf16[512,2048]{1,0:T(8,128)(2,1)S(1)} %copy-done.5), channel_id=1, source_target_pairs={{0,1},{1,0},{2,3},{3,2},{4,5},{5,4},{6,7},{7,6},{8,9},{9,8},{10,11... | collective-permute-start | bytes 6291464 | tf_op jit(solution)/shard_map/ppermute | solution.py:560
  1003.4 80.3 %collective-permute-start.24 = (bf16[512,2048]{1,0:T(8,128)(2,1)}, bf16[512,2048]{1,0:T(8,128)(2,1)}, u32[]{:S(2)}, u32[]{:S(2)}) collective-permute-start(bf16[512,2048]{1,0:T(8,128)(2,1)} %nt_product.12.refs_2_), channel_id=1, source_target_pairs={{0,1},{1,0},{2,3},{3,2},{4,5},{5,4},{6,7},{7,6},{8,9},{9,8},{10,11... | collective-permute-start | bytes 6291464 | tf_op jit(solution)/shard_map/ppermute | solution.py:560
  1011.4 37.5 %collective-permute-start.31 = (bf16[128,1024]{1,0:T(8,128)(2,1)S(1)}, bf16[128,1024]{1,0:T(8,128)(2,1)S(1)}, u32[]{:S(2)}, u32[]{:S(2)}) collective-permute-start(bf16[128,1024]{1,0:T(8,128)(2,1)S(1)} %slice.167), channel_id=1, source_target_pairs={{0,4},{4,0},{2,6},{6,2},{1,5},{5,1},{3,7},{7,3},{8,12},{12,8},{10,... | collective-permute-start | bytes 786440 | tf_op jit(solution)/shard_map/ppermute | solution.py:564
  1092.8 41.8 %collective-permute-start.29 = (bf16[128,1024]{1,0:T(8,128)(2,1)S(1)}, bf16[128,1024]{1,0:T(8,128)(2,1)S(1)}, u32[]{:S(2)}, u32[]{:S(2)}) collective-permute-start(bf16[128,1024]{1,0:T(8,128)(2,1)S(1)} %slice.157), channel_id=1, source_target_pairs={{0,4},{4,0},{2,6},{6,2},{1,5},{5,1},{3,7},{7,3},{8,12},{12,8},{10,... | collective-permute-start | bytes 786440 | tf_op jit(solution)/shard_map/ppermute | solution.py:564
  (61 other events, 1046.3 us)
Sparse Core Ops, SparseCore 0:
  18.2 106.7 all-gather.2
  126.5 230.5 all-gather.4
  603.6 33.5 reduce-scatter.17
  693.9 33.5 reduce-scatter.19
  743.4 42.2 reduce-scatter.11
  820.0 41.3 reduce-scatter.7
  889.6 42.0 reduce-scatter.9
  934.1 59.5 reduce-scatter.13
  996.1 60.2 reduce-scatter.15

commit v2 on v1

v2 whole, which is shorter than its diff:
```python
import functools

import jax
import jax.numpy as jnp
from jax import lax
from jax.experimental import pallas as pl
from jax.experimental.pallas import tpu as pltpu
from jax.sharding import PartitionSpec as P

HEAD_DIM = 128
GROUP = 2 * HEAD_DIM
BLOCK = 128
EPSILON = 1e-06
ROPE_BASE = 1000000.0
MASKED = -1e30
VMEM_LIMIT = 56 * 1024 * 1024
F32 = jnp.float32
BF16 = jnp.bfloat16
FLOPS_PER_US = 1e10

CORE_SWAP = [(0, 1), (1, 0), (2, 3), (3, 2)]
X_SWAP = [(0, 2), (2, 0), (1, 3), (3, 1)]
TP_SWAP = [(0, 1), (1, 0)]


def nn(left, right):
    return lax.dot_general(left, right, (((1,), (0,)), ((), ())), preferred_element_type=F32)


def nt(left, right):
    return lax.dot_general(left, right, (((1,), (1,)), ((), ())), preferred_element_type=F32)


def tn(left, right):
    return lax.dot_general(left, right, (((0,), (0,)), ((), ())), preferred_element_type=F32)


def unit_norm(values):
    inverse = lax.rsqrt(jnp.mean(values * values, axis=-1, keepdims=True) + EPSILON)
    return values * inverse, inverse


def swap_halves(values):
    return pltpu.roll(values, HEAD_DIM // 2, 1)


def call(kernel, grid, ins, outs, scratch=(), scalars=(), alias=None, after=(), name=None, cost=1.0):
    any_space = pl.BlockSpec(memory_space=pl.ANY)
    specs = [any_space if b is None else pl.BlockSpec(b, m) for _, b, m in ins]
    n_in, n_after, n_scalar = len(ins), len(after), len(scalars)

    def body(*refs):
        keep = refs[: n_scalar + n_in] + refs[n_scalar + n_in + n_after :]
        kernel(*keep)

    return pl.pallas_call(
        body,
        grid_spec=pltpu.PrefetchScalarGridSpec(
            num_scalar_prefetch=n_scalar,
            grid=grid,
            in_specs=specs + [any_space] * n_after,
            out_specs=[pl.BlockSpec(b, m) for _, _, b, m in outs],
            scratch_shapes=list(scratch),
        ),
        out_shape=[jax.ShapeDtypeStruct(s, d) for s, d, _, _ in outs],
        input_output_aliases={n_scalar + i: o for o, i in (alias or {}).items()},
        compiler_params=pltpu.CompilerParams(
            dimension_semantics=("arbitrary",) * len(grid), vmem_limit_bytes=VMEM_LIMIT
        ),
        cost_estimate=pl.CostEstimate(
            flops=int(cost * FLOPS_PER_US), bytes_accessed=0, transcendentals=0
        ),
        name=name,
    )(*scalars, *[a for a, _, _ in ins], *after)


def pack_first_kernel(q_ref, k_ref, v_ref, o_ref, g_ref, u_ref, d_ref, small_ref, out_ref):
    columns, third = q_ref.shape[1], g_ref.shape[1]
    out_ref[:, 0:columns] = q_ref[...]
    for at in range(columns // GROUP):
        cut = slice(at * HEAD_DIM, (at + 1) * HEAD_DIM)
        start = columns + at * GROUP
        out_ref[:, start : start + HEAD_DIM] = k_ref[:, cut]
        out_ref[:, start + HEAD_DIM : start + GROUP] = v_ref[:, cut]
    out_ref[:, 2 * columns : 3 * columns] = o_ref[...].T
    start = 3 * columns
    out_ref[:, start : start + third] = g_ref[...]
    out_ref[:, start + third : start + 2 * third] = u_ref[...]
    out_ref[:, start + 2 * third : start + 3 * third] = d_ref[...].T
    out_ref[:, start + 3 * third :] = small_ref[...]


def pack_first(q, k, v, o, g, u, d, small, third):
    shard, columns = q.shape
    whole = lambda array: (array, array.shape, lambda j: (0, 0))
    total = 3 * columns + 3 * third + BLOCK
    return call(
        pack_first_kernel,
        (1,),
        [whole(q), whole(k), whole(v), whole(o)]
        + [(g, (shard, third), lambda j: (0, 0)), (u, (shard, third), lambda j: (0, 0))]
        + [(d, (third, shard), lambda j: (0, 0)), whole(small)],
        [((shard, total), BF16, (shard, total), lambda j: (0, 0))],
        name="pack_first",
        cost=3,
    )[0]


def pack_second_kernel(g_ref, u_ref, d_ref, out_ref):
    step = pl.program_id(0)
    part = step // 2

    @pl.when(part == 0)
    def _():
        out_ref[...] = g_ref[...]

    @pl.when(part == 1)
    def _():
        out_ref[...] = u_ref[...]

    @pl.when(part == 2)
    def _():
        out_ref[...] = d_ref[...].T


def pack_second(g, u, d, third, after=()):
    shard = g.shape[0]
    return call(
        pack_second_kernel,
        (6,),
        [(g, (shard, third), lambda j: (0, 1 + j % 2)), (u, (shard, third), lambda j: (0, 1 + j % 2))]
        + [(d, (third, shard), lambda j: (1 + j % 2, 0))],
        [((shard, 6 * third), BF16, (shard, third), lambda j: (0, j))],
        after=after,
        name="pack_second",
        cost=5,
    )[0]


def norm_kernel(x_ref, gain_ref, out_ref):
    out_ref[...] = (unit_norm(x_ref[...].astype(F32))[0] * gain_ref[...]).astype(BF16)


def norm_rows(x, gain, after=()):
    tokens, width = x.shape
    tile = min(256, tokens)
    block = (tile, width)
    return call(
        norm_kernel,
        (tokens // tile,),
        [(x, block, lambda j: (j, 0)), (gain, (1, width), lambda j: (0, 0))],
        [((tokens, width), BF16, block, lambda j: (j, 0))],
        after=after,
        name="norm_rows",
        cost=5,
    )[0]


def project_kernel(x_ref, w_ref, cos_ref, sin_ref, gain_ref, out_ref, raw_ref, *, turned, rows):
    for at in range(0, x_ref.shape[0], rows):
        part = pl.ds(at, rows)
        raw = nn(x_ref[part, :], w_ref[...])
        raw_ref[part, :] = raw
        cosine, sine = cos_ref[part, :], sin_ref[part, :]
        for head in range(2):
            values = raw[:, head * HEAD_DIM : (head + 1) * HEAD_DIM]
            if head < turned:
                scaled = unit_norm(values)[0] * gain_ref[...]
                values = scaled * cosine + swap_halves(scaled) * sine
            out_ref[part, head * HEAD_DIM : (head + 1) * HEAD_DIM] = values.astype(BF16)


def project(x, weights, cosine, sine, gain, groups, first, turned, row, rows, after=()):
    width = x.shape[1]
    some = lambda j: (row // rows, 0)
    column = lambda j: (0, j)
    columns = groups * GROUP
    return call(
        functools.partial(project_kernel, turned=turned, rows=min(256, rows)),
        (groups,),
        [
            (x, (rows, width), some),
            (weights, (width, GROUP), lambda j: (0, first + j)),
            (cosine, (rows, HEAD_DIM), some),
            (sine, (rows, HEAD_DIM), some),
            (gain, (1, HEAD_DIM), lambda j: (0, 0)),
        ],
        [
            ((rows, columns), BF16, (rows, GROUP), column),
            ((rows, columns), F32, (rows, GROUP), column),
        ],
        after=after,
        name="project",
        cost=10,
    )


def span_places(orders_ref, seq, piece, span, shape, dim):
    index = lax.broadcasted_iota(jnp.int32, shape, dim)
    first, second = orders_ref[seq, 2 * piece], orders_ref[seq, 2 * piece + 1]
    return jnp.where(index < span, first * span + index, second * span + index - span)


def stacked_heads(block):
    return jnp.concatenate([block[:, 0:HEAD_DIM], block[:, HEAD_DIM:GROUP]], axis=0)


def masked_exponents(orders_ref, seq, query, pieces, span):
    rows, keys = query.shape[0], pieces[0].shape[0]
    scale = HEAD_DIM**-0.5
    places = span_places(orders_ref, seq, 0, span, (rows // 2, 1), 0)
    places = jnp.concatenate([places, places], axis=0)
    scores = []
    for at, piece in enumerate(pieces):
        key_places = span_places(orders_ref, seq, at, span, (1, keys), 1)
        product = nt(query, piece[:, 0:HEAD_DIM]) * scale
        scores.append(jnp.where(key_places <= places, product, MASKED))
    peak = functools.reduce(jnp.maximum, [jnp.max(s, axis=1, keepdims=True) for s in scores])
    exponents = [jnp.exp(s - peak) for s in scores]
    total = functools.reduce(jnp.add, [jnp.sum(e, axis=1, keepdims=True) for e in exponents])
    return exponents, 1.0 / total


def attend_kernel(orders_ref, q_ref, own_ref, core_ref, x_ref, diag_ref, out_ref, *, first, span):
    seq = pl.program_id(0) + first
    local = q_ref.shape[0]
    for group in range(q_ref.shape[1] // GROUP):
        columns = slice(group * GROUP, (group + 1) * GROUP)
        query = stacked_heads(q_ref[:, columns])
        pieces = [ref[:, columns] for ref in (own_ref, core_ref, x_ref, diag_ref)]
        exponents, inverse = masked_exponents(orders_ref, seq, query, pieces, span)
        total = functools.reduce(
            jnp.add, [nn(e.astype(BF16), p[:, HEAD_DIM:GROUP]) for e, p in zip(exponents, pieces)]
        )
        result = (total * inverse).astype(BF16)
        for head in range(2):
            start = group * GROUP + head * HEAD_DIM
            out_ref[:, start : start + HEAD_DIM] = result[head * local : (head + 1) * local]


def attend(orders, q, kv, others, first, count, local, after=()):
    columns = q.shape[1]
    block = (local, columns)
    at_whole = lambda s, o: (s + first, 0)
    at_half = lambda s, o: (s, 0)
    ins = [(q, block, at_whole), (kv, block, at_half)] + [(k, block, at_half) for k in others]
    return call(
        functools.partial(attend_kernel, first=first, span=local // 2),
        (count,),
        ins,
        [((count * local, columns), BF16, block, at_half)],
        scalars=(orders,),
        after=after,
        name="attend",
        cost=11,
    )[0]


def turn_back(grad, raw, cosine, sine, gain):
    turned = grad * cosine - swap_halves(grad) * sine
    unit, inverse = unit_norm(raw)
    grad_normed = turned * gain
    mean = jnp.mean(grad_normed * unit, axis=-1, keepdims=True)
    terms = jnp.sum((turned * unit).reshape(-1, 8, HEAD_DIM), axis=0)
    return (inverse * (grad_normed - unit * mean)).astype(BF16), terms


def clear_at_start(ref, dims):
    start = functools.reduce(jnp.logical_and, [pl.program_id(d) == 0 for d in range(dims)])

    @pl.when(start)
    def _():
        ref[...] = jnp.zeros_like(ref)


def attend_back_kernel(
    orders_ref, q_ref, own_ref, core_ref, x_ref, diag_ref, grad_ref, raw_ref, cos_ref, sin_ref, gain_ref,
    *rest, first, span
):
    q_back_ref, own_out, x_out, core_out, gain_out = rest[-5:]
    clear_at_start(gain_out, 1)
    seq = pl.program_id(0) + first
    scale = HEAD_DIM**-0.5
    local = q_ref.shape[0]
    for group in range(q_ref.shape[1] // GROUP):
        start = group * GROUP
        both = slice(start, start + GROUP)
        query = stacked_heads(q_ref[:, both])
        grad = stacked_heads(grad_ref[:, both])
        pieces = [ref[:, both] for ref in (own_ref, core_ref, x_ref, diag_ref)]
        exponents, inverse = masked_exponents(orders_ref, seq, query, pieces, span)
        probability = [e * inverse for e in exponents]
        grad_prob = [nt(grad, p[:, HEAD_DIM:GROUP]) for p in pieces]
        delta = functools.reduce(
            jnp.add, [jnp.sum(p * g, axis=1, keepdims=True) for p, g in zip(probability, grad_prob)]
        )
        grad_scores = [(p * (g - delta)).astype(BF16) for p, g in zip(probability, grad_prob)]
        grad_query = functools.reduce(
            jnp.add, [nn(s, p[:, 0:HEAD_DIM]) for s, p in zip(grad_scores, pieces)]
        )
        outs = (own_out, core_out.at[0], x_out, core_out.at[1])
        for out, scores, prob in zip(outs, grad_scores, probability):
            out[:, start : start + HEAD_DIM] = (tn(scores, query) * scale).astype(BF16)
            out[:, start + HEAD_DIM : start + GROUP] = tn(prob.astype(BF16), grad).astype(BF16)
        for head in range(2):
            columns = slice(start + head * HEAD_DIM, start + (head + 1) * HEAD_DIM)
            result, terms = turn_back(
                grad_query[head * local : (head + 1) * local] * scale,
                raw_ref[:, columns],
                cos_ref[...],
                sin_ref[...],
                gain_ref[...],
            )
            q_back_ref[:, columns] = result
            gain_out[...] += terms


def attend_back(orders, q, kv, others, grad, raw, cosine, sine, gain, first, count, local, into, after=()):
    columns = q.shape[1]
    block = (local, columns)
    at_whole = lambda s, o: (s + first, 0)
    at_half = lambda s, o: (s, 0)
    fixed = lambda s, o: (0, 0)
    ins = [(q, block, at_whole), (kv, block, at_half)] + [(k, block, at_half) for k in others]
    ins += [(grad, block, at_half), (raw, block, at_whole)]
    ins += [(cosine, (local, HEAD_DIM), at_whole), (sine, (local, HEAD_DIM), at_whole)]
    ins += [(gain, (1, HEAD_DIM), fixed)]
    if into is not None:
        ins.append((into, None, None))
    piece = ((count * local, columns), BF16, block, at_half)
    return call(
        functools.partial(attend_back_kernel, first=first, span=local // 2),
        (count,),
        ins,
        [(q.shape, BF16, block, at_whole)]
        + [piece] * 2
        + [((2, count * local, columns), BF16, (2, local, columns), lambda s, o: (0, s, 0))]
        + [((8, HEAD_DIM), F32, (8, HEAD_DIM), fixed)],
        scalars=(orders,),
        alias=None if into is None else {0: len(ins) - 1},
        after=after,
        name="attend_back",
        cost=25,
    )


def key_back_kernel(mine_ref, core_ref, x_ref, raw_ref, cos_ref, sin_ref, gain_ref, *rest):
    out_ref, gain_out = rest[-2:]
    clear_at_start(gain_out, 1)
    for group in range(mine_ref.shape[1] // GROUP):
        start = group * GROUP
        both = slice(start, start + GROUP)
        parts = [ref[:, both].astype(F32) for ref in (mine_ref, core_ref.at[0], x_ref)]
        grad = functools.reduce(jnp.add, parts)
        result, terms = turn_back(
            grad[:, 0:HEAD_DIM],
            raw_ref[:, start : start + HEAD_DIM],
            cos_ref[...],
            sin_ref[...],
            gain_ref[...],
        )
        out_ref[:, start : start + HEAD_DIM] = result
        out_ref[:, start + HEAD_DIM : start + GROUP] = grad[:, HEAD_DIM:GROUP].astype(BF16)
        gain_out[...] += terms


def key_back(mine, core, x, raw, cosine, sine, gain, first, count, local, tokens, into, after=()):
    columns = mine.shape[1]
    block = (local, columns)
    at_whole = lambda s: (s + first, 0)
    at_half = lambda s: (s, 0)
    fixed = lambda s: (0, 0)
    ins = [(mine, block, at_half), (core, (1,) + block, lambda s: (0, s, 0)), (x, block, at_half)]
    ins += [(raw, block, at_half)]
    ins += [(cosine, (local, HEAD_DIM), at_whole), (sine, (local, HEAD_DIM), at_whole)]
    ins += [(gain, (1, HEAD_DIM), fixed)]
    if into is not None:
        ins.append((into, None, None))
    return call(
        key_back_kernel,
        (count,),
        ins,
        [
            ((tokens, columns), BF16, block, at_whole),
            ((8, HEAD_DIM), F32, (8, HEAD_DIM), fixed),
        ],
        alias=None if into is None else {0: len(ins) - 1},
        after=after,
        name="key_back",
        cost=5,
    )


def feed_kernel(x_ref, c_ref, g_ref, u_ref, d_ref, *outs, rows, steps):
    step, pieces = pl.program_id(0), len(outs) // 3

    def fill(hidden_ref, gate_ref, up_ref):
        for at in range(0, x_ref.shape[0], rows):
            part = pl.ds(at, rows)
            gate = nn(x_ref[part, :], g_ref[...])
            upward = nn(x_ref[part, :], u_ref[...])
            grad = nn(c_ref[part, :], d_ref[...])
            sigmoid = jax.nn.sigmoid(gate)
            silu = gate * sigmoid
            hidden_ref[part, :] = (silu * upward).astype(BF16)
            slope = sigmoid + silu * (1.0 - sigmoid)
            gate_ref[part, :] = (grad * upward * slope).astype(BF16)
            up_ref[part, :] = (grad * silu).astype(BF16)

    for piece in range(pieces):
        run = functools.partial(fill, *outs[piece::pieces])
        if pieces == 1:
            run()
        else:
            pl.when(step // steps == piece)(run)


def feed(x, c, weights, starts, tile, piece, pieces, after=()):
    tokens, width = x.shape
    steps = piece // tile
    whole = lambda j: (0, 0)
    ins = [(x, (tokens, width), whole), (c, (tokens, width), whole)]
    for start in starts:
        ins.append((weights, (width, tile), lambda j, start=start: (0, start // tile + j)))
    outs = [
        ((tokens, piece), BF16, (tokens, tile), lambda j, at=at: (0, jnp.clip(j - at * steps, 0, steps - 1)))
        for _ in range(3)
        for at in range(pieces)
    ]
    found = call(
        functools.partial(feed_kernel, rows=min(256, tokens), steps=steps),
        (steps * pieces,),
        ins,
        outs,
        after=after,
        name="feed",
        cost=2 + piece * pieces * 0.0165,
    )
    return [found[kind * pieces : (kind + 1) * pieces] for kind in range(3)]


def nt_kernel(*refs, count):
    out_ref = refs[-1]
    total = None
    for left_ref, w_ref in zip(refs[:count], refs[count : 2 * count]):
        product = nt(left_ref[...], w_ref[...])
        total = product if total is None else total + product
    out_ref[...] = total.astype(out_ref.dtype)


def nt_product(terms, row, rows, after=()):
    width = terms[0][1].shape[0]
    tile = min(512, width)
    ins = [(left, (rows, left.shape[1]), lambda j: (row // rows, 0)) for left, _, _ in terms]
    ins += [
        (weights, (tile, left.shape[1]), lambda j, at=at // left.shape[1]: (j, at))
        for left, weights, at in terms
    ]
    return call(
        functools.partial(nt_kernel, count=len(terms)),
        (width // tile,),
        ins,
        [((rows, width), BF16, (rows, tile), lambda j: (0, j))],
        after=after,
        name="nt_product",
        cost=1.5 + rows * sum(left.shape[1] for left, _, _ in terms) * 6.0e-6,
    )[0]


def nn_kernel(x_ref, w_ref, out_ref):
    out_ref[...] = nn(x_ref[...], w_ref[...]).astype(out_ref.dtype)


def nn_product(left, weights, first_column, columns, row, rows, after=()):
    width = weights.shape[0]
    tile = min(512, columns)
    return call(
        nn_kernel,
        (columns // tile,),
        [
            (left, (rows, width), lambda j: (row // rows, 0)),
            (weights, (width, tile), lambda j: (0, first_column // tile + j)),
        ],
        [((rows, columns), BF16, (rows, tile), lambda j: (0, j))],
        after=after,
        name="nn_product",
        cost=6,
    )[0]


def output_join_kernel(
    at_ref, x_ref, mine_ref, other_ref, w_mine_ref, w_same_ref, w_swap_ref, gain_ref, *rest, steps
):
    middle_ref, normed_ref, rows_ref = rest[-3:]
    step = pl.program_id(0)
    tile = x_ref.shape[1]
    is_first, core = at_ref[0] == 0, at_ref[1]
    direct = (step * 2 // steps) == core
    mine, other, w_mine = mine_ref[...], other_ref[...], w_mine_ref[...]
    w_other = jnp.where(direct, w_same_ref[...], w_swap_ref[...])
    total = nt(jnp.where(is_first, mine, other), jnp.where(is_first, w_mine, w_other))
    total += nt(jnp.where(is_first, other, mine), jnp.where(is_first, w_other, w_mine))
    columns = pl.ds(pl.multiple_of(step * tile, tile), tile)
    rows_ref[:, columns] = x_ref[...].astype(F32) + total

    @pl.when(step == steps - 1)
    def _():
        middle = rows_ref[...]
        middle_ref[...] = middle
        normed_ref[...] = (unit_norm(middle)[0] * gain_ref[...]).astype(BF16)


def output_join(at, x, mine, other, weights, block, same, swapped, gain, row, into, after=()):
    tokens, width = x.shape
    rows, columns = mine.shape
    tile = min(512, width // 2)
    steps = width // tile
    fixed = lambda j, a: (0, 0)
    fetched = lambda j, a: (j % (steps // 2), 0)
    ins = [
        (x, (rows, tile), lambda j, a: (row // rows, j)),
        (mine, (rows, columns), fixed),
        (other, (rows, columns), fixed),
        (weights, (tile, columns), lambda j, a: (j, block)),
        (same, (tile, columns), fetched),
        (swapped, (tile, columns), fetched),
        (gain, (1, width), fixed),
    ]
    alias = None
    if into is not None:
        alias = {o: len(ins) + o for o in range(2)}
        ins += [(array, None, None) for array in into]
    out = lambda kind: ((tokens, width), kind, (rows, width), lambda j, a: (row // rows, 0))
    return call(
        functools.partial(output_join_kernel, steps=steps),
        (steps,),
        ins,
        [out(F32), out(BF16)],
        scratch=[pltpu.VMEM((rows, width), F32)],
        scalars=(at,),
        alias=alias,
        after=after,
        name="output_join",
        cost=15,
    )


def turn_kernel(order_ref, *refs):
    ins, outs = refs[:4], refs[4:]
    step = pl.program_id(0)

    def fill(out_ref):
        for at, ref in enumerate(ins):
            out_ref[at * BLOCK : (at + 1) * BLOCK, :] = ref[...].T

    pl.when(step < 2)(lambda: fill(outs[0]))
    pl.when(step >= 2)(lambda: fill(outs[1]))


def turned_blocks(order, left, after=()):
    tokens, width = left.shape
    ins = [(left, (tokens, BLOCK), lambda j, o, at=at: (0, o[4 * j + at])) for at in range(4)]
    out = lambda spot: ((width // 2, tokens), BF16, (4 * BLOCK, tokens), spot)
    return call(
        turn_kernel,
        (width // BLOCK // 4,),
        ins,
        [out(lambda j, o: (jnp.minimum(j, 1), 0)), out(lambda j, o: (jnp.maximum(j - 2, 0), 0))],
        scalars=(order,),
        after=after,
        name="turned_blocks",
        cost=6,
    )


def grad_kernel(*refs, plan, outs):
    step, begin, used = pl.program_id(0), 0, 0
    out_refs = refs[-outs:]

    def fill(left_refs, right_refs):
        for at, out in enumerate(out_refs):
            size, total = out.shape[0], None
            rows = pl.ds(at * size, size)
            for left_ref, pieces in zip(left_refs, right_refs):
                start = 0
                for piece in pieces:
                    tokens = piece.shape[0]
                    product = nn(left_ref[rows, start : start + tokens], piece[...])
                    total = product if total is None else total + product
                    start += tokens
            out[...] = total.astype(BF16)

    for pieces, count in plan:
        part = refs[used : used + 2 + 2 * pieces]
        run = functools.partial(fill, part[:2], (part[2 : 2 + pieces], part[2 + pieces :]))
        if len(plan) == 1:
            run()
        else:
            pl.when((step >= begin) & (step < begin + count))(run)
        begin, used = begin + count, used + 2 + 2 * pieces


def grad_product(parts, tile, cuts, after=()):
    width, tokens = parts[0][0][0].shape
    ins, begin, plan = [], 0, []
    for lefts, rights in parts:
        count = rights[0][0].shape[1] // tile
        ins += [(left, left.shape, lambda j: (0, 0)) for left in lefts]
        spot = lambda j, begin=begin, count=count: (0, jnp.clip(j - begin, 0, count - 1))
        ins += [(piece, (piece.shape[0], tile), spot) for pieces in rights for piece in pieces]
        plan.append((len(rights[0]), count))
        begin += count
    return call(
        functools.partial(grad_kernel, plan=plan, outs=len(cuts)),
        (begin,),
        ins,
        [((cut, begin * tile), BF16, (cut, tile), lambda j: (0, j)) for cut in cuts],
        after=after,
        name="grad_product",
        cost=3.5 + begin * tile * 0.0047,
    )


def join_kernel(x_ref, own_ref, other_ref, gain_ref, *rest):
    middle_ref, normed_ref = rest[-2:]
    middle = x_ref[...].astype(F32) + (own_ref[...].astype(F32) + other_ref[...].astype(F32))
    middle_ref[...] = middle
    normed_ref[...] = (unit_norm(middle)[0] * gain_ref[...]).astype(BF16)


def join(x, own, other, gain, row, into, after=()):
    tokens, width = x.shape
    rows = own.shape[0]
    tile = min(256, rows)
    block = (tile, width)
    at_whole = lambda j: (row // tile + j, 0)
    at_half = lambda j: (j, 0)
    ins = [(x, block, at_whole), (own, block, at_half), (other, block, at_half)]
    ins += [(gain, (1, width), lambda j: (0, 0))]
    alias = None
    if into is not None:
        alias = {o: len(ins) + o for o in range(2)}
        ins += [(array, None, None) for array in into]
    return call(
        join_kernel,
        (rows // tile,),
        ins,
        [((tokens, width), F32, block, at_whole), ((tokens, width), BF16, block, at_whole)],
        alias=alias,
        after=after,
        name="join",
        cost=7.5,
    )


def norm_back_kernel(v_ref, base_ref, own_ref, other_ref, gain_ref, *rest, outs):
    out_refs, terms_ref = rest[-outs - 1 : -1], rest[-1]
    clear_at_start(terms_ref, 1)
    own = own_ref[...].astype(F32)
    unit, inverse = unit_norm(v_ref[...].astype(F32))
    grad_normed = (own + other_ref[...].astype(F32)) * gain_ref[...]
    mean = jnp.mean(grad_normed * unit, axis=-1, keepdims=True)
    result = base_ref[...].astype(F32) + inverse * (grad_normed - unit * mean)
    for ref in out_refs:
        ref[...] = result.astype(ref.dtype)
    terms_ref[...] += jnp.sum((own * unit).reshape(-1, 8, own.shape[1]), axis=0)


def norm_back(values, base, own, other, gain, row, types, into, after=()):
    tokens, width = values.shape
    rows = own.shape[0]
    tile = min(256, rows)
    block = (tile, width)
    at_whole = lambda j: (row // tile + j, 0)
    at_half = lambda j: (j, 0)
    fixed = lambda j: (0, 0)
    ins = [(values, block, at_whole), (base, block, at_whole)]
    ins += [(own, block, at_half), (other, block, at_half), (gain, (1, width), fixed)]
    alias = None
    if into is not None:
        alias = {o: len(ins) + o for o in range(len(types))}
        ins += [(array, None, None) for array in into]
    return call(
        functools.partial(norm_back_kernel, outs=len(types)),
        (rows // tile,),
        ins,
        [((tokens, width), kind, block, at_whole) for kind in types]
        + [((8, width), F32, (8, width), fixed)],
        alias=alias,
        after=after,
        name="norm_back",
        cost=7.5,
    )


def sum_kernel(*refs):
    own, other = refs[1][...].astype(F32), refs[2][...].astype(F32)
    refs[-1][...] = (refs[0][...] + (own + other)).astype(BF16)


def sum_rows(values, parts, row, into, after=()):
    tokens, width = values.shape
    rows = parts[0].shape[0]
    tile = min(256, rows)
    block = (tile, width)
    at_whole = lambda j: (row // tile + j, 0)
    ins = [(values, block, at_whole)] + [(part, block, lambda j: (j, 0)) for part in parts]
    if into is not None:
        ins.append((into, None, None))
    return call(
        sum_kernel,
        (rows // tile,),
        ins,
        [((tokens, width), BF16, block, at_whole)],
        alias=None if into is None else {0: len(ins) - 1},
        after=after,
        name="sum_rows",
        cost=6,
    )[0]


def terms_kernel(v_ref, own_ref, terms_ref):
    clear_at_start(terms_ref, 1)
    unit = unit_norm(v_ref[...].astype(F32))[0]
    terms_ref[...] += jnp.sum((own_ref[...].astype(F32) * unit).reshape(-1, 8, unit.shape[1]), axis=0)


def gain_terms(values, own, row, after=()):
    width = values.shape[1]
    rows = own.shape[0]
    tile = min(256, rows)
    return call(
        terms_kernel,
        (rows // tile,),
        [
            (values, (tile, width), lambda j: (row // tile + j, 0)),
            (own, (tile, width), lambda j: (j, 0)),
        ],
        [((8, width), F32, (8, width), lambda j: (0, 0))],
        after=after,
        name="gain_terms",
        cost=4,
    )[0]


def add_kernel(*refs, widths):
    start = 0
    for at, width in enumerate(widths):
        left, right = refs[2 * at][...].astype(F32), refs[2 * at + 1][...].astype(F32)
        refs[-1][:, start : start + width] = (left + right.reshape(left.shape)).astype(BF16)
        start += width


def add_rows(parts, after=()):
    rows = parts[0][0].shape[0]
    widths = [left.shape[1] for left, _ in parts]
    tile, total = rows // 2, sum(widths)
    ins = []
    for left, right in parts:
        ins.append((left, (tile, left.shape[1]), lambda j: (j, 0)))
        if right.ndim == 3:
            ins.append((right, (1, tile, right.shape[2]), lambda j: (1, j, 0)))
        else:
            ins.append((right, (tile, right.shape[1]), lambda j: (j, 0)))
    return call(
        functools.partial(add_kernel, widths=widths),
        (2,),
        ins,
        [((rows, total), BF16, (tile, total), lambda j: (j, 0))],
        after=after,
        name="add_rows",
        cost=3,
    )[0]


def split_heads(both, which):
    cuts = range(which, both.shape[1] // HEAD_DIM, 2)
    return jnp.concatenate([both[:, at * HEAD_DIM : (at + 1) * HEAD_DIM] for at in cuts], axis=1)


def behind(value, *others):
    return lax.optimization_barrier((value,) + others)[0]


def shards(
    inputs,
    span_order,
    first_gain,
    query_proj,
    key_matrix,
    value_matrix,
    query_norm,
    key_norm,
    output_proj,
    second_gain,
    gate_proj,
    up_proj,
    down_proj,
    cotangent,
):
    seqs, local, width = inputs.shape
    tokens = seqs * local
    span = local // 2
    shard = query_proj.shape[0]
    head_shard = query_norm.shape[0]
    columns = query_proj.shape[1]
    groups = columns // GROUP
    units = gate_proj.shape[1]
    third = units // 3
    dp_size, tp_size = lax.axis_size("dp"), lax.axis_size("tp")
    ctx, tp_at = lax.axis_index("ctx"), lax.axis_index("tp")
    x_at, core_at = ctx // 2, ctx % 2
    share = lax.axis_index("dp") * 4 + ctx
    half_rows = tokens // 2
    half_seqs = seqs // 2
    pair = tp_size == 2

    def swap(axis, pairs, value, name):
        with jax.named_scope(name):
            return lax.ppermute(value, axis, pairs)

    tp_swap = lambda value, name: swap("tp", TP_SWAP, value, name + "_over_tp")
    core_swap = lambda value, name: swap("ctx", CORE_SWAP, value, name + "_over_core")
    x_swap = lambda value, name: swap("ctx", X_SWAP, value, name + "_over_x")

    def tp_start(part, name):
        if pair:
            return part, tp_swap(part, name)
        return lax.psum(part, "tp"), jnp.zeros_like(part)

    small = [first_gain, second_gain, jnp.pad(query_norm, (0, shard - head_shard))]
    small += [jnp.pad(key_norm, (0, shard - head_shard))]
    small = jnp.pad(jnp.stack(small), ((0, shard - len(small)), (0, BLOCK - shard)))
    shard_one = pack_first(
        query_proj, key_matrix, value_matrix, output_proj, gate_proj, up_proj, down_proj, small, third
    )
    weights = lax.all_gather(shard_one, ("dp", "ctx"), axis=0, tiled=True)

    pairs = span_order.reshape(seqs, 4, 2)
    relative = jnp.stack([ctx, ctx ^ 1, ctx ^ 2, ctx ^ 3])
    orders = jnp.take(pairs, relative, axis=1).reshape(seqs, 8)
    places = (
        orders[:, 0:2, None] * span + jnp.arange(span, dtype=jnp.int32)[None, None, :]
    ).reshape(tokens)
    half_dim = HEAD_DIM // 2
    frequency = ROPE_BASE ** (-(jnp.arange(half_dim, dtype=F32) * (2.0 / HEAD_DIM)))
    angles = places.astype(F32)[:, None] * frequency[None, :]
    cosine, sine = jnp.cos(angles), jnp.sin(angles)
    cosine = jnp.concatenate([cosine, cosine], axis=1)
    sine = jnp.concatenate([-sine, sine], axis=1)
    dps = jnp.arange(dp_size, dtype=jnp.int32)
    other_first = jnp.stack([1 - x_at, x_at])
    cores = jnp.stack([1 - core_at, core_at])
    order = cores[:, None, None] + 2 * other_first[None, :, None] + 4 * dps[None, None, :]
    order = order.reshape(-1).astype(jnp.int32)
    spot = jnp.stack([tp_at, core_at]).astype(jnp.int32)
    input_rows = inputs.reshape(tokens, width)
    cot_rows = cotangent.reshape(tokens, width)
    shard_two = pack_second(gate_proj, up_proj, down_proj, third, after=(shard_one,))

    def turned(left, name, after=()):
        to_core, own = turned_blocks(order, left, after=after)
        return own, core_swap(to_core, name)

    cot_turned = turned(cot_rows, "cotangent", after=(shard_two,))
    weights, cosine, sine, orders, order, spot, cot_turned, shard_two = lax.optimization_barrier(
        (weights, cosine, sine, orders, order, spot, cot_turned, shard_two)
    )

    small = weights[:, 3 * columns + 3 * third :].reshape(-1, shard, BLOCK)[:, 0:4, 0:shard]
    small = jnp.transpose(small, (1, 0, 2)).astype(F32)
    gain_first, gain_second = small[0].reshape(1, width), small[1].reshape(1, width)
    gain_query = small[2, :, 0:head_shard].reshape(1, HEAD_DIM)
    gain_key = small[3, :, 0:head_shard].reshape(1, HEAD_DIM)

    feed_one = norm_rows(input_rows, gain_first)
    kv, raw_kv, latest = [], [], ()
    for h in range(2):
        part = project(
            feed_one, weights, cosine, sine, gain_key, groups, groups, 1, h * half_rows, half_rows, after=latest
        )
        kv.append(part[0])
        raw_kv.append(part[1])
        latest = (part[0],)
        if pair and h == 0:
            half_width = width // 2
            sent = lax.dynamic_slice(
                behind(weights, part[0]), (core_at * half_width, 2 * columns), (half_width, columns)
            )
            output_same = tp_swap(sent, "output_proj")
            latest = (sent,)
    across = [x_swap(kv[0], "kv0")]
    q, raw_q = project(
        feed_one, weights, cosine, sine, gain_query, groups, 0, 2, 0, tokens, after=(kv[1],)
    )
    one_turned = turned(feed_one, "normed_one", after=(q,))
    across.append(x_swap(behind(kv[1], across[0], one_turned[0]), "kv1"))
    others = [
        (core_swap(kv[h], f"kv{h}"), across[h], core_swap(across[h], f"kv{h}_across"))
        for h in range(2)
    ]
    shard_two = behind(shard_two, across[1], *others[0])
    weights_two = lax.all_gather(shard_two, ("dp", "ctx"), axis=0, tiled=True)

    settled = ()
    if pair:
        output_swapped = core_swap(behind(output_same, across[1]), "output_proj")
        settled = (output_swapped,)
    attended, joined = [], None
    for h in range(2):
        attended.append(
            attend(
                orders, q, kv[h], others[h], h * half_seqs, half_seqs, local, after=tuple(attended) or settled
            )
        )
    attended_pair = attended, [core_swap(part, "attended") for part in attended]
    if pair:
        other_heads = [tp_swap(part, f"attended{h}") for h, part in enumerate(attended)]
        for h in range(2):
            joined = output_join(
                spot, input_rows, attended[h], other_heads[h], weights, 2,
                output_same, output_swapped, gain_second, h * half_rows, joined,
            )
    else:
        for h in range(2):
            part = nt_product([(attended[h], weights, 2 * columns)], 0, half_rows)
            started = tp_start(part, f"attended{h}")
            joined = join(input_rows, *started, gain_second, h * half_rows, joined)
    middle, feed_two = joined

    cut = width // 4
    tile = min(512, third)

    class Gradient:
        def __init__(self, name, parts, after=()):
            self.name = name
            to_x, self.keep = grad_product(parts, tile, (cut, cut), after=after)
            self.from_x = x_swap(to_x, name)

    def over_dp(name, grads, after=()):
        summed = add_rows([(grad.keep, grad.from_x) for grad in grads], after=after)
        with jax.named_scope(name + "_over_dp"):
            return summed, lax.psum_scatter(summed, "dp", scatter_dimension=0, tiled=True)

    def with_core(values, name):
        return [([value], [core_swap(value, name)]) for value in values]

    names = ("hidden", "gate_back", "up_back")
    starts = [3 * columns + at * third for at in range(3)]
    settled = (*attended_pair[1], one_turned[1])
    two_turned = turned(feed_two, "normed_two", after=settled)
    acts = feed(feed_two, cot_rows, weights, starts, tile, third, 1, after=(two_turned[0],))
    firsts = [([a[0]], [core_swap(a[0], n + "_one")]) for a, n in zip(acts, names)]
    parts = [(cot_turned, firsts[0]), (two_turned, firsts[1]), (two_turned, firsts[2])]
    first_third = Gradient("first_third", parts)
    starts = [at * 2 * third for at in range(3)]
    acts = feed(
        feed_two, cot_rows, weights_two, starts, tile, 2 * third, 1, after=(first_third.keep,)
    )
    seconds = [([a[0]], [core_swap(a[0], n + "_two")]) for a, n in zip(acts, names)]

    def feed_terms(at, kind):
        place = 3 * columns + kind * third
        return [(firsts[at][0][0], weights, place), (seconds[at][0][0], weights_two, 2 * kind * third)]

    back_terms = feed_terms(1, 0) + feed_terms(2, 1)
    back, out_started = [], []
    part = nt_product(back_terms, 0, half_rows)
    back.append(tp_start(part, "back0"))
    down_two = Gradient("down_two", [(cot_turned, seconds[0])], after=(part,))
    landed = (seconds[1][1][0], seconds[2][1][0])
    part = nt_product(back_terms, half_rows, half_rows, after=(down_two.keep, *landed))
    back.append(tp_start(part, "back1"))
    done, first_out = over_dp("first_third", [first_third], after=(part,))
    gate_two = Gradient("gate_two", [(two_turned, seconds[1])], after=(done,))

    def out_half(h, after):
        part = nt_product(feed_terms(0, 2), h * half_rows, half_rows, after=after)
        out_started.append(tp_start(part, f"out{h}"))
        return part

    grads, q_back, k_back, pieces, one = None, None, None, [], []
    sums = {"second": 0.0, "query": 0.0, "key": 0.0, "first": 0.0}

    def middle_half(h, after):
        *found, second = norm_back(
            middle, cot_rows, *back[h], gain_second, h * half_rows, (F32, BF16), grads, after=after
        )
        sums["second"] = sums["second"] + jnp.sum(second, axis=0)
        return found, nn_product(found[1], weights, 2 * columns, columns, h * half_rows, half_rows)

    def attention_half(h, grad_attended, after):
        found, to_own, to_x, to_core, query = attend_back(
            orders, q, kv[h], others[h], grad_attended, raw_q, cosine, sine, gain_query,
            h * half_seqs, half_seqs, local, q_back, after=after,
        )
        sums["query"] = sums["query"] + jnp.sum(query, axis=0)
        return found, to_own, to_x, core_swap(to_core, f"kv_grad{h}")

    def send_keys(h, held, after):
        to_own, to_x, from_core = held
        sent = add_rows([(to_x, from_core)], after=after)
        pieces.append((to_own, from_core, x_swap(sent, f"kv_grad{h}")))
        return sent

    def key_half(h, after):
        found, key = key_back(
            *pieces[h], raw_kv[h], cosine, sine, gain_key, h * half_seqs, half_seqs, local,
            tokens, k_back, after=after,
        )
        sums["key"] = sums["key"] + jnp.sum(key, axis=0)
        return found

    def one_half(h, after):
        terms = [(q_back, weights, 0), (k_back, weights, columns)]
        part = nt_product(terms, h * half_rows, half_rows, after=after)
        one.append(tp_start(part, f"one{h}"))
        return part

    grads, grad_attended = middle_half(0, (gate_two.keep,))
    part = out_half(0, (grad_attended,))
    q_back, *held = attention_half(0, grad_attended, (part,))
    grads, grad_attended = middle_half(1, (held[0],))
    grad_middle, middle_low = grads
    sent = send_keys(0, held, (grad_attended,))
    done, more_out = over_dp("down_gate_two", [down_two, gate_two], after=(sent, first_out))
    part = out_half(1, (done,))
    up_two = Gradient("up_two", [(two_turned, seconds[2])], after=(part,))
    landed = (pieces[0][2], out_started[0][1])
    q_back, *held = attention_half(1, grad_attended, (up_two.keep, *landed))
    q_pair = [q_back], [core_swap(q_back, "query_back")]
    k_back = key_half(0, (held[0],))
    sent = send_keys(1, held, (k_back,))
    outputs = sum_rows(middle, out_started[0], 0, None, after=(sent,))
    part = one_half(0, (outputs,))
    done, up_out = over_dp("up_two", [up_two], after=(part, more_out))
    query_grad = Gradient("query", [(one_turned, q_pair)], after=(done, out_started[1][1]))
    low_turned = turned(middle_low, "grad_middle", after=(query_grad.keep,))
    k_back = key_half(1, (low_turned[0],))
    outputs = sum_rows(middle, out_started[1], half_rows, outputs, after=(k_back,))
    part = one_half(1, (outputs,))
    k_pair = [k_back], [core_swap(k_back, "key_back")]
    key_grad = Gradient("key", [(one_turned, k_pair)], after=(part,))
    output_grad = Gradient("output", [(low_turned, attended_pair)], after=(key_grad.keep,))
    latest = (output_grad.keep,)
    for h in range(2):
        part = gain_terms(input_rows, one[h][0], h * half_rows, after=latest)
        latest = (part,)
        sums["first"] = sums["first"] + jnp.sum(part, axis=0)
    result = None
    for h in range(2):
        result = norm_back(
            input_rows, grad_middle, *one[h], gain_first, h * half_rows, (BF16,), result, after=latest
        )[0:1]
        latest = ()
    last = [query_grad, key_grad, output_grad]
    done, heads_out = over_dp("query_key_output", last, after=(result[0],))

    if not pair:
        sums["first"], sums["second"] = sums["first"] / tp_size, sums["second"] / tp_size
    totals = jnp.concatenate([sums[name] for name in ("first", "second", "query", "key")])
    totals = lax.psum(behind(totals, done), ("dp", "ctx", "tp"))
    cut_total = lambda start, size: lax.dynamic_slice(totals, (start + share * size,), (size,))

    grad_kv = heads_out[:, columns : 2 * columns].astype(F32)
    down_out, gate_out, up_first = [first_out[:, at * third : (at + 1) * third] for at in range(3)]
    beside = lambda left, right: jnp.concatenate([left, right], axis=1).astype(F32)
    return (
        outputs.reshape(inputs.shape),
        result[0].reshape(inputs.shape),
        cut_total(0, shard),
        heads_out[:, 0:columns].astype(F32),
        split_heads(grad_kv, 0),
        split_heads(grad_kv, 1),
        cut_total(2 * width, head_shard),
        cut_total(2 * width + HEAD_DIM, head_shard),
        heads_out[:, 2 * columns :].astype(F32).T,
        cut_total(width, shard),
        beside(gate_out, more_out[:, 2 * third :]),
        beside(up_first, up_out),
        beside(down_out, more_out[:, 0 : 2 * third]).T,
    )


def solution(mesh):
    rows = P(("dp", "ctx"))
    columns = P(("dp", "ctx"), "tp")
    turned = P("tp", ("dp", "ctx"))
    tokens = P("dp", "ctx", None)
    in_specs = (
        (tokens, P("dp", None), rows, columns, columns, columns, rows, rows, turned, rows)
        + (columns, columns, turned, tokens)
    )
    out_specs = (
        (tokens, tokens, rows, columns, columns, columns, rows, rows, turned, rows)
        + (columns, columns, turned)
    )
    return jax.shard_map(shards, mesh=mesh, in_specs=in_specs, out_specs=out_specs, check_vma=False)
```

time: 1160 us -> 821 us (0.71)
  waiting for transfers between devices: 505 us -> 213 us
  other arithmetic: 82.7 us -> 13.1 us
  Pallas kernels: 445 us -> 478 us
  local copies, waits for them, and re-layouts: 37.2 us -> 25.5 us
    ppermute x33 -> x41, waiting for transfers between devices: 401 us -> 88.6 us  [swap(): return lax.ppermute(value, axis, pairs)]
    convert_element_type x20 -> x3, other arithmetic: 67.7 us -> 3.64 us  [the longest x2 3.64 us: shards(): jnp.concatenate([left, right], axis=1).astype(F32)]
    pallas_call x35 -> x49, Pallas kernels: 445 us -> 478 us  [call(): pl.pallas_call(body, grid_spec=pltpu.PrefetchScalarGridSpec(num_scalar_pr...]
    unnamed x118 -> x61, local copies, waits for them, and re-layouts: 26.4 us -> 15.5 us
    ppermute x33 -> x41, starting transfers between devices: 21.8 us -> 23.8 us  [swap(): return lax.ppermute(value, axis, pairs)]
  transfers between devices with their start and end apart: 42 -> 47, of which waited for: 15 -> 14; matrix products, arithmetic and copies ran while one was open for 8% -> 2% of each run, Pallas kernels for 29% -> 57%
where the time goes in v2:
time: 821 us; the launch traced here: 813 us
  Pallas kernels  478 us (58%)
  waiting for transfers between devices  213 us (26%)
  blocking collectives  44.3 us (5%)
  local copies, waits for them, and re-layouts  25.5 us (3%)
  starting transfers between devices  24.3 us (3%)
  between operations  15 us (2%)
  other arithmetic  13.1 us (2%)
    pallas_call x49, Pallas kernels, call(): pl.pallas_call(body, grid_spec=pltpu.PrefetchScalarGridSpec(num_scalar_pr...  478 us
    all_gather x1, waiting for transfers between devices, shards(): weights = lax.all_gather(shard_one, ('dp', 'ctx'), axis=0, tiled=True)  115 us
    ppermute x41, waiting for transfers between devices, swap(): return lax.ppermute(value, axis, pairs)  88.6 us
    psum x1, blocking collectives, shards(): totals = lax.psum(behind(totals, done), ('dp', 'ctx', 'tp'))  44.3 us
    ppermute x41, starting transfers between devices, swap(): return lax.ppermute(value, axis, pairs)  23.8 us
  transfers between devices with their start and end apart: 47, of which 14 were waited for; matrix products, arithmetic and copies ran while one was open for 2% of the time, Pallas kernels for 57%

profile of v2, /device:TPU:0, one launch (start us, length us, event | category | flops | bytes accessed | tf_op | source)
XLA Modules:
  0.0 812.7 jit_solution(977748780727202322)
XLA Ops:
  30.8 115.1 %all-gather.3.cloned.1.call-done.refs_1_.refs_4_.refs_2_.refs_3_.refs_6_ = bf16[2048,6272]{1,0:T(8,128)(2,1)} async-done(((bf16[128,6272]{1,0:T(8,128)(2,1)}), bf16[2048,6272]{1,0:T(8,128)(2,1)}) %all-gather.3.cloned.1.call-update) | async-done | bytes 25690128 | tf_op jit(solution)/shard_map/all_gather | solution.py:837
  174.3 9.9 %project.5 = (bf16[1024,1024]{1,0:T(8,128)(2,1)}, f32[1024,1024]{1,0:T(8,128)}) custom-call(bf16[1024,2048]{1,0:T(8,128)(2,1)} %norm_rows.1.refs_0_.refs_1_.refs_2_.refs_3_.refs_4_, bf16[2048,6272]{1,0:T(8,128)(2,1)} %all-gather.3.cloned.1.call-done.refs_1_.refs_4_.refs_2_.refs_3_.refs_6_, f32[1024,128]{1,0:T(8,128)} %get-tuple-element.92.refs_2_.refs_8_.refs_4_, ...), custom_call_target="tpu_custom_call" | custom-call | flops 99999997952 | tf_op jit(solution)/shard_map/project/pallas_call | solution.py:56
  191.6 21.7 %collective-permute-done.7.refs_5_ = bf16[1024,1024]{1,0:T(8,128)(2,1)} collective-permute-done((bf16[1024,1024]{1,0:T(8,128)(2,1)}, bf16[1024,1024]{1,0:T(8,128)(2,1)}, u32[]{:S(2)}, u32[]{:S(2)}) %collective-permute-start.7) | collective-permute-done | bytes 2097184 | tf_op jit(solution)/shard_map/output_proj_over_tp/ppermute | solution.py:820
  226.9 11.0 %attend.2.refs_6_.refs_2_ = bf16[512,1024]{1,0:T(8,128)(2,1)} custom-call(s32[4,8]{1,0:T(4,128)} %copy-done.7, bf16[1024,1024]{1,0:T(8,128)(2,1)} %get-tuple-element.97.refs_5_.refs_1_, bf16[512,1024]{1,0:T(8,128)(2,1)} %get-tuple-element.94.refs_2_, bf16[512,1024]{1,0:T(8,128)(2,1)} %copy-done.27, bf16[512,1024]{1,0:T(8,128)(2,1)} %collective-permute-done.2.refs_4_, ...), custom_call_target="tpu_custom_call" | custom-call | flops 109999996928 | tf_op jit(solution)/shard_map/attend/pallas_call | solution.py:56
  239.4 11.0 %attend.3.refs_2_.refs_3_ = bf16[512,1024]{1,0:T(8,128)(2,1)} custom-call(s32[4,8]{1,0:T(4,128)} %copy-done.7, bf16[1024,1024]{1,0:T(8,128)(2,1)} %get-tuple-element.97.refs_5_.refs_1_, bf16[512,1024]{1,0:T(8,128)(2,1)} %get-tuple-element.100.refs_5_.refs_2_, bf16[512,1024]{1,0:T(8,128)(2,1)} %collective-permute-done.1.refs_3_, ...), custom_call_target="tpu_custom_call" | custom-call | flops 109999996928 | tf_op jit(solution)/shard_map/attend/pallas_call | solution.py:56
  252.0 12.0 %collective-permute-done.10.refs_3_ = bf16[512,1024]{1,0:T(8,128)(2,1)S(1)} collective-permute-done((bf16[512,1024]{1,0:T(8,128)(2,1)}, bf16[512,1024]{1,0:T(8,128)(2,1)S(1)}, u32[]{:S(2)}, u32[]{:S(2)}) %collective-permute-start.10) | collective-permute-done | bytes 1048608 | tf_op jit(solution)/shard_map/attended0_over_tp/ppermute | solution.py:820
  265.1 13.9 %output_join.2 = (f32[1024,2048]{1,0:T(8,128)}, bf16[1024,2048]{1,0:T(8,128)(2,1)}) custom-call(s32[2]{0:T(128)} %pad_add_fusion.1.refs_0_, bf16[1024,2048]{1,0:T(8,128)(2,1)} %bitcast.61, bf16[512,1024]{1,0:T(8,128)(2,1)} %attend.2.refs_6_.refs_2_, bf16[512,1024]{1,0:T(8,128)(2,1)} %copy-done.28, ...), custom_call_target="tpu_custom_call" | custom-call | flops 149999992832 | tf_op jit(solution)/shard_map/output_join/pallas_call | solution.py:56
  285.8 14.3 %output_join.3 = (f32[1024,2048]{1,0:T(8,128)}, bf16[1024,2048]{1,0:T(8,128)(2,1)}) custom-call(s32[2]{0:T(128)} %pad_add_fusion.1.refs_0_, bf16[1024,2048]{1,0:T(8,128)(2,1)} %bitcast.62, bf16[512,1024]{1,0:T(8,128)(2,1)} %attend.3.refs_2_.refs_3_, bf16[512,1024]{1,0:T(8,128)(2,1)} %collective-permute-done.9.refs_3_, ...), custom_call_target="tpu_custom_call", output_to_operand_aliasing={{0}: (8, {}), {1}: (9, {})} | custom-call | flops 149999992832 | tf_op jit(solution)/shard_map/output_join/pallas_call | solution.py:56
  306.5 21.0 %feed.2 = (bf16[1024,1024]{1,0:T(8,128)(2,1)}, bf16[1024,1024]{1,0:T(8,128)(2,1)}, bf16[1024,1024]{1,0:T(8,128)(2,1)}) custom-call(bf16[1024,2048]{1,0:T(8,128)(2,1)} %get-tuple-element.105.refs_1_.refs_2_.refs_3_.refs_4_.refs_0_, bf16[1024,2048]{1,0:T(8,128)(2,1)} %bitcast.56, ...), custom_call_target="tpu_custom_call" | custom-call | flops 188959997952 | tf_op jit(solution)/shard_map/feed/pallas_call | solution.py:56
  340.3 22.9 %grad_product.7 = (bf16[512,3072]{1,0:T(8,128)(2,1)}, bf16[512,3072]{1,0:T(8,128)(2,1)}) custom-call(bf16[1024,1024]{1,0:T(8,128)(2,1)} %get-tuple-element.111.refs_0_, bf16[1024,1024]{1,0:T(8,128)(2,1)} %copy-done.13, bf16[1024,1024]{1,0:T(8,128)(2,1)} %get-tuple-element.108.refs_2_.refs_0_, bf16[1024,1024]{1,0:T(8,128)(2,1)} %copy-done.20, ...), custom_call_target="tpu_custom_call" | custom-call | flops 179383992320 | tf_op jit(solution)/shard_map/grad_product/pallas_call | solution.py:56
  364.0 35.4 %feed.3 = (bf16[1024,2048]{1,0:T(8,128)(2,1)}, bf16[1024,2048]{1,0:T(8,128)(2,1)}, bf16[1024,2048]{1,0:T(8,128)(2,1)}) custom-call(bf16[1024,2048]{1,0:T(8,128)(2,1)} %get-tuple-element.105.refs_1_.refs_2_.refs_3_.refs_4_.refs_0_, bf16[1024,2048]{1,0:T(8,128)(2,1)} %bitcast.57, ...), custom_call_target="tpu_custom_call" | custom-call | flops 357920014336 | tf_op jit(solution)/shard_map/feed/pallas_call | solution.py:56
  400.0 20.1 %nt_product.6.refs_4_.refs_2_ = bf16[512,2048]{1,0:T(8,128)(2,1)} custom-call(bf16[1024,1024]{1,0:T(8,128)(2,1)} %get-tuple-element.114.refs_6_.refs_0_, bf16[1024,2048]{1,0:T(8,128)(2,1)} %get-tuple-element.118.refs_1_.refs_2_, bf16[1024,1024]{1,0:T(8,128)(2,1)} %get-tuple-element.115.refs_10_.refs_2_, ...), custom_call_target="tpu_custom_call" | custom-call | flops 203743674368 | tf_op jit(solution)/shard_map/nt_product/pallas_call | solution.py:56
  420.3 13.4 %grad_product.8 = (bf16[512,2048]{1,0:T(8,128)(2,1)}, bf16[512,2048]{1,0:T(8,128)(2,1)}) custom-call(bf16[1024,1024]{1,0:T(8,128)(2,1)} %get-tuple-element.111.refs_0_, bf16[1024,1024]{1,0:T(8,128)(2,1)} %copy-done.13, bf16[1024,2048]{1,0:T(8,128)(2,1)} %get-tuple-element.117.refs_2_.refs_1_, bf16[1024,2048]{1,0:T(8,128)(2,1)} %collective-permute-done.18.refs_3_, ...), custom_call_target="tpu_custom_call" | custom-call | flops 131256000512 | tf_op jit(solution)/shard_map/grad_product/pallas_call | solution.py:56
  434.8 20.0 %nt_product.7.refs_2_ = bf16[512,2048]{1,0:T(8,128)(2,1)} custom-call(bf16[1024,1024]{1,0:T(8,128)(2,1)} %get-tuple-element.114.refs_6_.refs_0_, bf16[1024,2048]{1,0:T(8,128)(2,1)} %get-tuple-element.118.refs_1_.refs_2_, bf16[1024,1024]{1,0:T(8,128)(2,1)} %get-tuple-element.115.refs_10_.refs_2_, bf16[1024,2048]{1,0:T(8,128)(2,1)} %get-tuple-element.119.refs_3_.refs_2_, ...), custom_call_target="tpu_custom_call" | custom-call | flops 203743674368 | tf_op jit(solution)/shard_map/nt_product/pallas_call | solution.py:56
  461.3 13.2 %grad_product.9 = (bf16[512,2048]{1,0:T(8,128)(2,1)}, bf16[512,2048]{1,0:T(8,128)(2,1)}) custom-call(bf16[1024,1024]{1,0:T(8,128)(2,1)} %get-tuple-element.107.refs_5_.refs_4_.refs_8_.refs_0_, bf16[1024,1024]{1,0:T(8,128)(2,1)} %collective-permute-done.15.refs_5_.refs_9_.refs_1_, bf16[1024,2048]{1,0:T(8,128)(2,1)} %get-tuple-element.118.refs_1_.refs_2_, ...), custom_call_target="tpu_custom_call" | custom-call | flops 131256000512 | tf_op jit(solution)/shard_map/grad_product/pallas_call | solution.py:56
  475.2 7.5 norm_back.4
  488.3 11.4 %nt_product.8.refs_11_.refs_1_ = bf16[512,2048]{1,0:T(8,128)(2,1)} custom-call(bf16[1024,1024]{1,0:T(8,128)(2,1)} %get-tuple-element.108.refs_2_.refs_0_, bf16[1024,2048]{1,0:T(8,128)(2,1)} %get-tuple-element.117.refs_2_.refs_1_, bf16[2048,6272]{1,0:T(8,128)(2,1)} %all-gather.3.cloned.1.call-done.refs_1_.refs_4_.refs_2_.refs_3_.refs_6_, ...), custom_call_target="tpu_custom_call" | custom-call | flops 109371842560 | tf_op jit(solution)/shard_map/nt_product/pallas_call | solution.py:56
  500.1 25.2 %attend_back.2 = (bf16[1024,1024]{1,0:T(8,128)(2,1)}, bf16[512,1024]{1,0:T(8,128)(2,1)}, bf16[512,1024]{1,0:T(8,128)(2,1)}, bf16[2,512,1024]{2,1,0:T(8,128)(2,1)}, f32[8,128]{1,0:T(8,128)}) custom-call(s32[4,8]{1,0:T(4,128)} %copy-done.7, bf16[1024,1024]{1,0:T(8,128)(2,1)} %get-tuple-element.97.refs_5_.refs_1_, bf16[512,1024]{1,0:T(8,128)(2,1)} %get-tuple-element.94.refs_2_, ...), custom_call_target="tpu_custom_call" | custom-call | flops 249999998976 | tf_op jit(solution)/shard_map/attend_back/pallas_call | solution.py:56
  525.4 7.5 norm_back.5
  548.9 11.7 %nt_product.9.refs_4_.refs_1_ = bf16[512,2048]{1,0:T(8,128)(2,1)} custom-call(bf16[1024,1024]{1,0:T(8,128)(2,1)} %get-tuple-element.108.refs_2_.refs_0_, bf16[1024,2048]{1,0:T(8,128)(2,1)} %get-tuple-element.117.refs_2_.refs_1_, bf16[2048,6272]{1,0:T(8,128)(2,1)} %all-gather.3.cloned.1.call-done.refs_1_.refs_4_.refs_2_.refs_3_.refs_6_, ...), custom_call_target="tpu_custom_call" | custom-call | flops 109371842560 | tf_op jit(solution)/shard_map/nt_product/pallas_call | solution.py:56
  562.5 13.2 %grad_product.10 = (bf16[512,2048]{1,0:T(8,128)(2,1)}, bf16[512,2048]{1,0:T(8,128)(2,1)}) custom-call(bf16[1024,1024]{1,0:T(8,128)(2,1)} %get-tuple-element.107.refs_5_.refs_4_.refs_8_.refs_0_, bf16[1024,1024]{1,0:T(8,128)(2,1)} %collective-permute-done.15.refs_5_.refs_9_.refs_1_, bf16[1024,2048]{1,0:T(8,128)(2,1)} %get-tuple-element.119.refs_3_.refs_2_, ...), custom_call_target="tpu_custom_call" | custom-call | flops 131256000512 | tf_op jit(solution)/shard_map/grad_product/pallas_call | solution.py:56
  576.7 24.6 %attend_back.3 = (bf16[1024,1024]{1,0:T(8,128)(2,1)}, bf16[512,1024]{1,0:T(8,128)(2,1)}, bf16[512,1024]{1,0:T(8,128)(2,1)}, bf16[2,512,1024]{2,1,0:T(8,128)(2,1)}, f32[8,128]{1,0:T(8,128)}) custom-call(s32[4,8]{1,0:T(4,128)} %copy-done.7, bf16[1024,1024]{1,0:T(8,128)(2,1)} %get-tuple-element.97.refs_5_.refs_1_, ...), custom_call_target="tpu_custom_call", output_to_operand_aliasing={{0}: (11, {})} | custom-call | flops 249999998976 | tf_op jit(solution)/shard_map/attend_back/pallas_call | solution.py:56
  617.8 9.0 %nt_product.10.refs_2_.refs_1_ = bf16[512,2048]{1,0:T(8,128)(2,1)} custom-call(bf16[1024,1024]{1,0:T(8,128)(2,1)} %get-tuple-element.140.refs_0_.refs_2_, bf16[1024,1024]{1,0:T(8,128)(2,1)} %get-tuple-element.138.refs_2_.refs_1_.refs_7_, bf16[2048,6272]{1,0:T(8,128)(2,1)} %all-gather.3.cloned.1.call-done.refs_1_.refs_4_.refs_2_.refs_3_.refs_6_, ...), custom_call_target="tpu_custom_call" | custom-call | flops 77914562560 | tf_op jit(solution)/shard_map/nt_product/pallas_call | solution.py:56
  630.3 8.4 %grad_product.11 = (bf16[512,1024]{1,0:T(8,128)(2,1)}, bf16[512,1024]{1,0:T(8,128)(2,1)}) custom-call(bf16[1024,1024]{1,0:T(8,128)(2,1)} %get-tuple-element.99.refs_0_, bf16[1024,1024]{1,0:T(8,128)(2,1)} %collective-permute-done.13.refs_7_.refs_1_, bf16[1024,1024]{1,0:T(8,128)(2,1)} %get-tuple-element.140.refs_0_.refs_2_, ...), custom_call_target="tpu_custom_call" | custom-call | flops 83128000512 | tf_op jit(solution)/shard_map/grad_product/pallas_call | solution.py:56
  655.3 9.0 %nt_product.11.refs_4_.refs_1_.refs_2_ = bf16[512,2048]{1,0:T(8,128)(2,1)} custom-call(bf16[1024,1024]{1,0:T(8,128)(2,1)} %get-tuple-element.140.refs_0_.refs_2_, bf16[1024,1024]{1,0:T(8,128)(2,1)} %get-tuple-element.144.refs_4_.refs_1_.refs_2_, bf16[2048,6272]{1,0:T(8,128)(2,1)} %all-gather.3.cloned.1.call-done.refs_1_.refs_4_.refs_2_.refs_3_.refs_6_, ...), custom_call_target="tpu_custom_call" | custom-call | flops 77914562560 | tf_op jit(solution)/shard_map/nt_product/pallas_call | solution.py:56
  667.2 8.4 %grad_product.12 = (bf16[512,1024]{1,0:T(8,128)(2,1)}, bf16[512,1024]{1,0:T(8,128)(2,1)}) custom-call(bf16[1024,1024]{1,0:T(8,128)(2,1)} %get-tuple-element.99.refs_0_, bf16[1024,1024]{1,0:T(8,128)(2,1)} %collective-permute-done.13.refs_7_.refs_1_, bf16[1024,1024]{1,0:T(8,128)(2,1)} %get-tuple-element.144.refs_4_.refs_1_.refs_2_, ...), custom_call_target="tpu_custom_call" | custom-call | flops 83128000512 | tf_op jit(solution)/shard_map/grad_product/pallas_call | solution.py:56
  678.2 8.6 %grad_product.13 = (bf16[512,1024]{1,0:T(8,128)(2,1)}, bf16[512,1024]{1,0:T(8,128)(2,1)}) custom-call(bf16[1024,1024]{1,0:T(8,128)(2,1)} %get-tuple-element.143.refs_8_.refs_0_, bf16[1024,1024]{1,0:T(8,128)(2,1)} %copy-done.19, bf16[512,1024]{1,0:T(8,128)(2,1)} %attend.2.refs_6_.refs_2_, bf16[512,1024]{1,0:T(8,128)(2,1)} %attend.3.refs_2_.refs_3_, ...), custom_call_target="tpu_custom_call" | custom-call | flops 83128000512 | tf_op jit(solution)/shard_map/grad_product/pallas_call | solution.py:56
  694.8 7.5 norm_back.6
  702.3 17.1 %collective-permute-done.34.refs_3_ = bf16[512,2048]{1,0:T(8,128)(2,1)} collective-permute-done((bf16[512,2048]{1,0:T(8,128)(2,1)}, bf16[512,2048]{1,0:T(8,128)(2,1)}, u32[]{:S(2)}, u32[]{:S(2)}) %collective-permute-start.34) | collective-permute-done | bytes 2097184 | tf_op jit(solution)/shard_map/one1_over_tp/ppermute | solution.py:820
  726.8 8.2 %collective-permute-done.40.refs_5_ = bf16[512,1024]{1,0:T(8,128)(2,1)} collective-permute-done((bf16[512,1024]{1,0:T(8,128)(2,1)}, bf16[512,1024]{1,0:T(8,128)(2,1)}, u32[]{:S(2)}, u32[]{:S(2)}) %collective-permute-start.40) | collective-permute-done | bytes 1048608 | tf_op jit(solution)/shard_map/output_over_x/ppermute | solution.py:820
  744.2 44.3 %psum.7 = f32[4352]{0:T(1024)S(1)} all-reduce(f32[4352]{0:T(1024)S(1)} %pad_maximum_fusion.4), channel_id=1, replica_groups=mesh['dp'=4,'ctx'=4,'tp'=2] {'dp','ctx','tp'}, use_global_device_ids=true, to_apply=%region_10.11 | all-reduce | flops 4352 | bytes 34816 | tf_op jit(solution)/shard_map/psum | solution.py:1062
  791.9 8.9 %reduce-scatter.9.cloned.1.call-done = bf16[128,3072]{1,0:T(8,128)(2,1)} async-done(((bf16[512,3072]{1,0:T(8,128)(2,1)}), bf16[128,3072]{1,0:T(8,128)(2,1)}) %reduce-scatter.9.cloned.1.call-update) | async-done | bytes 786448 | tf_op jit(solution)/shard_map/query_key_output_over_dp/reduce_scatter | solution.py:943
  (232 shorter events, 212.3 us)
Async XLA Ops:
  7.2 138.7 %all-gather.3.cloned.1.call-start = ((), (), s32[]{:S(2)}) async-start(), calls=%async_computation.4 | async-start | bytes 27295744 | tf_op jit(solution)/shard_map/all_gather | solution.py:837
  12.0 352.0 %all-gather.5.cloned.1.call-start = ((), (), s32[]{:S(2)}) async-start(), calls=%async_computation.5 | async-start | bytes 26738688 | tf_op jit(solution)/shard_map/all_gather | solution.py:903
  161.2 29.5 %collective-permute-start.2 = (bf16[512,1024]{1,0:T(8,128)(2,1)}, bf16[512,1024]{1,0:T(8,128)(2,1)}, u32[]{:S(2)}, u32[]{:S(2)}) collective-permute-start(bf16[512,1024]{1,0:T(8,128)(2,1)} %get-tuple-element.94.refs_2_), channel_id=1, source_target_pairs={{0,4},{4,0},{2,6},{6,2},{1,5},{5,1},{3,7},{7,3},{8,12},{12,8},{10,... | collective-permute-start | bytes 3145736 | tf_op jit(solution)/shard_map/kv0_over_x/ppermute | solution.py:820
  165.4 47.8 %collective-permute-start.7 = (bf16[1024,1024]{1,0:T(8,128)(2,1)}, bf16[1024,1024]{1,0:T(8,128)(2,1)}, u32[]{:S(2)}, u32[]{:S(2)}) collective-permute-start(bf16[1024,1024]{1,0:T(8,128)(2,1)} %constant_dynamic-slice_fusion.refs_5_), channel_id=1, source_target_pairs={{0,1},{1,0},{2,3},{3,2},{4,5},{5,4},{6,7},{7,6},{8,9},{9,8},{10,11... | collective-permute-start | bytes 6291464 | tf_op jit(solution)/shard_map/output_proj_over_tp/ppermute | solution.py:820
  190.7 24.8 %collective-permute-start.3 = (bf16[512,1024]{1,0:T(8,128)(2,1)S(1)}, bf16[512,1024]{1,0:T(8,128)(2,1)S(1)}, u32[]{:S(2)}, u32[]{:S(2)}) collective-permute-start(bf16[512,1024]{1,0:T(8,128)(2,1)S(1)} %copy-done.23), channel_id=1, source_target_pairs={{0,4},{4,0},{2,6},{6,2},{1,5},{5,1},{3,7},{7,3},{8,12},{12,8},{10,... | collective-permute-start | bytes 3145736 | tf_op jit(solution)/shard_map/kv1_over_x/ppermute | solution.py:820
  216.6 83.5 %collective-permute-start.13 = (bf16[1024,1024]{1,0:T(8,128)(2,1)}, bf16[1024,1024]{1,0:T(8,128)(2,1)}, u32[]{:S(2)}, u32[]{:S(2)}) collective-permute-start(bf16[1024,1024]{1,0:T(8,128)(2,1)} %get-tuple-element.106), channel_id=1, source_target_pairs={{0,2},{2,0},{4,6},{6,4},{1,3},{3,1},{5,7},{7,5},{8,10},{10,8},{12,... | collective-permute-start | bytes 6291464 | tf_op jit(solution)/shard_map/normed_one_over_core/ppermute | solution.py:820
  224.8 318.7 %reduce-scatter.5.cloned.1.call-start = ((), (), s32[]{:S(2)}) async-start(), calls=%async_computation.6 | async-start | bytes 3932160 | tf_op jit(solution)/shard_map/first_third_over_dp/reduce_scatter | solution.py:943
  237.8 26.2 %collective-permute-start.10 = (bf16[512,1024]{1,0:T(8,128)(2,1)}, bf16[512,1024]{1,0:T(8,128)(2,1)S(1)}, u32[]{:S(2)}, u32[]{:S(2)}) collective-permute-start(bf16[512,1024]{1,0:T(8,128)(2,1)} %attend.2.refs_6_.refs_2_), channel_id=1, source_target_pairs={{0,1},{1,0},{2,3},{3,2},{4,5},{5,4},{6,7},{7,6},{8,9},{9,8},{10,11... | collective-permute-start | bytes 3145736 | tf_op jit(solution)/shard_map/attended0_over_tp/ppermute | solution.py:820
  250.3 49.8 %collective-permute-start.12 = (bf16[512,1024]{1,0:T(8,128)(2,1)}, bf16[512,1024]{1,0:T(8,128)(2,1)}, u32[]{:S(2)}, u32[]{:S(2)}) collective-permute-start(bf16[512,1024]{1,0:T(8,128)(2,1)} %attend.3.refs_2_.refs_3_), channel_id=1, source_target_pairs={{0,2},{2,0},{4,6},{6,4},{1,3},{3,1},{5,7},{7,5},{8,10},{10,8},{12,... | collective-permute-start | bytes 3145736 | tf_op jit(solution)/shard_map/attended_over_core/ppermute | solution.py:820
  250.3 35.5 %collective-permute-start.9 = (bf16[512,1024]{1,0:T(8,128)(2,1)}, bf16[512,1024]{1,0:T(8,128)(2,1)}, u32[]{:S(2)}, u32[]{:S(2)}) collective-permute-start(bf16[512,1024]{1,0:T(8,128)(2,1)} %attend.3.refs_2_.refs_3_), channel_id=1, source_target_pairs={{0,1},{1,0},{2,3},{3,2},{4,5},{5,4},{6,7},{7,6},{8,9},{9,8},{10,11... | collective-permute-start | bytes 3145736 | tf_op jit(solution)/shard_map/attended1_over_tp/ppermute | solution.py:820
  251.8 48.3 %collective-permute-start.11 = (bf16[512,1024]{1,0:T(8,128)(2,1)}, bf16[512,1024]{1,0:T(8,128)(2,1)}, u32[]{:S(2)}, u32[]{:S(2)}) collective-permute-start(bf16[512,1024]{1,0:T(8,128)(2,1)} %attend.2.refs_6_.refs_2_), channel_id=1, source_target_pairs={{0,2},{2,0},{4,6},{6,4},{1,3},{3,1},{5,7},{7,5},{8,10},{10,8},{12,... | collective-permute-start | bytes 3145736 | tf_op jit(solution)/shard_map/attended_over_core/ppermute | solution.py:820
  363.2 93.7 %collective-permute-start.21 = (bf16[512,3072]{1,0:T(8,128)(2,1)}, bf16[512,3072]{1,0:T(8,128)(2,1)}, u32[]{:S(2)}, u32[]{:S(2)}) collective-permute-start(bf16[512,3072]{1,0:T(8,128)(2,1)} %get-tuple-element.122), channel_id=1, source_target_pairs={{0,4},{4,0},{2,6},{6,2},{1,5},{5,1},{3,7},{7,3},{8,12},{12,8},{10,... | collective-permute-start | bytes 9437192 | tf_op jit(solution)/shard_map/first_third_over_x/ppermute | solution.py:820
  399.4 35.4 %collective-permute-start.20 = (bf16[1024,2048]{1,0:T(8,128)(2,1)}, bf16[1024,2048]{1,0:T(8,128)(2,1)}, u32[]{:S(2)}, u32[]{:S(2)}) collective-permute-start(bf16[1024,2048]{1,0:T(8,128)(2,1)} %get-tuple-element.118.refs_1_.refs_2_), channel_id=1, source_target_pairs={{0,2},{2,0},{4,6},{6,4},{1,3},{3,1},{5,7},{7,5},{8,10},{10,8},{12,... | collective-permute-start | bytes 12582920 | tf_op jit(solution)/shard_map/gate_back_two_over_core/ppermute | solution.py:820
  399.9 34.9 %collective-permute-start.22 = (bf16[1024,2048]{1,0:T(8,128)(2,1)}, bf16[1024,2048]{1,0:T(8,128)(2,1)}, u32[]{:S(2)}, u32[]{:S(2)}) collective-permute-start(bf16[1024,2048]{1,0:T(8,128)(2,1)} %get-tuple-element.119.refs_3_.refs_2_), channel_id=1, source_target_pairs={{0,2},{2,0},{4,6},{6,4},{1,3},{3,1},{5,7},{7,5},{8,10},{10,8},{12,... | collective-permute-start | bytes 12582920 | tf_op jit(solution)/shard_map/up_back_two_over_core/ppermute | solution.py:820
  420.1 55.1 %collective-permute-start.24 = (bf16[512,2048]{1,0:T(8,128)(2,1)}, bf16[512,2048]{1,0:T(8,128)(2,1)}, u32[]{:S(2)}, u32[]{:S(2)}) collective-permute-start(bf16[512,2048]{1,0:T(8,128)(2,1)} %nt_product.6.refs_4_.refs_2_), channel_id=1, source_target_pairs={{0,1},{1,0},{2,3},{3,2},{4,5},{5,4},{6,7},{7,6},{8,9},{9,8},{10,11... | collective-permute-start | bytes 6291464 | tf_op jit(solution)/shard_map/back0_over_tp/ppermute | solution.py:820
  433.7 109.8 %collective-permute-start.19 = (bf16[512,2048]{1,0:T(8,128)(2,1)}, bf16[512,2048]{1,0:T(8,128)(2,1)}, u32[]{:S(2)}, u32[]{:S(2)}) collective-permute-start(bf16[512,2048]{1,0:T(8,128)(2,1)} %get-tuple-element.121), channel_id=1, source_target_pairs={{0,4},{4,0},{2,6},{6,2},{1,5},{5,1},{3,7},{7,3},{8,12},{12,8},{10,... | collective-permute-start | bytes 6291464 | tf_op jit(solution)/shard_map/down_two_over_x/ppermute | solution.py:820
  454.8 70.5 %collective-permute-start.26 = (bf16[512,2048]{1,0:T(8,128)(2,1)}, bf16[512,2048]{1,0:T(8,128)(2,1)}, u32[]{:S(2)}, u32[]{:S(2)}) collective-permute-start(bf16[512,2048]{1,0:T(8,128)(2,1)} %nt_product.7.refs_2_), channel_id=1, source_target_pairs={{0,1},{1,0},{2,3},{3,2},{4,5},{5,4},{6,7},{7,6},{8,9},{9,8},{10,11... | collective-permute-start | bytes 6291464 | tf_op jit(solution)/shard_map/back1_over_tp/ppermute | solution.py:820
  461.2 165.6 %reduce-scatter.7.cloned.1.call-start = ((), (), s32[]{:S(2)}) async-start(), calls=%async_computation.7 | async-start | bytes 5242880 | tf_op jit(solution)/shard_map/down_gate_two_over_dp/reduce_scatter | solution.py:943
  474.5 69.0 %collective-permute-start.23 = (bf16[512,2048]{1,0:T(8,128)(2,1)}, bf16[512,2048]{1,0:T(8,128)(2,1)}, u32[]{:S(2)}, u32[]{:S(2)}) collective-permute-start(bf16[512,2048]{1,0:T(8,128)(2,1)} %get-tuple-element.124), channel_id=1, source_target_pairs={{0,4},{4,0},{2,6},{6,2},{1,5},{5,1},{3,7},{7,3},{8,12},{12,8},{10,... | collective-permute-start | bytes 6291464 | tf_op jit(solution)/shard_map/gate_two_over_x/ppermute | solution.py:820
  499.7 77.0 %collective-permute-start.28 = (bf16[512,2048]{1,0:T(8,128)(2,1)}, bf16[512,2048]{1,0:T(8,128)(2,1)}, u32[]{:S(2)}, u32[]{:S(2)}) collective-permute-start(bf16[512,2048]{1,0:T(8,128)(2,1)} %nt_product.8.refs_11_.refs_1_), channel_id=1, source_target_pairs={{0,1},{1,0},{2,3},{3,2},{4,5},{5,4},{6,7},{7,6},{8,9},{9,8},{10,11... | collective-permute-start | bytes 6291464 | tf_op jit(solution)/shard_map/out0_over_tp/ppermute | solution.py:820
  542.4 34.3 %collective-permute-start.29 = (bf16[512,1024]{1,0:T(8,128)(2,1)}, bf16[512,1024]{1,0:T(8,128)(2,1)}, u32[]{:S(2)}, u32[]{:S(2)}) collective-permute-start(bf16[512,1024]{1,0:T(8,128)(2,1)} %add_rows.7.refs_4_), channel_id=1, source_target_pairs={{0,4},{4,0},{2,6},{6,2},{1,5},{5,1},{3,7},{7,3},{8,12},{12,8},{10,... | collective-permute-start | bytes 3145736 | tf_op jit(solution)/shard_map/kv_grad0_over_x/ppermute | solution.py:820
  548.8 240.8 %reduce-scatter.11.cloned.1.call-start = ((), (), s32[]{:S(2)}) async-start(), calls=%async_computation.9 | async-start | bytes 2621440 | tf_op jit(solution)/shard_map/up_two_over_dp/reduce_scatter | solution.py:943
  560.6 69.7 %collective-permute-start.27 = (bf16[512,2048]{1,0:T(8,128)(2,1)}, bf16[512,2048]{1,0:T(8,128)(2,1)}, u32[]{:S(2)}, u32[]{:S(2)}) collective-permute-start(bf16[512,2048]{1,0:T(8,128)(2,1)} %nt_product.9.refs_4_.refs_1_), channel_id=1, source_target_pairs={{0,1},{1,0},{2,3},{3,2},{4,5},{5,4},{6,7},{7,6},{8,9},{9,8},{10,11... | collective-permute-start | bytes 6291464 | tf_op jit(solution)/shard_map/out1_over_tp/ppermute | solution.py:820
  575.7 51.0 %collective-permute-start.33 = (bf16[512,2048]{1,0:T(8,128)(2,1)}, bf16[512,2048]{1,0:T(8,128)(2,1)}, u32[]{:S(2)}, u32[]{:S(2)}) collective-permute-start(bf16[512,2048]{1,0:T(8,128)(2,1)} %get-tuple-element.141), channel_id=1, source_target_pairs={{0,4},{4,0},{2,6},{6,2},{1,5},{5,1},{3,7},{7,3},{8,12},{12,8},{10,... | collective-permute-start | bytes 6291464 | tf_op jit(solution)/shard_map/up_two_over_x/ppermute | solution.py:820
  601.4 28.9 %collective-permute-start.32 = (bf16[1024,1024]{1,0:T(8,128)(2,1)}, bf16[1024,1024]{1,0:T(8,128)(2,1)}, u32[]{:S(2)}, u32[]{:S(2)}) collective-permute-start(bf16[1024,1024]{1,0:T(8,128)(2,1)} %get-tuple-element.140.refs_0_.refs_2_), channel_id=1, source_target_pairs={{0,2},{2,0},{4,6},{6,4},{1,3},{3,1},{5,7},{7,5},{8,10},{10,8},{12,... | collective-permute-start | bytes 6291464 | tf_op jit(solution)/shard_map/query_back_over_core/ppermute | solution.py:820
  611.8 34.2 %collective-permute-start.31 = (bf16[512,1024]{1,0:T(8,128)(2,1)}, bf16[512,1024]{1,0:T(8,128)(2,1)}, u32[]{:S(2)}, u32[]{:S(2)}) collective-permute-start(bf16[512,1024]{1,0:T(8,128)(2,1)} %add_rows.9.refs_3_), channel_id=1, source_target_pairs={{0,4},{4,0},{2,6},{6,2},{1,5},{5,1},{3,7},{7,3},{8,12},{12,8},{10,... | collective-permute-start | bytes 3145736 | tf_op jit(solution)/shard_map/kv_grad1_over_x/ppermute | solution.py:820
  626.8 68.0 %collective-permute-start.35 = (bf16[512,2048]{1,0:T(8,128)(2,1)}, bf16[512,2048]{1,0:T(8,128)(2,1)}, u32[]{:S(2)}, u32[]{:S(2)}) collective-permute-start(bf16[512,2048]{1,0:T(8,128)(2,1)} %nt_product.10.refs_2_.refs_1_), channel_id=1, source_target_pairs={{0,1},{1,0},{2,3},{3,2},{4,5},{5,4},{6,7},{7,6},{8,9},{9,8},{10,11... | collective-permute-start | bytes 6291464 | tf_op jit(solution)/shard_map/one0_over_tp/ppermute | solution.py:820
  630.2 170.6 %reduce-scatter.9.cloned.1.call-start = ((), (), s32[]{:S(2)}) async-start(), calls=%async_computation.8 | async-start | bytes 3932160 | tf_op jit(solution)/shard_map/query_key_output_over_dp/reduce_scatter | solution.py:943
  664.3 62.4 %collective-permute-start.38 = (bf16[512,1024]{1,0:T(8,128)(2,1)}, bf16[512,1024]{1,0:T(8,128)(2,1)}, u32[]{:S(2)}, u32[]{:S(2)}) collective-permute-start(bf16[512,1024]{1,0:T(8,128)(2,1)} %get-tuple-element.157), channel_id=1, source_target_pairs={{0,4},{4,0},{2,6},{6,2},{1,5},{5,1},{3,7},{7,3},{8,12},{12,8},{10,... | collective-permute-start | bytes 3145736 | tf_op jit(solution)/shard_map/query_over_x/ppermute | solution.py:820
  665.2 54.2 %collective-permute-start.34 = (bf16[512,2048]{1,0:T(8,128)(2,1)}, bf16[512,2048]{1,0:T(8,128)(2,1)}, u32[]{:S(2)}, u32[]{:S(2)}) collective-permute-start(bf16[512,2048]{1,0:T(8,128)(2,1)} %nt_product.11.refs_4_.refs_1_.refs_2_), channel_id=1, source_target_pairs={{0,1},{1,0},{2,3},{3,2},{4,5},{5,4},{6,7},{7,6},{8,9},{9,8},{10,11... | collective-permute-start | bytes 6291464 | tf_op jit(solution)/shard_map/one1_over_tp/ppermute | solution.py:820
  675.6 51.1 %collective-permute-start.39 = (bf16[512,1024]{1,0:T(8,128)(2,1)}, bf16[512,1024]{1,0:T(8,128)(2,1)}, u32[]{:S(2)}, u32[]{:S(2)}) collective-permute-start(bf16[512,1024]{1,0:T(8,128)(2,1)} %get-tuple-element.158), channel_id=1, source_target_pairs={{0,4},{4,0},{2,6},{6,2},{1,5},{5,1},{3,7},{7,3},{8,12},{12,8},{10,... | collective-permute-start | bytes 3145736 | tf_op jit(solution)/shard_map/key_over_x/ppermute | solution.py:820
  690.5 44.5 %collective-permute-start.40 = (bf16[512,1024]{1,0:T(8,128)(2,1)}, bf16[512,1024]{1,0:T(8,128)(2,1)}, u32[]{:S(2)}, u32[]{:S(2)}) collective-permute-start(bf16[512,1024]{1,0:T(8,128)(2,1)} %get-tuple-element.159), channel_id=1, source_target_pairs={{0,4},{4,0},{2,6},{6,2},{1,5},{5,1},{3,7},{7,3},{8,12},{12,8},{10,... | collective-permute-start | bytes 3145736 | tf_op jit(solution)/shard_map/output_over_x/ppermute | solution.py:820
  (44 other events, 406.0 us)
Sparse Core Ops, SparseCore 0:
  12.1 133.7 all-gather.2
  225.0 127.9 all-gather.4
  461.4 59.6 reduce-scatter.4
  548.9 77.5 reduce-scatter.6
  630.3 44.8 reduce-scatter.10
  739.5 61.3 reduce-scatter.8

commit v3 on v2

--- a/solution.py
+++ b/solution.py
@@ -221,18 +221,22 @@
     return exponents, 1.0 / total
 
 
-def attend_kernel(orders_ref, q_ref, own_ref, core_ref, x_ref, diag_ref, out_ref, *, first, span):
+def attend_kernel(orders_ref, q_ref, own_ref, core_ref, x_ref, diag_ref, out_ref, prob_ref, *, first, span):
     seq = pl.program_id(0) + first
     local = q_ref.shape[0]
     for group in range(q_ref.shape[1] // GROUP):
         columns = slice(group * GROUP, (group + 1) * GROUP)
+        rows = slice(group * 2 * local, (group + 1) * 2 * local)
         query = stacked_heads(q_ref[:, columns])
         pieces = [ref[:, columns] for ref in (own_ref, core_ref, x_ref, diag_ref)]
         exponents, inverse = masked_exponents(orders_ref, seq, query, pieces, span)
-        total = functools.reduce(
-            jnp.add, [nn(e.astype(BF16), p[:, HEAD_DIM:GROUP]) for e, p in zip(exponents, pieces)]
-        )
-        result = (total * inverse).astype(BF16)
+        total = None
+        for at, (exponent, piece) in enumerate(zip(exponents, pieces)):
+            prob = (exponent * inverse).astype(BF16)
+            prob_ref[0, rows, at * local : (at + 1) * local] = prob
+            product = nn(prob, piece[:, HEAD_DIM:GROUP])
+            total = product if total is None else total + product
+        result = total.astype(BF16)
         for head in range(2):
             start = group * GROUP + head * HEAD_DIM
             out_ref[:, start : start + HEAD_DIM] = result[head * local : (head + 1) * local]
@@ -244,16 +248,20 @@
     at_whole = lambda s, o: (s + first, 0)
     at_half = lambda s, o: (s, 0)
     ins = [(q, block, at_whole), (kv, block, at_half)] + [(k, block, at_half) for k in others]
+    prob = (1, columns // GROUP * 2 * local, 4 * local)
     return call(
         functools.partial(attend_kernel, first=first, span=local // 2),
         (count,),
         ins,
-        [((count * local, columns), BF16, block, at_half)],
+        [
+            ((count * local, columns), BF16, block, at_half),
+            ((count,) + prob[1:], BF16, prob, lambda s, o: (s, 0, 0)),
+        ],
         scalars=(orders,),
         after=after,
         name="attend",
         cost=11,
-    )[0]
+    )
 
 
 def turn_back(grad, raw, cosine, sine, gain):
@@ -274,34 +282,30 @@
 
 
 def attend_back_kernel(
-    orders_ref, q_ref, own_ref, core_ref, x_ref, diag_ref, grad_ref, raw_ref, cos_ref, sin_ref, gain_ref,
-    *rest, first, span
+    q_ref, own_ref, core_ref, x_ref, diag_ref, prob_ref, grad_ref, raw_ref, cos_ref, sin_ref, gain_ref, *rest
 ):
     q_back_ref, own_out, x_out, core_out, gain_out = rest[-5:]
     clear_at_start(gain_out, 1)
-    seq = pl.program_id(0) + first
     scale = HEAD_DIM**-0.5
     local = q_ref.shape[0]
+    outs = (own_out, core_out.at[0], x_out, core_out.at[1])
     for group in range(q_ref.shape[1] // GROUP):
         start = group * GROUP
         both = slice(start, start + GROUP)
+        rows = slice(group * 2 * local, (group + 1) * 2 * local)
         query = stacked_heads(q_ref[:, both])
         grad = stacked_heads(grad_ref[:, both])
         pieces = [ref[:, both] for ref in (own_ref, core_ref, x_ref, diag_ref)]
-        exponents, inverse = masked_exponents(orders_ref, seq, query, pieces, span)
-        probability = [e * inverse for e in exponents]
-        grad_prob = [nt(grad, p[:, HEAD_DIM:GROUP]) for p in pieces]
-        delta = functools.reduce(
-            jnp.add, [jnp.sum(p * g, axis=1, keepdims=True) for p, g in zip(probability, grad_prob)]
-        )
-        grad_scores = [(p * (g - delta)).astype(BF16) for p, g in zip(probability, grad_prob)]
+        lows = [prob_ref[0, rows, at * local : (at + 1) * local] for at in range(4)]
+        products = [low.astype(F32) * nt(grad, p[:, HEAD_DIM:GROUP]) for low, p in zip(lows, pieces)]
+        delta = functools.reduce(jnp.add, [jnp.sum(p, axis=1, keepdims=True) for p in products])
+        grad_scores = [(p - low.astype(F32) * delta).astype(BF16) for p, low in zip(products, lows)]
         grad_query = functools.reduce(
             jnp.add, [nn(s, p[:, 0:HEAD_DIM]) for s, p in zip(grad_scores, pieces)]
         )
-        outs = (own_out, core_out.at[0], x_out, core_out.at[1])
-        for out, scores, prob in zip(outs, grad_scores, probability):
+        for out, scores, low in zip(outs, grad_scores, lows):
             out[:, start : start + HEAD_DIM] = (tn(scores, query) * scale).astype(BF16)
-            out[:, start + HEAD_DIM : start + GROUP] = tn(prob.astype(BF16), grad).astype(BF16)
+            out[:, start + HEAD_DIM : start + GROUP] = tn(low, grad).astype(BF16)
         for head in range(2):
             columns = slice(start + head * HEAD_DIM, start + (head + 1) * HEAD_DIM)
             result, terms = turn_back(
@@ -315,13 +319,14 @@
             gain_out[...] += terms
 
 
-def attend_back(orders, q, kv, others, grad, raw, cosine, sine, gain, first, count, local, into, after=()):
+def attend_back(q, kv, others, prob, grad, raw, cosine, sine, gain, first, count, local, into, after=()):
     columns = q.shape[1]
     block = (local, columns)
-    at_whole = lambda s, o: (s + first, 0)
-    at_half = lambda s, o: (s, 0)
-    fixed = lambda s, o: (0, 0)
+    at_whole = lambda s: (s + first, 0)
+    at_half = lambda s: (s, 0)
+    fixed = lambda s: (0, 0)
     ins = [(q, block, at_whole), (kv, block, at_half)] + [(k, block, at_half) for k in others]
+    ins += [(prob, (1,) + prob.shape[1:], lambda s: (s, 0, 0))]
     ins += [(grad, block, at_half), (raw, block, at_whole)]
     ins += [(cosine, (local, HEAD_DIM), at_whole), (sine, (local, HEAD_DIM), at_whole)]
     ins += [(gain, (1, HEAD_DIM), fixed)]
@@ -329,14 +334,13 @@
         ins.append((into, None, None))
     piece = ((count * local, columns), BF16, block, at_half)
     return call(
-        functools.partial(attend_back_kernel, first=first, span=local // 2),
+        attend_back_kernel,
         (count,),
         ins,
         [(q.shape, BF16, block, at_whole)]
         + [piece] * 2
-        + [((2, count * local, columns), BF16, (2, local, columns), lambda s, o: (0, s, 0))]
+        + [((2, count * local, columns), BF16, (2, local, columns), lambda s: (0, s, 0))]
         + [((8, HEAD_DIM), F32, (8, HEAD_DIM), fixed)],
-        scalars=(orders,),
         alias=None if into is None else {0: len(ins) - 1},
         after=after,
         name="attend_back",
@@ -890,29 +894,29 @@
             output_same = tp_swap(sent, "output_proj")
             latest = (sent,)
     across = [x_swap(kv[0], "kv0")]
+    beside = [core_swap(kv[0], "kv0")]
+    one_turned = turned(feed_one, "normed_one", after=(kv[1],))
+    across.append(x_swap(behind(kv[1], across[0], one_turned[0]), "kv1"))
+    beside.append(core_swap(kv[1], "kv1"))
+    others = [(beside[0], across[0], core_swap(across[0], "kv0_across"))]
     q, raw_q = project(
-        feed_one, weights, cosine, sine, gain_query, groups, 0, 2, 0, tokens, after=(kv[1],)
-    )
-    one_turned = turned(feed_one, "normed_one", after=(q,))
-    across.append(x_swap(behind(kv[1], across[0], one_turned[0]), "kv1"))
-    others = [
-        (core_swap(kv[h], f"kv{h}"), across[h], core_swap(across[h], f"kv{h}_across"))
-        for h in range(2)
-    ]
-    shard_two = behind(shard_two, across[1], *others[0])
+        feed_one, weights, cosine, sine, gain_query, groups, 0, 2, 0, tokens,
+        after=(one_turned[0], beside[0], across[0], beside[1]),
+    )
+    found = [attend(orders, q, kv[0], others[0], 0, half_seqs, local)]
+    attended = [found[0][0]]
+    arrived = behind(across[1], attended[0])
+    shard_two = behind(shard_two, arrived)
+    others.append((beside[1], arrived, core_swap(arrived, "kv1_across")))
     weights_two = lax.all_gather(shard_two, ("dp", "ctx"), axis=0, tiled=True)
 
-    settled = ()
+    settled = (attended[0],)
     if pair:
-        output_swapped = core_swap(behind(output_same, across[1]), "output_proj")
-        settled = (output_swapped,)
-    attended, joined = [], None
-    for h in range(2):
-        attended.append(
-            attend(
-                orders, q, kv[h], others[h], h * half_seqs, half_seqs, local, after=tuple(attended) or settled
-            )
-        )
+        output_swapped = core_swap(behind(output_same, arrived), "output_proj")
+        settled += (output_swapped,)
+    found.append(attend(orders, q, kv[1], others[1], half_seqs, half_seqs, local, after=settled))
+    attended, probs = [list(parts) for parts in zip(*found)]
+    joined = None
     attended_pair = attended, [core_swap(part, "attended") for part in attended]
     if pair:
         other_heads = [tp_swap(part, f"attended{h}") for h, part in enumerate(attended)]
@@ -991,7 +995,7 @@
 
     def attention_half(h, grad_attended, after):
         found, to_own, to_x, to_core, query = attend_back(
-            orders, q, kv[h], others[h], grad_attended, raw_q, cosine, sine, gain_query,
+            q, kv[h], others[h], probs[h], grad_attended, raw_q, cosine, sine, gain_query,
             h * half_seqs, half_seqs, local, q_back, after=after,
         )
         sums["query"] = sums["query"] + jnp.sum(query, axis=0)
@@ -1022,27 +1026,27 @@
     q_back, *held = attention_half(0, grad_attended, (part,))
     grads, grad_attended = middle_half(1, (held[0],))
     grad_middle, middle_low = grads
-    sent = send_keys(0, held, (grad_attended,))
+    low_turned = turned(middle_low, "grad_middle", after=(grad_attended, gate_two.from_x))
+    sent = send_keys(0, held, (low_turned[0],))
     done, more_out = over_dp("down_gate_two", [down_two, gate_two], after=(sent, first_out))
-    part = out_half(1, (done,))
-    up_two = Gradient("up_two", [(two_turned, seconds[2])], after=(part,))
-    landed = (pieces[0][2], out_started[0][1])
-    q_back, *held = attention_half(1, grad_attended, (up_two.keep, *landed))
+    output_grad = Gradient("output", [(low_turned, attended_pair)], after=(done,))
+    part = out_half(1, (output_grad.keep,))
+    landed = (part, out_started[0][1])
+    up_two = Gradient("up_two", [(two_turned, seconds[2])], after=landed)
+    k_back = key_half(0, (up_two.keep,))
+    part = one_half(0, (output_grad.from_x,))
+    q_back, *held = attention_half(1, grad_attended, (part,))
     q_pair = [q_back], [core_swap(q_back, "query_back")]
-    k_back = key_half(0, (held[0],))
-    sent = send_keys(1, held, (k_back,))
-    outputs = sum_rows(middle, out_started[0], 0, None, after=(sent,))
-    part = one_half(0, (outputs,))
-    done, up_out = over_dp("up_two", [up_two], after=(part, more_out))
-    query_grad = Gradient("query", [(one_turned, q_pair)], after=(done, out_started[1][1]))
-    low_turned = turned(middle_low, "grad_middle", after=(query_grad.keep,))
-    k_back = key_half(1, (low_turned[0],))
-    outputs = sum_rows(middle, out_started[1], half_rows, outputs, after=(k_back,))
-    part = one_half(1, (outputs,))
+    outputs = sum_rows(middle, out_started[0], 0, None, after=(held[0],))
+    sent = send_keys(1, held, (outputs,))
+    outputs = sum_rows(middle, out_started[1], half_rows, outputs, after=(sent,))
+    done, up_out = over_dp("up_two_output", [up_two, output_grad], after=(outputs, more_out))
+    query_grad = Gradient("query", [(one_turned, q_pair)], after=(done,))
+    k_back = key_half(1, (query_grad.keep,))
+    part = one_half(1, ())
     k_pair = [k_back], [core_swap(k_back, "key_back")]
     key_grad = Gradient("key", [(one_turned, k_pair)], after=(part,))
-    output_grad = Gradient("output", [(low_turned, attended_pair)], after=(key_grad.keep,))
-    latest = (output_grad.keep,)
+    latest = (key_grad.keep,)
     for h in range(2):
         part = gain_terms(input_rows, one[h][0], h * half_rows, after=latest)
         latest = (part,)
@@ -1053,8 +1057,7 @@
             input_rows, grad_middle, *one[h], gain_first, h * half_rows, (BF16,), result, after=latest
         )[0:1]
         latest = ()
-    last = [query_grad, key_grad, output_grad]
-    done, heads_out = over_dp("query_key_output", last, after=(result[0],))
+    done, heads_out = over_dp("query_key", [query_grad, key_grad], after=(result[0],))
 
     if not pair:
         sums["first"], sums["second"] = sums["first"] / tp_size, sums["second"] / tp_size
@@ -1062,7 +1065,7 @@
     totals = lax.psum(behind(totals, done), ("dp", "ctx", "tp"))
     cut_total = lambda start, size: lax.dynamic_slice(totals, (start + share * size,), (size,))
 
-    grad_kv = heads_out[:, columns : 2 * columns].astype(F32)
+    grad_kv = heads_out[:, columns:].astype(F32)
     down_out, gate_out, up_first = [first_out[:, at * third : (at + 1) * third] for at in range(3)]
     beside = lambda left, right: jnp.concatenate([left, right], axis=1).astype(F32)
     return (
@@ -1074,10 +1077,10 @@
         split_heads(grad_kv, 1),
         cut_total(2 * width, head_shard),
         cut_total(2 * width + HEAD_DIM, head_shard),
-        heads_out[:, 2 * columns :].astype(F32).T,
+        up_out[:, 2 * third :].astype(F32).T,
         cut_total(width, shard),
         beside(gate_out, more_out[:, 2 * third :]),
-        beside(up_first, up_out),
+        beside(up_first, up_out[:, 0 : 2 * third]),
         beside(down_out, more_out[:, 0 : 2 * third]).T,
     )
 

time: 821 us -> 784 us (0.955)
  waiting for transfers between devices: 213 us -> 182 us
    ppermute x41, waiting for transfers between devices: 88.6 us -> 63.1 us  [swap(): return lax.ppermute(value, axis, pairs)]
    reduce_scatter x4, waiting for transfers between devices: 8.92 us -> 0.01 us  [over_dp(): lax.psum_scatter(summed, 'dp', scatter_dimension=0, tiled=True)]
  transfers between devices with their start and end apart: 47 -> 47, of which waited for: 14 -> 14; matrix products, arithmetic and copies ran while one was open for 2% -> 2% of each run, Pallas kernels for 57% -> 59%
where the time goes in v3:
time: 784 us; the launch traced here: 776 us
  Pallas kernels  474 us (60%)
  waiting for transfers between devices  182 us (23%)
  blocking collectives  42.7 us (5%)
  starting transfers between devices  25.9 us (3%)
  local copies, waits for them, and re-layouts  24.3 us (3%)
  between operations  15 us (2%)
  other arithmetic  12.9 us (2%)
    pallas_call x49, Pallas kernels, call(): pl.pallas_call(body, grid_spec=pltpu.PrefetchScalarGridSpec(num_scalar_pr...  474 us
    all_gather x1, waiting for transfers between devices, shards(): weights = lax.all_gather(shard_one, ('dp', 'ctx'), axis=0, tiled=True)  115 us
    ppermute x41, waiting for transfers between devices, swap(): return lax.ppermute(value, axis, pairs)  63.1 us
    psum x1, blocking collectives, shards(): totals = lax.psum(behind(totals, done), ('dp', 'ctx', 'tp'))  42.7 us
    ppermute x41, starting transfers between devices, swap(): return lax.ppermute(value, axis, pairs)  25.6 us
  transfers between devices with their start and end apart: 47, of which 14 were waited for; matrix products, arithmetic and copies ran while one was open for 2% of the time, Pallas kernels for 59%

profile of v3, /device:TPU:0, one launch (start us, length us, event | category | flops | bytes accessed | tf_op | source)
XLA Modules:
  0.0 776.2 jit_solution(12245947672151595014)
XLA Ops:
  30.8 115.1 %all-gather.3.cloned.1.call-done.refs_1_.refs_4_.refs_2_.refs_3_.refs_6_ = bf16[2048,6272]{1,0:T(8,128)(2,1)} async-done(((bf16[128,6272]{1,0:T(8,128)(2,1)}), bf16[2048,6272]{1,0:T(8,128)(2,1)}) %all-gather.3.cloned.1.call-update) | async-done | bytes 25690128 | tf_op jit(solution)/shard_map/all_gather | solution.py:841
  154.2 6.8 project.3
  188.9 9.9 %project.5 = (bf16[1024,1024]{1,0:T(8,128)(2,1)}, f32[1024,1024]{1,0:T(8,128)}) custom-call(bf16[1024,2048]{1,0:T(8,128)(2,1)} %norm_rows.1.refs_0_.refs_1_.refs_2_.refs_3_.refs_4_, bf16[2048,6272]{1,0:T(8,128)(2,1)} %all-gather.3.cloned.1.call-done.refs_1_.refs_4_.refs_2_.refs_3_.refs_6_, f32[1024,128]{1,0:T(8,128)} %get-tuple-element.97.refs_2_.refs_8_.refs_4_, ...), custom_call_target="tpu_custom_call" | custom-call | flops 99999997952 | tf_op jit(solution)/shard_map/project/pallas_call | solution.py:56
  199.8 13.6 %attend.2 = (bf16[512,1024]{1,0:T(8,128)(2,1)}, bf16[2,2048,1024]{2,1,0:T(8,128)(2,1)}) custom-call(s32[4,8]{1,0:T(4,128)} %copy-done.7, bf16[1024,1024]{1,0:T(8,128)(2,1)} %get-tuple-element.104.refs_1_.refs_0_, bf16[512,1024]{1,0:T(8,128)(2,1)} %get-tuple-element.100.refs_2_.refs_1_, bf16[512,1024]{1,0:T(8,128)(2,1)} %collective-permute-done.1.refs_6_.refs_3_.refs_2_, ...), custom_call_target="tpu_custom_call" | custom-call | flops 109999996928 | tf_op jit(solution)/shard_map/attend/pallas_call | solution.py:56
  223.5 13.5 %attend.3 = (bf16[512,1024]{1,0:T(8,128)(2,1)}, bf16[2,2048,1024]{2,1,0:T(8,128)(2,1)}) custom-call(s32[4,8]{1,0:T(4,128)} %copy-done.7, bf16[1024,1024]{1,0:T(8,128)(2,1)} %get-tuple-element.104.refs_1_.refs_0_, bf16[512,1024]{1,0:T(8,128)(2,1)} %get-tuple-element.105.refs_5_.refs_2_.refs_1_, bf16[512,1024]{1,0:T(8,128)(2,1)} %copy-done.21, ...), custom_call_target="tpu_custom_call" | custom-call | flops 109999996928 | tf_op jit(solution)/shard_map/attend/pallas_call | solution.py:56
  240.4 13.9 %output_join.2 = (f32[1024,2048]{1,0:T(8,128)}, bf16[1024,2048]{1,0:T(8,128)(2,1)}) custom-call(s32[2]{0:T(128)} %pad_add_fusion.1.refs_0_, bf16[1024,2048]{1,0:T(8,128)(2,1)} %bitcast.61, bf16[512,1024]{1,0:T(8,128)(2,1)} %get-tuple-element.106.refs_6_.refs_2_, bf16[512,1024]{1,0:T(8,128)(2,1)} %collective-permute-done.10.refs_3_, ...), custom_call_target="tpu_custom_call" | custom-call | flops 149999992832 | tf_op jit(solution)/shard_map/output_join/pallas_call | solution.py:56
  254.4 8.5 %collective-permute-done.9.refs_3_ = bf16[512,1024]{1,0:T(8,128)(2,1)} collective-permute-done((bf16[512,1024]{1,0:T(8,128)(2,1)}, bf16[512,1024]{1,0:T(8,128)(2,1)}, u32[]{:S(2)}, u32[]{:S(2)}) %collective-permute-start.9) | collective-permute-done | bytes 1048608 | tf_op jit(solution)/shard_map/attended1_over_tp/ppermute | solution.py:824
  262.9 13.7 %output_join.3 = (f32[1024,2048]{1,0:T(8,128)}, bf16[1024,2048]{1,0:T(8,128)(2,1)}) custom-call(s32[2]{0:T(128)} %pad_add_fusion.1.refs_0_, bf16[1024,2048]{1,0:T(8,128)(2,1)} %bitcast.62, bf16[512,1024]{1,0:T(8,128)(2,1)} %get-tuple-element.109.refs_2_.refs_3_, ...), custom_call_target="tpu_custom_call", output_to_operand_aliasing={{0}: (8, {}), {1}: (9, {})} | custom-call | flops 149999992832 | tf_op jit(solution)/shard_map/output_join/pallas_call | solution.py:56
  282.9 21.4 %feed.2 = (bf16[1024,1024]{1,0:T(8,128)(2,1)}, bf16[1024,1024]{1,0:T(8,128)(2,1)}, bf16[1024,1024]{1,0:T(8,128)(2,1)}) custom-call(bf16[1024,2048]{1,0:T(8,128)(2,1)} %get-tuple-element.113.refs_1_.refs_2_.refs_3_.refs_4_.refs_0_, bf16[1024,2048]{1,0:T(8,128)(2,1)} %bitcast.56, ...), custom_call_target="tpu_custom_call" | custom-call | flops 188959997952 | tf_op jit(solution)/shard_map/feed/pallas_call | solution.py:56
  317.3 22.9 %grad_product.7 = (bf16[512,3072]{1,0:T(8,128)(2,1)}, bf16[512,3072]{1,0:T(8,128)(2,1)}) custom-call(bf16[1024,1024]{1,0:T(8,128)(2,1)} %get-tuple-element.119.refs_0_, bf16[1024,1024]{1,0:T(8,128)(2,1)} %copy-done.13, bf16[1024,1024]{1,0:T(8,128)(2,1)} %get-tuple-element.116.refs_2_.refs_0_, bf16[1024,1024]{1,0:T(8,128)(2,1)} %copy-done.18, ...), custom_call_target="tpu_custom_call" | custom-call | flops 179383992320 | tf_op jit(solution)/shard_map/grad_product/pallas_call | solution.py:56
  344.4 35.6 %feed.3 = (bf16[1024,2048]{1,0:T(8,128)(2,1)}, bf16[1024,2048]{1,0:T(8,128)(2,1)}, bf16[1024,2048]{1,0:T(8,128)(2,1)}) custom-call(bf16[1024,2048]{1,0:T(8,128)(2,1)} %get-tuple-element.113.refs_1_.refs_2_.refs_3_.refs_4_.refs_0_, bf16[1024,2048]{1,0:T(8,128)(2,1)} %bitcast.57, ...), custom_call_target="tpu_custom_call" | custom-call | flops 357920014336 | tf_op jit(solution)/shard_map/feed/pallas_call | solution.py:56
  380.7 20.0 %nt_product.6.refs_4_.refs_2_ = bf16[512,2048]{1,0:T(8,128)(2,1)} custom-call(bf16[1024,1024]{1,0:T(8,128)(2,1)} %get-tuple-element.122.refs_6_.refs_0_, bf16[1024,2048]{1,0:T(8,128)(2,1)} %get-tuple-element.126.refs_1_.refs_2_, bf16[1024,1024]{1,0:T(8,128)(2,1)} %get-tuple-element.123.refs_10_.refs_2_, ...), custom_call_target="tpu_custom_call" | custom-call | flops 203743674368 | tf_op jit(solution)/shard_map/nt_product/pallas_call | solution.py:56
  402.2 13.2 %grad_product.8 = (bf16[512,2048]{1,0:T(8,128)(2,1)}, bf16[512,2048]{1,0:T(8,128)(2,1)}) custom-call(bf16[1024,1024]{1,0:T(8,128)(2,1)} %get-tuple-element.119.refs_0_, bf16[1024,1024]{1,0:T(8,128)(2,1)} %copy-done.13, bf16[1024,2048]{1,0:T(8,128)(2,1)} %get-tuple-element.125.refs_2_.refs_1_, bf16[1024,2048]{1,0:T(8,128)(2,1)} %collective-permute-done.18.refs_3_, ...), custom_call_target="tpu_custom_call" | custom-call | flops 131256000512 | tf_op jit(solution)/shard_map/grad_product/pallas_call | solution.py:56
  416.6 20.4 %nt_product.7.refs_2_ = bf16[512,2048]{1,0:T(8,128)(2,1)} custom-call(bf16[1024,1024]{1,0:T(8,128)(2,1)} %get-tuple-element.122.refs_6_.refs_0_, bf16[1024,2048]{1,0:T(8,128)(2,1)} %get-tuple-element.126.refs_1_.refs_2_, bf16[1024,1024]{1,0:T(8,128)(2,1)} %get-tuple-element.123.refs_10_.refs_2_, bf16[1024,2048]{1,0:T(8,128)(2,1)} %get-tuple-element.127.refs_3_.refs_2_, ...), custom_call_target="tpu_custom_call" | custom-call | flops 203743674368 | tf_op jit(solution)/shard_map/nt_product/pallas_call | solution.py:56
  442.1 13.2 %grad_product.9 = (bf16[512,2048]{1,0:T(8,128)(2,1)}, bf16[512,2048]{1,0:T(8,128)(2,1)}) custom-call(bf16[1024,1024]{1,0:T(8,128)(2,1)} %get-tuple-element.115.refs_5_.refs_4_.refs_8_.refs_0_, bf16[1024,1024]{1,0:T(8,128)(2,1)} %collective-permute-done.15.refs_5_.refs_9_.refs_1_, bf16[1024,2048]{1,0:T(8,128)(2,1)} %get-tuple-element.126.refs_1_.refs_2_, ...), custom_call_target="tpu_custom_call" | custom-call | flops 131256000512 | tf_op jit(solution)/shard_map/grad_product/pallas_call | solution.py:56
  456.1 7.5 norm_back.4
  469.3 11.5 %nt_product.8.refs_11_.refs_1_ = bf16[512,2048]{1,0:T(8,128)(2,1)} custom-call(bf16[1024,1024]{1,0:T(8,128)(2,1)} %get-tuple-element.116.refs_2_.refs_0_, bf16[1024,2048]{1,0:T(8,128)(2,1)} %get-tuple-element.125.refs_2_.refs_1_, bf16[2048,6272]{1,0:T(8,128)(2,1)} %all-gather.3.cloned.1.call-done.refs_1_.refs_4_.refs_2_.refs_3_.refs_6_, ...), custom_call_target="tpu_custom_call" | custom-call | flops 109371842560 | tf_op jit(solution)/shard_map/nt_product/pallas_call | solution.py:56
  482.3 20.4 %attend_back.2 = (bf16[1024,1024]{1,0:T(8,128)(2,1)}, bf16[512,1024]{1,0:T(8,128)(2,1)}, bf16[512,1024]{1,0:T(8,128)(2,1)}, bf16[2,512,1024]{2,1,0:T(8,128)(2,1)}, f32[8,128]{1,0:T(8,128)}) custom-call(bf16[1024,1024]{1,0:T(8,128)(2,1)} %get-tuple-element.104.refs_1_.refs_0_, bf16[512,1024]{1,0:T(8,128)(2,1)} %get-tuple-element.100.refs_2_.refs_1_, ...), custom_call_target="tpu_custom_call" | custom-call | flops 249999998976 | tf_op jit(solution)/shard_map/attend_back/pallas_call | solution.py:56
  502.8 7.5 norm_back.5
  532.8 8.7 %grad_product.10 = (bf16[512,1024]{1,0:T(8,128)(2,1)}, bf16[512,1024]{1,0:T(8,128)(2,1)}) custom-call(bf16[1024,1024]{1,0:T(8,128)(2,1)} %get-tuple-element.138.refs_2_.refs_0_, bf16[1024,1024]{1,0:T(8,128)(2,1)} %copy-done.16, bf16[512,1024]{1,0:T(8,128)(2,1)} %get-tuple-element.106.refs_6_.refs_2_, bf16[512,1024]{1,0:T(8,128)(2,1)} %get-tuple-element.109.refs_2_.refs_3_, ...), custom_call_target="tpu_custom_call" | custom-call | flops 83128000512 | tf_op jit(solution)/shard_map/grad_product/pallas_call | solution.py:56
  542.4 11.4 %nt_product.9.refs_4_.refs_1_ = bf16[512,2048]{1,0:T(8,128)(2,1)} custom-call(bf16[1024,1024]{1,0:T(8,128)(2,1)} %get-tuple-element.116.refs_2_.refs_0_, bf16[1024,2048]{1,0:T(8,128)(2,1)} %get-tuple-element.125.refs_2_.refs_1_, bf16[2048,6272]{1,0:T(8,128)(2,1)} %all-gather.3.cloned.1.call-done.refs_1_.refs_4_.refs_2_.refs_3_.refs_6_, ...), custom_call_target="tpu_custom_call" | custom-call | flops 109371842560 | tf_op jit(solution)/shard_map/nt_product/pallas_call | solution.py:56
  554.3 13.2 %grad_product.11 = (bf16[512,2048]{1,0:T(8,128)(2,1)}, bf16[512,2048]{1,0:T(8,128)(2,1)}) custom-call(bf16[1024,1024]{1,0:T(8,128)(2,1)} %get-tuple-element.115.refs_5_.refs_4_.refs_8_.refs_0_, bf16[1024,1024]{1,0:T(8,128)(2,1)} %collective-permute-done.15.refs_5_.refs_9_.refs_1_, bf16[1024,2048]{1,0:T(8,128)(2,1)} %get-tuple-element.127.refs_3_.refs_2_, ...), custom_call_target="tpu_custom_call" | custom-call | flops 131256000512 | tf_op jit(solution)/shard_map/grad_product/pallas_call | solution.py:56
  573.8 8.8 %nt_product.10.refs_12_.refs_1_.refs_2_ = bf16[512,2048]{1,0:T(8,128)(2,1)} custom-call(bf16[1024,1024]{1,0:T(8,128)(2,1)} %get-tuple-element.145.refs_0_.refs_11_, bf16[1024,1024]{1,0:T(8,128)(2,1)} %get-tuple-element.148.refs_1_.refs_7_, bf16[2048,6272]{1,0:T(8,128)(2,1)} %all-gather.3.cloned.1.call-done.refs_1_.refs_4_.refs_2_.refs_3_.refs_6_, ...), custom_call_target="tpu_custom_call" | custom-call | flops 77914562560 | tf_op jit(solution)/shard_map/nt_product/pallas_call | solution.py:56
  583.6 20.5 %attend_back.3 = (bf16[1024,1024]{1,0:T(8,128)(2,1)}, bf16[512,1024]{1,0:T(8,128)(2,1)}, bf16[512,1024]{1,0:T(8,128)(2,1)}, bf16[2,512,1024]{2,1,0:T(8,128)(2,1)}, f32[8,128]{1,0:T(8,128)}) custom-call(bf16[1024,1024]{1,0:T(8,128)(2,1)} %get-tuple-element.104.refs_1_.refs_0_, ...), custom_call_target="tpu_custom_call", output_to_operand_aliasing={{0}: (11, {})} | custom-call | flops 249999998976 | tf_op jit(solution)/shard_map/attend_back/pallas_call | solution.py:56
  624.5 8.4 %grad_product.12 = (bf16[512,1024]{1,0:T(8,128)(2,1)}, bf16[512,1024]{1,0:T(8,128)(2,1)}) custom-call(bf16[1024,1024]{1,0:T(8,128)(2,1)} %get-tuple-element.103.refs_5_.refs_0_, bf16[1024,1024]{1,0:T(8,128)(2,1)} %collective-permute-done.13.refs_7_.refs_1_, bf16[1024,1024]{1,0:T(8,128)(2,1)} %get-tuple-element.154.refs_2_.refs_0_, ...), custom_call_target="tpu_custom_call" | custom-call | flops 83128000512 | tf_op jit(solution)/shard_map/grad_product/pallas_call | solution.py:56
  632.8 7.5 collective-permute-done.33.refs_2_
  644.8 8.8 %nt_product.11.refs_4_.refs_1_.refs_2_ = bf16[512,2048]{1,0:T(8,128)(2,1)} custom-call(bf16[1024,1024]{1,0:T(8,128)(2,1)} %get-tuple-element.154.refs_2_.refs_0_, bf16[1024,1024]{1,0:T(8,128)(2,1)} %get-tuple-element.158.refs_1_.refs_2_, bf16[2048,6272]{1,0:T(8,128)(2,1)} %all-gather.3.cloned.1.call-done.refs_1_.refs_4_.refs_2_.refs_3_.refs_6_, ...), custom_call_target="tpu_custom_call" | custom-call | flops 77914562560 | tf_op jit(solution)/shard_map/nt_product/pallas_call | solution.py:56
  657.0 9.2 %grad_product.13 = (bf16[512,1024]{1,0:T(8,128)(2,1)}, bf16[512,1024]{1,0:T(8,128)(2,1)}) custom-call(bf16[1024,1024]{1,0:T(8,128)(2,1)} %get-tuple-element.103.refs_5_.refs_0_, bf16[1024,1024]{1,0:T(8,128)(2,1)} %collective-permute-done.13.refs_7_.refs_1_, bf16[1024,1024]{1,0:T(8,128)(2,1)} %get-tuple-element.158.refs_1_.refs_2_, ...), custom_call_target="tpu_custom_call" | custom-call | flops 83128000512 | tf_op jit(solution)/shard_map/grad_product/pallas_call | solution.py:56
  673.6 7.5 norm_back.6
  681.1 21.8 %collective-permute-done.36.refs_3_ = bf16[512,2048]{1,0:T(8,128)(2,1)} collective-permute-done((bf16[512,2048]{1,0:T(8,128)(2,1)}, bf16[512,2048]{1,0:T(8,128)(2,1)}, u32[]{:S(2)}, u32[]{:S(2)}) %collective-permute-start.36) | collective-permute-done | bytes 2097184 | tf_op jit(solution)/shard_map/one1_over_tp/ppermute | solution.py:824
  702.9 7.2 norm_back.7
  718.4 42.7 %psum.7 = f32[4352]{0:T(1024)S(1)} all-reduce(f32[4352]{0:T(1024)S(1)} %pad_maximum_fusion.4), channel_id=1, replica_groups=mesh['dp'=4,'ctx'=4,'tp'=2] {'dp','ctx','tp'}, use_global_device_ids=true, to_apply=%region_10.11 | all-reduce | flops 4352 | bytes 34816 | tf_op jit(solution)/shard_map/psum | solution.py:1065
  (225 shorter events, 197.0 us)
Async XLA Ops:
  7.2 138.7 %all-gather.3.cloned.1.call-start = ((), (), s32[]{:S(2)}) async-start(), calls=%async_computation.4 | async-start | bytes 27295744 | tf_op jit(solution)/shard_map/all_gather | solution.py:841
  12.0 332.4 %all-gather.5.cloned.1.call-start = ((), (), s32[]{:S(2)}) async-start(), calls=%async_computation.5 | async-start | bytes 26738688 | tf_op jit(solution)/shard_map/all_gather | solution.py:911
  161.1 25.6 %collective-permute-start.2 = (bf16[512,1024]{1,0:T(8,128)(2,1)}, bf16[512,1024]{1,0:T(8,128)(2,1)}, u32[]{:S(2)}, u32[]{:S(2)}) collective-permute-start(bf16[512,1024]{1,0:T(8,128)(2,1)} %get-tuple-element.100.refs_2_.refs_1_), channel_id=1, source_target_pairs={{0,4},{4,0},{2,6},{6,2},{1,5},{5,1},{3,7},{7,3},{8,12},{12,8},{10,... | collective-permute-start | bytes 3145736 | tf_op jit(solution)/shard_map/kv0_over_x/ppermute | solution.py:824
  162.3 25.6 %collective-permute-start.1 = (bf16[512,1024]{1,0:T(8,128)(2,1)}, bf16[512,1024]{1,0:T(8,128)(2,1)}, u32[]{:S(2)}, u32[]{:S(2)}) collective-permute-start(bf16[512,1024]{1,0:T(8,128)(2,1)} %get-tuple-element.100.refs_2_.refs_1_), channel_id=1, source_target_pairs={{0,2},{2,0},{4,6},{6,4},{1,3},{3,1},{5,7},{7,5},{8,10},{10,8},{12,... | collective-permute-start | bytes 3145736 | tf_op jit(solution)/shard_map/kv0_over_core/ppermute | solution.py:824
  165.4 48.4 %collective-permute-start.7 = (bf16[1024,1024]{1,0:T(8,128)(2,1)}, bf16[1024,1024]{1,0:T(8,128)(2,1)}, u32[]{:S(2)}, u32[]{:S(2)}) collective-permute-start(bf16[1024,1024]{1,0:T(8,128)(2,1)} %constant_dynamic-slice_fusion.refs_5_), channel_id=1, source_target_pairs={{0,1},{1,0},{2,3},{3,2},{4,5},{5,4},{6,7},{7,6},{8,9},{9,8},{10,11... | collective-permute-start | bytes 6291464 | tf_op jit(solution)/shard_map/output_proj_over_tp/ppermute | solution.py:824
  186.7 26.7 %collective-permute-start.4 = (bf16[512,1024]{1,0:T(8,128)(2,1)}, bf16[512,1024]{1,0:T(8,128)(2,1)}, u32[]{:S(2)}, u32[]{:S(2)}) collective-permute-start(bf16[512,1024]{1,0:T(8,128)(2,1)} %get-tuple-element.105.refs_5_.refs_2_.refs_1_), channel_id=1, source_target_pairs={{0,4},{4,0},{2,6},{6,2},{1,5},{5,1},{3,7},{7,3},{8,12},{12,8},{10,... | collective-permute-start | bytes 3145736 | tf_op jit(solution)/shard_map/kv1_over_x/ppermute | solution.py:824
  214.3 62.4 %collective-permute-start.13 = (bf16[1024,1024]{1,0:T(8,128)(2,1)}, bf16[1024,1024]{1,0:T(8,128)(2,1)}, u32[]{:S(2)}, u32[]{:S(2)}) collective-permute-start(bf16[1024,1024]{1,0:T(8,128)(2,1)} %get-tuple-element.114), channel_id=1, source_target_pairs={{0,2},{2,0},{4,6},{6,4},{1,3},{3,1},{5,7},{7,5},{8,10},{10,8},{12,... | collective-permute-start | bytes 6291464 | tf_op jit(solution)/shard_map/normed_one_over_core/ppermute | solution.py:824
  214.5 62.1 %collective-permute-start.11 = (bf16[512,1024]{1,0:T(8,128)(2,1)}, bf16[512,1024]{1,0:T(8,128)(2,1)}, u32[]{:S(2)}, u32[]{:S(2)}) collective-permute-start(bf16[512,1024]{1,0:T(8,128)(2,1)} %get-tuple-element.106.refs_6_.refs_2_), channel_id=1, source_target_pairs={{0,2},{2,0},{4,6},{6,4},{1,3},{3,1},{5,7},{7,5},{8,10},{10,8},{12,... | collective-permute-start | bytes 3145736 | tf_op jit(solution)/shard_map/attended_over_core/ppermute | solution.py:824
  214.8 25.7 %collective-permute-start.10 = (bf16[512,1024]{1,0:T(8,128)(2,1)}, bf16[512,1024]{1,0:T(8,128)(2,1)}, u32[]{:S(2)}, u32[]{:S(2)}) collective-permute-start(bf16[512,1024]{1,0:T(8,128)(2,1)} %get-tuple-element.106.refs_6_.refs_2_), channel_id=1, source_target_pairs={{0,1},{1,0},{2,3},{3,2},{4,5},{5,4},{6,7},{7,6},{8,9},{9,8},{10,11... | collective-permute-start | bytes 3145736 | tf_op jit(solution)/shard_map/attended0_over_tp/ppermute | solution.py:824
  216.3 309.9 %reduce-scatter.5.cloned.1.call-start = ((), (), s32[]{:S(2)}) async-start(), calls=%async_computation.6 | async-start | bytes 3932160 | tf_op jit(solution)/shard_map/first_third_over_dp/reduce_scatter | solution.py:947
  236.9 39.7 %collective-permute-start.12 = (bf16[512,1024]{1,0:T(8,128)(2,1)}, bf16[512,1024]{1,0:T(8,128)(2,1)}, u32[]{:S(2)}, u32[]{:S(2)}) collective-permute-start(bf16[512,1024]{1,0:T(8,128)(2,1)} %get-tuple-element.109.refs_2_.refs_3_), channel_id=1, source_target_pairs={{0,2},{2,0},{4,6},{6,4},{1,3},{3,1},{5,7},{7,5},{8,10},{10,8},{12,... | collective-permute-start | bytes 3145736 | tf_op jit(solution)/shard_map/attended_over_core/ppermute | solution.py:824
  237.2 25.7 %collective-permute-start.9 = (bf16[512,1024]{1,0:T(8,128)(2,1)}, bf16[512,1024]{1,0:T(8,128)(2,1)}, u32[]{:S(2)}, u32[]{:S(2)}) collective-permute-start(bf16[512,1024]{1,0:T(8,128)(2,1)} %get-tuple-element.109.refs_2_.refs_3_), channel_id=1, source_target_pairs={{0,1},{1,0},{2,3},{3,2},{4,5},{5,4},{6,7},{7,6},{8,9},{9,8},{10,11... | collective-permute-start | bytes 3145736 | tf_op jit(solution)/shard_map/attended1_over_tp/ppermute | solution.py:824
  340.2 97.5 %collective-permute-start.23 = (bf16[512,3072]{1,0:T(8,128)(2,1)}, bf16[512,3072]{1,0:T(8,128)(2,1)}, u32[]{:S(2)}, u32[]{:S(2)}) collective-permute-start(bf16[512,3072]{1,0:T(8,128)(2,1)} %get-tuple-element.129), channel_id=1, source_target_pairs={{0,4},{4,0},{2,6},{6,2},{1,5},{5,1},{3,7},{7,3},{8,12},{12,8},{10,... | collective-permute-start | bytes 9437192 | tf_op jit(solution)/shard_map/first_third_over_x/ppermute | solution.py:824
  380.2 36.4 %collective-permute-start.19 = (bf16[1024,2048]{1,0:T(8,128)(2,1)}, bf16[1024,2048]{1,0:T(8,128)(2,1)}, u32[]{:S(2)}, u32[]{:S(2)}) collective-permute-start(bf16[1024,2048]{1,0:T(8,128)(2,1)} %get-tuple-element.126.refs_1_.refs_2_), channel_id=1, source_target_pairs={{0,2},{2,0},{4,6},{6,4},{1,3},{3,1},{5,7},{7,5},{8,10},{10,8},{12,... | collective-permute-start | bytes 12582920 | tf_op jit(solution)/shard_map/gate_back_two_over_core/ppermute | solution.py:824
  380.5 36.1 %collective-permute-start.20 = (bf16[1024,2048]{1,0:T(8,128)(2,1)}, bf16[1024,2048]{1,0:T(8,128)(2,1)}, u32[]{:S(2)}, u32[]{:S(2)}) collective-permute-start(bf16[1024,2048]{1,0:T(8,128)(2,1)} %get-tuple-element.127.refs_3_.refs_2_), channel_id=1, source_target_pairs={{0,2},{2,0},{4,6},{6,4},{1,3},{3,1},{5,7},{7,5},{8,10},{10,8},{12,... | collective-permute-start | bytes 12582920 | tf_op jit(solution)/shard_map/up_back_two_over_core/ppermute | solution.py:824
  400.8 55.4 %collective-permute-start.22 = (bf16[512,2048]{1,0:T(8,128)(2,1)}, bf16[512,2048]{1,0:T(8,128)(2,1)}, u32[]{:S(2)}, u32[]{:S(2)}) collective-permute-start(bf16[512,2048]{1,0:T(8,128)(2,1)} %nt_product.6.refs_4_.refs_2_), channel_id=1, source_target_pairs={{0,1},{1,0},{2,3},{3,2},{4,5},{5,4},{6,7},{7,6},{8,9},{9,8},{10,11... | collective-permute-start | bytes 6291464 | tf_op jit(solution)/shard_map/back0_over_tp/ppermute | solution.py:824
  415.4 110.7 %collective-permute-start.26 = (bf16[512,2048]{1,0:T(8,128)(2,1)}, bf16[512,2048]{1,0:T(8,128)(2,1)}, u32[]{:S(2)}, u32[]{:S(2)}) collective-permute-start(bf16[512,2048]{1,0:T(8,128)(2,1)} %get-tuple-element.140), channel_id=1, source_target_pairs={{0,4},{4,0},{2,6},{6,2},{1,5},{5,1},{3,7},{7,3},{8,12},{12,8},{10,... | collective-permute-start | bytes 6291464 | tf_op jit(solution)/shard_map/down_two_over_x/ppermute | solution.py:824
  437.1 65.7 %collective-permute-start.21 = (bf16[512,2048]{1,0:T(8,128)(2,1)}, bf16[512,2048]{1,0:T(8,128)(2,1)}, u32[]{:S(2)}, u32[]{:S(2)}) collective-permute-start(bf16[512,2048]{1,0:T(8,128)(2,1)} %nt_product.7.refs_2_), channel_id=1, source_target_pairs={{0,1},{1,0},{2,3},{3,2},{4,5},{5,4},{6,7},{7,6},{8,9},{9,8},{10,11... | collective-permute-start | bytes 6291464 | tf_op jit(solution)/shard_map/back1_over_tp/ppermute | solution.py:824
  442.1 178.0 %reduce-scatter.7.cloned.1.call-start = ((), (), s32[]{:S(2)}) async-start(), calls=%async_computation.7 | async-start | bytes 5242880 | tf_op jit(solution)/shard_map/down_gate_two_over_dp/reduce_scatter | solution.py:947
  455.3 60.5 %collective-permute-start.24 = (bf16[512,2048]{1,0:T(8,128)(2,1)}, bf16[512,2048]{1,0:T(8,128)(2,1)}, u32[]{:S(2)}, u32[]{:S(2)}) collective-permute-start(bf16[512,2048]{1,0:T(8,128)(2,1)} %get-tuple-element.137), channel_id=1, source_target_pairs={{0,4},{4,0},{2,6},{6,2},{1,5},{5,1},{3,7},{7,3},{8,12},{12,8},{10,... | collective-permute-start | bytes 6291464 | tf_op jit(solution)/shard_map/gate_two_over_x/ppermute | solution.py:824
  480.8 73.6 %collective-permute-start.29 = (bf16[512,2048]{1,0:T(8,128)(2,1)}, bf16[512,2048]{1,0:T(8,128)(2,1)}, u32[]{:S(2)}, u32[]{:S(2)}) collective-permute-start(bf16[512,2048]{1,0:T(8,128)(2,1)} %nt_product.8.refs_11_.refs_1_), channel_id=1, source_target_pairs={{0,1},{1,0},{2,3},{3,2},{4,5},{5,4},{6,7},{7,6},{8,9},{9,8},{10,11... | collective-permute-start | bytes 6291464 | tf_op jit(solution)/shard_map/out0_over_tp/ppermute | solution.py:824
  525.0 43.7 %collective-permute-start.30 = (bf16[512,1024]{1,0:T(8,128)(2,1)}, bf16[512,1024]{1,0:T(8,128)(2,1)}, u32[]{:S(2)}, u32[]{:S(2)}) collective-permute-start(bf16[512,1024]{1,0:T(8,128)(2,1)} %add_rows.7.refs_4_), channel_id=1, source_target_pairs={{0,4},{4,0},{2,6},{6,2},{1,5},{5,1},{3,7},{7,3},{8,12},{12,8},{10,... | collective-permute-start | bytes 3145736 | tf_op jit(solution)/shard_map/kv_grad0_over_x/ppermute | solution.py:824
  531.4 230.8 %reduce-scatter.11.cloned.1.call-start = ((), (), s32[]{:S(2)}) async-start(), calls=%async_computation.9 | async-start | bytes 3932160 | tf_op jit(solution)/shard_map/up_two_output_over_dp/reduce_scatter | solution.py:947
  541.6 32.2 %collective-permute-start.31 = (bf16[512,1024]{1,0:T(8,128)(2,1)}, bf16[512,1024]{1,0:T(8,128)(2,1)}, u32[]{:S(2)}, u32[]{:S(2)}) collective-permute-start(bf16[512,1024]{1,0:T(8,128)(2,1)} %get-tuple-element.149), channel_id=1, source_target_pairs={{0,4},{4,0},{2,6},{6,2},{1,5},{5,1},{3,7},{7,3},{8,12},{12,8},{10,... | collective-permute-start | bytes 3145736 | tf_op jit(solution)/shard_map/output_over_x/ppermute | solution.py:824
  553.8 61.6 %collective-permute-start.28 = (bf16[512,2048]{1,0:T(8,128)(2,1)}, bf16[512,2048]{1,0:T(8,128)(2,1)}, u32[]{:S(2)}, u32[]{:S(2)}) collective-permute-start(bf16[512,2048]{1,0:T(8,128)(2,1)} %nt_product.9.refs_4_.refs_1_), channel_id=1, source_target_pairs={{0,1},{1,0},{2,3},{3,2},{4,5},{5,4},{6,7},{7,6},{8,9},{9,8},{10,11... | collective-permute-start | bytes 6291464 | tf_op jit(solution)/shard_map/out1_over_tp/ppermute | solution.py:824
  567.5 52.6 %collective-permute-start.35 = (bf16[512,2048]{1,0:T(8,128)(2,1)}, bf16[512,2048]{1,0:T(8,128)(2,1)}, u32[]{:S(2)}, u32[]{:S(2)}) collective-permute-start(bf16[512,2048]{1,0:T(8,128)(2,1)} %get-tuple-element.156), channel_id=1, source_target_pairs={{0,4},{4,0},{2,6},{6,2},{1,5},{5,1},{3,7},{7,3},{8,12},{12,8},{10,... | collective-permute-start | bytes 6291464 | tf_op jit(solution)/shard_map/up_two_over_x/ppermute | solution.py:824
  582.6 91.1 %collective-permute-start.37 = (bf16[512,2048]{1,0:T(8,128)(2,1)}, bf16[512,2048]{1,0:T(8,128)(2,1)}, u32[]{:S(2)}, u32[]{:S(2)}) collective-permute-start(bf16[512,2048]{1,0:T(8,128)(2,1)} %nt_product.10.refs_12_.refs_1_.refs_2_), channel_id=1, source_target_pairs={{0,1},{1,0},{2,3},{3,2},{4,5},{5,4},{6,7},{7,6},{8,9},{9,8},{10,11... | collective-permute-start | bytes 6291464 | tf_op jit(solution)/shard_map/one0_over_tp/ppermute | solution.py:824
  614.5 25.8 %collective-permute-start.33 = (bf16[512,1024]{1,0:T(8,128)(2,1)}, bf16[512,1024]{1,0:T(8,128)(2,1)}, u32[]{:S(2)}, u32[]{:S(2)}) collective-permute-start(bf16[512,1024]{1,0:T(8,128)(2,1)} %add_rows.9.refs_4_), channel_id=1, source_target_pairs={{0,4},{4,0},{2,6},{6,2},{1,5},{5,1},{3,7},{7,3},{8,12},{12,8},{10,... | collective-permute-start | bytes 3145736 | tf_op jit(solution)/shard_map/kv_grad1_over_x/ppermute | solution.py:824
  653.6 112.0 %reduce-scatter.9.cloned.1.call-start = ((), (), s32[]{:S(2)}) async-start(), calls=%async_computation.8 | async-start | bytes 2621440 | tf_op jit(solution)/shard_map/query_key_over_dp/reduce_scatter | solution.py:947
  653.6 56.5 %collective-permute-start.39 = (bf16[512,1024]{1,0:T(8,128)(2,1)}, bf16[512,1024]{1,0:T(8,128)(2,1)}, u32[]{:S(2)}, u32[]{:S(2)}) collective-permute-start(bf16[512,1024]{1,0:T(8,128)(2,1)} %get-tuple-element.168), channel_id=1, source_target_pairs={{0,4},{4,0},{2,6},{6,2},{1,5},{5,1},{3,7},{7,3},{8,12},{12,8},{10,... | collective-permute-start | bytes 3145736 | tf_op jit(solution)/shard_map/query_over_x/ppermute | solution.py:824
  654.9 48.0 %collective-permute-start.36 = (bf16[512,2048]{1,0:T(8,128)(2,1)}, bf16[512,2048]{1,0:T(8,128)(2,1)}, u32[]{:S(2)}, u32[]{:S(2)}) collective-permute-start(bf16[512,2048]{1,0:T(8,128)(2,1)} %nt_product.11.refs_4_.refs_1_.refs_2_), channel_id=1, source_target_pairs={{0,1},{1,0},{2,3},{3,2},{4,5},{5,4},{6,7},{7,6},{8,9},{9,8},{10,11... | collective-permute-start | bytes 6291464 | tf_op jit(solution)/shard_map/one1_over_tp/ppermute | solution.py:824
  669.8 40.3 %collective-permute-start.40 = (bf16[512,1024]{1,0:T(8,128)(2,1)}, bf16[512,1024]{1,0:T(8,128)(2,1)}, u32[]{:S(2)}, u32[]{:S(2)}) collective-permute-start(bf16[512,1024]{1,0:T(8,128)(2,1)} %get-tuple-element.169), channel_id=1, source_target_pairs={{0,4},{4,0},{2,6},{6,2},{1,5},{5,1},{3,7},{7,3},{8,12},{12,8},{10,... | collective-permute-start | bytes 3145736 | tf_op jit(solution)/shard_map/key_over_x/ppermute | solution.py:824
  (40 other events, 355.7 us)
Sparse Core Ops, SparseCore 0:
  12.1 133.7 all-gather.2
  216.4 127.9 all-gather.4
  442.2 60.5 reduce-scatter.4
  531.5 76.0 reduce-scatter.6
  653.7 59.6 reduce-scatter.10
  715.6 44.8 reduce-scatter.8

commit v4 on v3

--- a/solution.py
+++ b/solution.py
@@ -670,7 +670,7 @@
     terms_ref[...] += jnp.sum((own * unit).reshape(-1, 8, own.shape[1]), axis=0)
 
 
-def norm_back(values, base, own, other, gain, row, types, into, after=()):
+def norm_back(values, base, own, other, gain, row, types, into, after=(), cost=7.5):
     tokens, width = values.shape
     rows = own.shape[0]
     tile = min(256, rows)
@@ -693,7 +693,7 @@
         alias=alias,
         after=after,
         name="norm_back",
-        cost=7.5,
+        cost=cost,
     )
 
 
@@ -814,7 +814,6 @@
     dp_size, tp_size = lax.axis_size("dp"), lax.axis_size("tp")
     ctx, tp_at = lax.axis_index("ctx"), lax.axis_index("tp")
     x_at, core_at = ctx // 2, ctx % 2
-    share = lax.axis_index("dp") * 4 + ctx
     half_rows = tokens // 2
     half_seqs = seqs // 2
     pair = tp_size == 2
@@ -1039,48 +1038,53 @@
     q_pair = [q_back], [core_swap(q_back, "query_back")]
     outputs = sum_rows(middle, out_started[0], 0, None, after=(held[0],))
     sent = send_keys(1, held, (outputs,))
-    outputs = sum_rows(middle, out_started[1], half_rows, outputs, after=(sent,))
-    done, up_out = over_dp("up_two_output", [up_two, output_grad], after=(outputs, more_out))
-    query_grad = Gradient("query", [(one_turned, q_pair)], after=(done,))
-    k_back = key_half(1, (query_grad.keep,))
+    query_grad = Gradient("query", [(one_turned, q_pair)], after=(sent,))
+    outputs = sum_rows(middle, out_started[1], half_rows, outputs, after=(query_grad.keep,))
+    done, output_out = over_dp("output", [output_grad], after=(outputs, more_out))
+    done, up_out = over_dp("up_two", [up_two], after=(done,))
+    terms = gain_terms(input_rows, one[0][0], 0, after=(done,))
+    k_back = key_half(1, (terms,))
     part = one_half(1, ())
     k_pair = [k_back], [core_swap(k_back, "key_back")]
     key_grad = Gradient("key", [(one_turned, k_pair)], after=(part,))
-    latest = (key_grad.keep,)
-    for h in range(2):
-        part = gain_terms(input_rows, one[h][0], h * half_rows, after=latest)
-        latest = (part,)
-        sums["first"] = sums["first"] + jnp.sum(part, axis=0)
-    result = None
-    for h in range(2):
-        result = norm_back(
-            input_rows, grad_middle, *one[h], gain_first, h * half_rows, (BF16,), result, after=latest
+
+    def input_half(h, into, after, cost):
+        return norm_back(
+            input_rows, grad_middle, *one[h], gain_first, h * half_rows, (BF16,), into, after=after, cost=cost
         )[0:1]
-        latest = ()
+
+    result = input_half(0, None, (key_grad.keep, query_grad.from_x), 7.5)
     done, heads_out = over_dp("query_key", [query_grad, key_grad], after=(result[0],))
+    part = gain_terms(input_rows, one[1][0], half_rows, after=(done,))
+    sums["first"] = jnp.sum(terms + part, axis=0)
 
     if not pair:
         sums["first"], sums["second"] = sums["first"] / tp_size, sums["second"] / tp_size
-    totals = jnp.concatenate([sums[name] for name in ("first", "second", "query", "key")])
-    totals = lax.psum(behind(totals, done), ("dp", "ctx", "tp"))
-    cut_total = lambda start, size: lax.dynamic_slice(totals, (start + share * size,), (size,))
-
+    places = dp_size * 4
+    totals = [sums[name].reshape(places, -1) for name in ("first", "second", "query", "key")]
+    totals = jnp.concatenate(totals, axis=1)
+    totals = jnp.broadcast_to(totals[:, None, :], (places, tp_size, totals.shape[1]))
+    totals = totals.reshape(places * tp_size, -1)
+    totals = lax.all_to_all(totals, ("dp", "ctx", "tp"), 0, 0, tiled=True)
+
+    result = input_half(1, result, (part,), 300)
+    totals = jnp.sum(behind(totals, result[0]), axis=0)
     grad_kv = heads_out[:, columns:].astype(F32)
     down_out, gate_out, up_first = [first_out[:, at * third : (at + 1) * third] for at in range(3)]
     beside = lambda left, right: jnp.concatenate([left, right], axis=1).astype(F32)
     return (
         outputs.reshape(inputs.shape),
         result[0].reshape(inputs.shape),
-        cut_total(0, shard),
+        totals[0:shard],
         heads_out[:, 0:columns].astype(F32),
         split_heads(grad_kv, 0),
         split_heads(grad_kv, 1),
-        cut_total(2 * width, head_shard),
-        cut_total(2 * width + HEAD_DIM, head_shard),
-        up_out[:, 2 * third :].astype(F32).T,
-        cut_total(width, shard),
+        totals[2 * shard : 2 * shard + head_shard],
+        totals[2 * shard + head_shard :],
+        output_out.astype(F32).T,
+        totals[shard : 2 * shard],
         beside(gate_out, more_out[:, 2 * third :]),
-        beside(up_first, up_out[:, 0 : 2 * third]),
+        beside(up_first, up_out),
         beside(down_out, more_out[:, 0 : 2 * third]).T,
     )
 

time: 784 us -> 774 us (0.987)
  blocking collectives: 42.7 us -> 0 us
  waiting for transfers between devices: 182 us -> 195 us
    psum x1 -> x0, blocking collectives: 42.7 us -> none  [shards(): totals = lax.psum(behind(totals, done), ('dp', 'ctx', 'tp'))]
    reduce_scatter x4 -> x5, waiting for transfers between devices: 0.01 us -> 28.9 us  [over_dp(): lax.psum_scatter(summed, 'dp', scatter_dimension=0, tiled=True)]
    ppermute x41, waiting for transfers between devices: 63.1 us -> 47.2 us  [swap(): return lax.ppermute(value, axis, pairs)]
    unnamed x51 -> x66, local copies, waits for them, and re-layouts: 14.2 us -> 16.4 us
    pallas_call x49 -> x50, Pallas kernels: 474 us -> 475 us  [call(): pl.pallas_call(body, grid_spec=pltpu.PrefetchScalarGridSpec(num_scalar_pr...]
  transfers between devices with their start and end apart: 47 -> 49, of which waited for: 14 -> 12; matrix products, arithmetic and copies ran while one was open for 2% -> 3% of each run, Pallas kernels for 59% -> 60%
where the time goes in v4:
time: 774 us; the launch traced here: 766 us
  Pallas kernels  475 us (61%)
  waiting for transfers between devices  195 us (25%)
  starting transfers between devices  33.6 us (4%)
  local copies, waits for them, and re-layouts  29.2 us (4%)
  other arithmetic  18.2 us (2%)
  between operations  14.8 us (2%)
    pallas_call x50, Pallas kernels, call(): pl.pallas_call(body, grid_spec=pltpu.PrefetchScalarGridSpec(num_scalar_pr...  475 us
    all_gather x1, waiting for transfers between devices, shards(): weights = lax.all_gather(shard_one, ('dp', 'ctx'), axis=0, tiled=True)  115 us
    ppermute x41, waiting for transfers between devices, swap(): return lax.ppermute(value, axis, pairs)  47.2 us
    ppermute x41, starting transfers between devices, swap(): return lax.ppermute(value, axis, pairs)  29.3 us
    reduce_scatter x5, waiting for transfers between devices, over_dp(): lax.psum_scatter(summed, 'dp', scatter_dimension=0, tiled=True)  28.9 us
    unnamed x66, local copies, waits for them, and re-layouts  16.4 us
  transfers between devices with their start and end apart: 49, of which 12 were waited for; matrix products, arithmetic and copies ran while one was open for 3% of the time, Pallas kernels for 60%

profile of v4, /device:TPU:0, one launch (start us, length us, event | category | flops | bytes accessed | tf_op | source)
XLA Modules:
  0.0 766.2 jit_solution(16999788894904135295)
XLA Ops:
  30.7 115.1 %all-gather.3.cloned.1.call-done.refs_1_.refs_4_.refs_2_.refs_3_.refs_6_ = bf16[2048,6272]{1,0:T(8,128)(2,1)} async-done(((bf16[128,6272]{1,0:T(8,128)(2,1)}), bf16[2048,6272]{1,0:T(8,128)(2,1)}) %all-gather.3.cloned.1.call-update) | async-done | bytes 25690128 | tf_op jit(solution)/shard_map/all_gather | solution.py:840
  154.2 6.8 project.3
  166.8 6.8 project.4
  188.9 9.9 %project.5 = (bf16[1024,1024]{1,0:T(8,128)(2,1)}, f32[1024,1024]{1,0:T(8,128)}) custom-call(bf16[1024,2048]{1,0:T(8,128)(2,1)} %norm_rows.1.refs_0_.refs_1_.refs_2_.refs_3_.refs_4_, bf16[2048,6272]{1,0:T(8,128)(2,1)} %all-gather.3.cloned.1.call-done.refs_1_.refs_4_.refs_2_.refs_3_.refs_6_, f32[1024,128]{1,0:T(8,128)} %get-tuple-element.97.refs_2_.refs_8_.refs_4_, ...), custom_call_target="tpu_custom_call" | custom-call | flops 99999997952 | tf_op jit(solution)/shard_map/project/pallas_call | solution.py:56
  199.8 13.9 %attend.2 = (bf16[512,1024]{1,0:T(8,128)(2,1)}, bf16[2,2048,1024]{2,1,0:T(8,128)(2,1)}) custom-call(s32[4,8]{1,0:T(4,128)} %copy-done.14, bf16[1024,1024]{1,0:T(8,128)(2,1)} %get-tuple-element.104.refs_1_.refs_0_, bf16[512,1024]{1,0:T(8,128)(2,1)} %get-tuple-element.100.refs_2_.refs_1_, bf16[512,1024]{1,0:T(8,128)(2,1)} %collective-permute-done.1.refs_6_.refs_3_.refs_2_, ...), custom_call_target="tpu_custom_call" | custom-call | flops 109999996928 | tf_op jit(solution)/shard_map/attend/pallas_call | solution.py:56
  223.6 13.5 %attend.3 = (bf16[512,1024]{1,0:T(8,128)(2,1)}, bf16[2,2048,1024]{2,1,0:T(8,128)(2,1)}) custom-call(s32[4,8]{1,0:T(4,128)} %copy-done.14, bf16[1024,1024]{1,0:T(8,128)(2,1)} %get-tuple-element.104.refs_1_.refs_0_, bf16[512,1024]{1,0:T(8,128)(2,1)} %get-tuple-element.105.refs_5_.refs_2_.refs_1_, bf16[512,1024]{1,0:T(8,128)(2,1)} %copy-done.27, ...), custom_call_target="tpu_custom_call" | custom-call | flops 109999996928 | tf_op jit(solution)/shard_map/attend/pallas_call | solution.py:56
  240.9 13.9 %output_join.2 = (f32[1024,2048]{1,0:T(8,128)}, bf16[1024,2048]{1,0:T(8,128)(2,1)}) custom-call(s32[2]{0:T(128)} %pad_add_fusion.1.refs_0_, bf16[1024,2048]{1,0:T(8,128)(2,1)} %bitcast.69, bf16[512,1024]{1,0:T(8,128)(2,1)} %get-tuple-element.106.refs_6_.refs_2_, bf16[512,1024]{1,0:T(8,128)(2,1)} %collective-permute-done.10.refs_3_, ...), custom_call_target="tpu_custom_call" | custom-call | flops 149999992832 | tf_op jit(solution)/shard_map/output_join/pallas_call | solution.py:56
  254.8 8.4 %collective-permute-done.9.refs_3_ = bf16[512,1024]{1,0:T(8,128)(2,1)} collective-permute-done((bf16[512,1024]{1,0:T(8,128)(2,1)}, bf16[512,1024]{1,0:T(8,128)(2,1)}, u32[]{:S(2)}, u32[]{:S(2)}) %collective-permute-start.9) | collective-permute-done | bytes 1048608 | tf_op jit(solution)/shard_map/attended1_over_tp/ppermute | solution.py:823
  263.2 13.7 %output_join.3 = (f32[1024,2048]{1,0:T(8,128)}, bf16[1024,2048]{1,0:T(8,128)(2,1)}) custom-call(s32[2]{0:T(128)} %pad_add_fusion.1.refs_0_, bf16[1024,2048]{1,0:T(8,128)(2,1)} %bitcast.70, bf16[512,1024]{1,0:T(8,128)(2,1)} %get-tuple-element.109.refs_2_.refs_3_, ...), custom_call_target="tpu_custom_call", output_to_operand_aliasing={{0}: (8, {}), {1}: (9, {})} | custom-call | flops 149999992832 | tf_op jit(solution)/shard_map/output_join/pallas_call | solution.py:56
  283.2 21.2 %feed.2 = (bf16[1024,1024]{1,0:T(8,128)(2,1)}, bf16[1024,1024]{1,0:T(8,128)(2,1)}, bf16[1024,1024]{1,0:T(8,128)(2,1)}) custom-call(bf16[1024,2048]{1,0:T(8,128)(2,1)} %get-tuple-element.113.refs_1_.refs_2_.refs_3_.refs_4_.refs_0_, bf16[1024,2048]{1,0:T(8,128)(2,1)} %bitcast.64, ...), custom_call_target="tpu_custom_call" | custom-call | flops 188959997952 | tf_op jit(solution)/shard_map/feed/pallas_call | solution.py:56
  317.4 22.9 %grad_product.7 = (bf16[512,3072]{1,0:T(8,128)(2,1)}, bf16[512,3072]{1,0:T(8,128)(2,1)}) custom-call(bf16[1024,1024]{1,0:T(8,128)(2,1)} %get-tuple-element.119.refs_0_, bf16[1024,1024]{1,0:T(8,128)(2,1)} %copy-done.19, bf16[1024,1024]{1,0:T(8,128)(2,1)} %get-tuple-element.116.refs_2_.refs_0_, bf16[1024,1024]{1,0:T(8,128)(2,1)} %copy-done.23, ...), custom_call_target="tpu_custom_call" | custom-call | flops 179383992320 | tf_op jit(solution)/shard_map/grad_product/pallas_call | solution.py:56
  344.5 35.8 %feed.3 = (bf16[1024,2048]{1,0:T(8,128)(2,1)}, bf16[1024,2048]{1,0:T(8,128)(2,1)}, bf16[1024,2048]{1,0:T(8,128)(2,1)}) custom-call(bf16[1024,2048]{1,0:T(8,128)(2,1)} %get-tuple-element.113.refs_1_.refs_2_.refs_3_.refs_4_.refs_0_, bf16[1024,2048]{1,0:T(8,128)(2,1)} %bitcast.65, ...), custom_call_target="tpu_custom_call" | custom-call | flops 357920014336 | tf_op jit(solution)/shard_map/feed/pallas_call | solution.py:56
  381.1 20.0 %nt_product.6.refs_4_.refs_2_ = bf16[512,2048]{1,0:T(8,128)(2,1)} custom-call(bf16[1024,1024]{1,0:T(8,128)(2,1)} %get-tuple-element.122.refs_6_.refs_0_, bf16[1024,2048]{1,0:T(8,128)(2,1)} %get-tuple-element.126.refs_1_.refs_2_, bf16[1024,1024]{1,0:T(8,128)(2,1)} %get-tuple-element.123.refs_10_.refs_2_, ...), custom_call_target="tpu_custom_call" | custom-call | flops 203743674368 | tf_op jit(solution)/shard_map/nt_product/pallas_call | solution.py:56
  402.6 13.2 %grad_product.8 = (bf16[512,2048]{1,0:T(8,128)(2,1)}, bf16[512,2048]{1,0:T(8,128)(2,1)}) custom-call(bf16[1024,1024]{1,0:T(8,128)(2,1)} %get-tuple-element.119.refs_0_, bf16[1024,1024]{1,0:T(8,128)(2,1)} %copy-done.19, bf16[1024,2048]{1,0:T(8,128)(2,1)} %get-tuple-element.125.refs_2_.refs_1_, bf16[1024,2048]{1,0:T(8,128)(2,1)} %collective-permute-done.18.refs_3_, ...), custom_call_target="tpu_custom_call" | custom-call | flops 131256000512 | tf_op jit(solution)/shard_map/grad_product/pallas_call | solution.py:56
  417.0 20.2 %nt_product.7.refs_2_ = bf16[512,2048]{1,0:T(8,128)(2,1)} custom-call(bf16[1024,1024]{1,0:T(8,128)(2,1)} %get-tuple-element.122.refs_6_.refs_0_, bf16[1024,2048]{1,0:T(8,128)(2,1)} %get-tuple-element.126.refs_1_.refs_2_, bf16[1024,1024]{1,0:T(8,128)(2,1)} %get-tuple-element.123.refs_10_.refs_2_, bf16[1024,2048]{1,0:T(8,128)(2,1)} %get-tuple-element.127.refs_3_.refs_2_, ...), custom_call_target="tpu_custom_call" | custom-call | flops 203743674368 | tf_op jit(solution)/shard_map/nt_product/pallas_call | solution.py:56
  442.2 13.2 %grad_product.9 = (bf16[512,2048]{1,0:T(8,128)(2,1)}, bf16[512,2048]{1,0:T(8,128)(2,1)}) custom-call(bf16[1024,1024]{1,0:T(8,128)(2,1)} %get-tuple-element.115.refs_5_.refs_4_.refs_8_.refs_0_, bf16[1024,1024]{1,0:T(8,128)(2,1)} %collective-permute-done.15.refs_5_.refs_9_.refs_1_, bf16[1024,2048]{1,0:T(8,128)(2,1)} %get-tuple-element.126.refs_1_.refs_2_, ...), custom_call_target="tpu_custom_call" | custom-call | flops 131256000512 | tf_op jit(solution)/shard_map/grad_product/pallas_call | solution.py:56
  456.2 7.5 norm_back.4
  469.4 11.5 %nt_product.8.refs_11_.refs_1_ = bf16[512,2048]{1,0:T(8,128)(2,1)} custom-call(bf16[1024,1024]{1,0:T(8,128)(2,1)} %get-tuple-element.116.refs_2_.refs_0_, bf16[1024,2048]{1,0:T(8,128)(2,1)} %get-tuple-element.125.refs_2_.refs_1_, bf16[2048,6272]{1,0:T(8,128)(2,1)} %all-gather.3.cloned.1.call-done.refs_1_.refs_4_.refs_2_.refs_3_.refs_6_, ...), custom_call_target="tpu_custom_call" | custom-call | flops 109371842560 | tf_op jit(solution)/shard_map/nt_product/pallas_call | solution.py:56
  482.3 20.5 %attend_back.2 = (bf16[1024,1024]{1,0:T(8,128)(2,1)}, bf16[512,1024]{1,0:T(8,128)(2,1)}, bf16[512,1024]{1,0:T(8,128)(2,1)}, bf16[2,512,1024]{2,1,0:T(8,128)(2,1)}, f32[8,128]{1,0:T(8,128)}) custom-call(bf16[1024,1024]{1,0:T(8,128)(2,1)} %get-tuple-element.104.refs_1_.refs_0_, bf16[512,1024]{1,0:T(8,128)(2,1)} %get-tuple-element.100.refs_2_.refs_1_, ...), custom_call_target="tpu_custom_call" | custom-call | flops 249999998976 | tf_op jit(solution)/shard_map/attend_back/pallas_call | solution.py:56
  504.6 7.5 norm_back.5
  535.5 9.0 %grad_product.10 = (bf16[512,1024]{1,0:T(8,128)(2,1)}, bf16[512,1024]{1,0:T(8,128)(2,1)}) custom-call(bf16[1024,1024]{1,0:T(8,128)(2,1)} %get-tuple-element.138.refs_2_.refs_0_, bf16[1024,1024]{1,0:T(8,128)(2,1)} %copy-done.22, bf16[512,1024]{1,0:T(8,128)(2,1)} %get-tuple-element.106.refs_6_.refs_2_, bf16[512,1024]{1,0:T(8,128)(2,1)} %get-tuple-element.109.refs_2_.refs_3_, ...), custom_call_target="tpu_custom_call" | custom-call | flops 83128000512 | tf_op jit(solution)/shard_map/grad_product/pallas_call | solution.py:56
  545.4 11.4 %nt_product.9.refs_4_.refs_1_ = bf16[512,2048]{1,0:T(8,128)(2,1)} custom-call(bf16[1024,1024]{1,0:T(8,128)(2,1)} %get-tuple-element.116.refs_2_.refs_0_, bf16[1024,2048]{1,0:T(8,128)(2,1)} %get-tuple-element.125.refs_2_.refs_1_, bf16[2048,6272]{1,0:T(8,128)(2,1)} %all-gather.3.cloned.1.call-done.refs_1_.refs_4_.refs_2_.refs_3_.refs_6_, ...), custom_call_target="tpu_custom_call" | custom-call | flops 109371842560 | tf_op jit(solution)/shard_map/nt_product/pallas_call | solution.py:56
  557.3 13.2 %grad_product.11 = (bf16[512,2048]{1,0:T(8,128)(2,1)}, bf16[512,2048]{1,0:T(8,128)(2,1)}) custom-call(bf16[1024,1024]{1,0:T(8,128)(2,1)} %get-tuple-element.115.refs_5_.refs_4_.refs_8_.refs_0_, bf16[1024,1024]{1,0:T(8,128)(2,1)} %collective-permute-done.15.refs_5_.refs_9_.refs_1_, bf16[1024,2048]{1,0:T(8,128)(2,1)} %get-tuple-element.127.refs_3_.refs_2_, ...), custom_call_target="tpu_custom_call" | custom-call | flops 131256000512 | tf_op jit(solution)/shard_map/grad_product/pallas_call | solution.py:56
  578.6 8.9 %nt_product.10.refs_12_.refs_1_.refs_2_ = bf16[512,2048]{1,0:T(8,128)(2,1)} custom-call(bf16[1024,1024]{1,0:T(8,128)(2,1)} %get-tuple-element.145.refs_0_.refs_11_, bf16[1024,1024]{1,0:T(8,128)(2,1)} %get-tuple-element.148.refs_1_.refs_7_, bf16[2048,6272]{1,0:T(8,128)(2,1)} %all-gather.3.cloned.1.call-done.refs_1_.refs_4_.refs_2_.refs_3_.refs_6_, ...), custom_call_target="tpu_custom_call" | custom-call | flops 77914562560 | tf_op jit(solution)/shard_map/nt_product/pallas_call | solution.py:56
  588.9 20.5 %attend_back.3 = (bf16[1024,1024]{1,0:T(8,128)(2,1)}, bf16[512,1024]{1,0:T(8,128)(2,1)}, bf16[512,1024]{1,0:T(8,128)(2,1)}, bf16[2,512,1024]{2,1,0:T(8,128)(2,1)}, f32[8,128]{1,0:T(8,128)}) custom-call(bf16[1024,1024]{1,0:T(8,128)(2,1)} %get-tuple-element.104.refs_1_.refs_0_, ...), custom_call_target="tpu_custom_call", output_to_operand_aliasing={{0}: (11, {})} | custom-call | flops 249999998976 | tf_op jit(solution)/shard_map/attend_back/pallas_call | solution.py:56
  621.9 8.4 %grad_product.12 = (bf16[512,1024]{1,0:T(8,128)(2,1)}, bf16[512,1024]{1,0:T(8,128)(2,1)}) custom-call(bf16[1024,1024]{1,0:T(8,128)(2,1)} %get-tuple-element.103.refs_5_.refs_0_, bf16[1024,1024]{1,0:T(8,128)(2,1)} %collective-permute-done.13.refs_7_.refs_1_, bf16[1024,1024]{1,0:T(8,128)(2,1)} %get-tuple-element.151.refs_2_.refs_0_, ...), custom_call_target="tpu_custom_call" | custom-call | flops 83128000512 | tf_op jit(solution)/shard_map/grad_product/pallas_call | solution.py:56
  651.2 8.9 %nt_product.11.refs_4_.refs_1_.refs_2_ = bf16[512,2048]{1,0:T(8,128)(2,1)} custom-call(bf16[1024,1024]{1,0:T(8,128)(2,1)} %get-tuple-element.151.refs_2_.refs_0_, bf16[1024,1024]{1,0:T(8,128)(2,1)} %get-tuple-element.158.refs_1_.refs_2_, bf16[2048,6272]{1,0:T(8,128)(2,1)} %all-gather.3.cloned.1.call-done.refs_1_.refs_4_.refs_2_.refs_3_.refs_6_, ...), custom_call_target="tpu_custom_call" | custom-call | flops 77914562560 | tf_op jit(solution)/shard_map/nt_product/pallas_call | solution.py:56
  667.5 8.5 %grad_product.13 = (bf16[512,1024]{1,0:T(8,128)(2,1)}, bf16[512,1024]{1,0:T(8,128)(2,1)}) custom-call(bf16[1024,1024]{1,0:T(8,128)(2,1)} %get-tuple-element.103.refs_5_.refs_0_, bf16[1024,1024]{1,0:T(8,128)(2,1)} %collective-permute-done.13.refs_7_.refs_1_, bf16[1024,1024]{1,0:T(8,128)(2,1)} %get-tuple-element.158.refs_1_.refs_2_, ...), custom_call_target="tpu_custom_call" | custom-call | flops 83128000512 | tf_op jit(solution)/shard_map/grad_product/pallas_call | solution.py:56
  677.2 7.5 norm_back.6
  686.7 14.6 %collective-permute-done.40.refs_3_ = bf16[512,1024]{1,0:T(8,128)(2,1)S(1)} collective-permute-done((bf16[512,1024]{1,0:T(8,128)(2,1)}, bf16[512,1024]{1,0:T(8,128)(2,1)S(1)}, u32[]{:S(2)}, u32[]{:S(2)}) %collective-permute-start.40) | collective-permute-done | bytes 1048608 | tf_op jit(solution)/shard_map/key_over_x/ppermute | solution.py:823
  715.1 7.5 norm_back.7
  726.9 28.9 %reduce-scatter.10.cloned.1.call-done = bf16[128,2048]{1,0:T(8,128)(2,1)} async-done(((bf16[512,2048]{1,0:T(8,128)(2,1)}), bf16[128,2048]{1,0:T(8,128)(2,1)}) %reduce-scatter.10.cloned.1.call-update) | async-done | bytes 524304 | tf_op jit(solution)/shard_map/query_key_over_dp/reduce_scatter | solution.py:946
  (246 shorter events, 208.7 us)
Async XLA Ops:
  7.2 138.7 %all-gather.3.cloned.1.call-start = ((), (), s32[]{:S(2)}) async-start(), calls=%async_computation.6 | async-start | bytes 27295744 | tf_op jit(solution)/shard_map/all_gather | solution.py:840
  12.0 332.6 %all-gather.5.cloned.1.call-start = ((), (), s32[]{:S(2)}) async-start(), calls=%async_computation.7 | async-start | bytes 26738688 | tf_op jit(solution)/shard_map/all_gather | solution.py:910
  161.1 25.6 %collective-permute-start.2 = (bf16[512,1024]{1,0:T(8,128)(2,1)}, bf16[512,1024]{1,0:T(8,128)(2,1)}, u32[]{:S(2)}, u32[]{:S(2)}) collective-permute-start(bf16[512,1024]{1,0:T(8,128)(2,1)} %get-tuple-element.100.refs_2_.refs_1_), channel_id=1, source_target_pairs={{0,4},{4,0},{2,6},{6,2},{1,5},{5,1},{3,7},{7,3},{8,12},{12,8},{10,... | collective-permute-start | bytes 3145736 | tf_op jit(solution)/shard_map/kv0_over_x/ppermute | solution.py:823
  162.3 25.6 %collective-permute-start.1 = (bf16[512,1024]{1,0:T(8,128)(2,1)}, bf16[512,1024]{1,0:T(8,128)(2,1)}, u32[]{:S(2)}, u32[]{:S(2)}) collective-permute-start(bf16[512,1024]{1,0:T(8,128)(2,1)} %get-tuple-element.100.refs_2_.refs_1_), channel_id=1, source_target_pairs={{0,2},{2,0},{4,6},{6,4},{1,3},{3,1},{5,7},{7,5},{8,10},{10,8},{12,... | collective-permute-start | bytes 3145736 | tf_op jit(solution)/shard_map/kv0_over_core/ppermute | solution.py:823
  165.4 48.4 %collective-permute-start.7 = (bf16[1024,1024]{1,0:T(8,128)(2,1)}, bf16[1024,1024]{1,0:T(8,128)(2,1)}, u32[]{:S(2)}, u32[]{:S(2)}) collective-permute-start(bf16[1024,1024]{1,0:T(8,128)(2,1)} %constant_dynamic-slice_fusion.refs_5_), channel_id=1, source_target_pairs={{0,1},{1,0},{2,3},{3,2},{4,5},{5,4},{6,7},{7,6},{8,9},{9,8},{10,11... | collective-permute-start | bytes 6291464 | tf_op jit(solution)/shard_map/output_proj_over_tp/ppermute | solution.py:823
  186.7 27.0 %collective-permute-start.4 = (bf16[512,1024]{1,0:T(8,128)(2,1)}, bf16[512,1024]{1,0:T(8,128)(2,1)}, u32[]{:S(2)}, u32[]{:S(2)}) collective-permute-start(bf16[512,1024]{1,0:T(8,128)(2,1)} %get-tuple-element.105.refs_5_.refs_2_.refs_1_), channel_id=1, source_target_pairs={{0,4},{4,0},{2,6},{6,2},{1,5},{5,1},{3,7},{7,3},{8,12},{12,8},{10,... | collective-permute-start | bytes 3145736 | tf_op jit(solution)/shard_map/kv1_over_x/ppermute | solution.py:823
  214.4 62.5 %collective-permute-start.13 = (bf16[1024,1024]{1,0:T(8,128)(2,1)}, bf16[1024,1024]{1,0:T(8,128)(2,1)}, u32[]{:S(2)}, u32[]{:S(2)}) collective-permute-start(bf16[1024,1024]{1,0:T(8,128)(2,1)} %get-tuple-element.114), channel_id=1, source_target_pairs={{0,2},{2,0},{4,6},{6,4},{1,3},{3,1},{5,7},{7,5},{8,10},{10,8},{12,... | collective-permute-start | bytes 6291464 | tf_op jit(solution)/shard_map/normed_one_over_core/ppermute | solution.py:823
  214.8 62.1 %collective-permute-start.11 = (bf16[512,1024]{1,0:T(8,128)(2,1)}, bf16[512,1024]{1,0:T(8,128)(2,1)}, u32[]{:S(2)}, u32[]{:S(2)}) collective-permute-start(bf16[512,1024]{1,0:T(8,128)(2,1)} %get-tuple-element.106.refs_6_.refs_2_), channel_id=1, source_target_pairs={{0,2},{2,0},{4,6},{6,4},{1,3},{3,1},{5,7},{7,5},{8,10},{10,8},{12,... | collective-permute-start | bytes 3145736 | tf_op jit(solution)/shard_map/attended_over_core/ppermute | solution.py:823
  214.9 26.0 %collective-permute-start.10 = (bf16[512,1024]{1,0:T(8,128)(2,1)}, bf16[512,1024]{1,0:T(8,128)(2,1)}, u32[]{:S(2)}, u32[]{:S(2)}) collective-permute-start(bf16[512,1024]{1,0:T(8,128)(2,1)} %get-tuple-element.106.refs_6_.refs_2_), channel_id=1, source_target_pairs={{0,1},{1,0},{2,3},{3,2},{4,5},{5,4},{6,7},{7,6},{8,9},{9,8},{10,11... | collective-permute-start | bytes 3145736 | tf_op jit(solution)/shard_map/attended0_over_tp/ppermute | solution.py:823
  216.4 312.5 %reduce-scatter.6.cloned.1.call-start = ((), (), s32[]{:S(2)}) async-start(), calls=%async_computation.8 | async-start | bytes 3932160 | tf_op jit(solution)/shard_map/first_third_over_dp/reduce_scatter | solution.py:946
  237.1 39.8 %collective-permute-start.12 = (bf16[512,1024]{1,0:T(8,128)(2,1)}, bf16[512,1024]{1,0:T(8,128)(2,1)}, u32[]{:S(2)}, u32[]{:S(2)}) collective-permute-start(bf16[512,1024]{1,0:T(8,128)(2,1)} %get-tuple-element.109.refs_2_.refs_3_), channel_id=1, source_target_pairs={{0,2},{2,0},{4,6},{6,4},{1,3},{3,1},{5,7},{7,5},{8,10},{10,8},{12,... | collective-permute-start | bytes 3145736 | tf_op jit(solution)/shard_map/attended_over_core/ppermute | solution.py:823
  237.5 25.8 %collective-permute-start.9 = (bf16[512,1024]{1,0:T(8,128)(2,1)}, bf16[512,1024]{1,0:T(8,128)(2,1)}, u32[]{:S(2)}, u32[]{:S(2)}) collective-permute-start(bf16[512,1024]{1,0:T(8,128)(2,1)} %get-tuple-element.109.refs_2_.refs_3_), channel_id=1, source_target_pairs={{0,1},{1,0},{2,3},{3,2},{4,5},{5,4},{6,7},{7,6},{8,9},{9,8},{10,11... | collective-permute-start | bytes 3145736 | tf_op jit(solution)/shard_map/attended1_over_tp/ppermute | solution.py:823
  340.3 97.5 %collective-permute-start.23 = (bf16[512,3072]{1,0:T(8,128)(2,1)}, bf16[512,3072]{1,0:T(8,128)(2,1)}, u32[]{:S(2)}, u32[]{:S(2)}) collective-permute-start(bf16[512,3072]{1,0:T(8,128)(2,1)} %get-tuple-element.129), channel_id=1, source_target_pairs={{0,4},{4,0},{2,6},{6,2},{1,5},{5,1},{3,7},{7,3},{8,12},{12,8},{10,... | collective-permute-start | bytes 9437192 | tf_op jit(solution)/shard_map/first_third_over_x/ppermute | solution.py:823
  380.6 36.4 %collective-permute-start.19 = (bf16[1024,2048]{1,0:T(8,128)(2,1)}, bf16[1024,2048]{1,0:T(8,128)(2,1)}, u32[]{:S(2)}, u32[]{:S(2)}) collective-permute-start(bf16[1024,2048]{1,0:T(8,128)(2,1)} %get-tuple-element.126.refs_1_.refs_2_), channel_id=1, source_target_pairs={{0,2},{2,0},{4,6},{6,4},{1,3},{3,1},{5,7},{7,5},{8,10},{10,8},{12,... | collective-permute-start | bytes 12582920 | tf_op jit(solution)/shard_map/gate_back_two_over_core/ppermute | solution.py:823
  380.8 36.1 %collective-permute-start.20 = (bf16[1024,2048]{1,0:T(8,128)(2,1)}, bf16[1024,2048]{1,0:T(8,128)(2,1)}, u32[]{:S(2)}, u32[]{:S(2)}) collective-permute-start(bf16[1024,2048]{1,0:T(8,128)(2,1)} %get-tuple-element.127.refs_3_.refs_2_), channel_id=1, source_target_pairs={{0,2},{2,0},{4,6},{6,4},{1,3},{3,1},{5,7},{7,5},{8,10},{10,8},{12,... | collective-permute-start | bytes 12582920 | tf_op jit(solution)/shard_map/up_back_two_over_core/ppermute | solution.py:823
  401.1 55.1 %collective-permute-start.22 = (bf16[512,2048]{1,0:T(8,128)(2,1)}, bf16[512,2048]{1,0:T(8,128)(2,1)}, u32[]{:S(2)}, u32[]{:S(2)}) collective-permute-start(bf16[512,2048]{1,0:T(8,128)(2,1)} %nt_product.6.refs_4_.refs_2_), channel_id=1, source_target_pairs={{0,1},{1,0},{2,3},{3,2},{4,5},{5,4},{6,7},{7,6},{8,9},{9,8},{10,11... | collective-permute-start | bytes 6291464 | tf_op jit(solution)/shard_map/back0_over_tp/ppermute | solution.py:823
  415.8 113.1 %collective-permute-start.26 = (bf16[512,2048]{1,0:T(8,128)(2,1)}, bf16[512,2048]{1,0:T(8,128)(2,1)}, u32[]{:S(2)}, u32[]{:S(2)}) collective-permute-start(bf16[512,2048]{1,0:T(8,128)(2,1)} %get-tuple-element.140), channel_id=1, source_target_pairs={{0,4},{4,0},{2,6},{6,2},{1,5},{5,1},{3,7},{7,3},{8,12},{12,8},{10,... | collective-permute-start | bytes 6291464 | tf_op jit(solution)/shard_map/down_two_over_x/ppermute | solution.py:823
  437.2 67.5 %collective-permute-start.21 = (bf16[512,2048]{1,0:T(8,128)(2,1)}, bf16[512,2048]{1,0:T(8,128)(2,1)}, u32[]{:S(2)}, u32[]{:S(2)}) collective-permute-start(bf16[512,2048]{1,0:T(8,128)(2,1)} %nt_product.7.refs_2_), channel_id=1, source_target_pairs={{0,1},{1,0},{2,3},{3,2},{4,5},{5,4},{6,7},{7,6},{8,9},{9,8},{10,11... | collective-permute-start | bytes 6291464 | tf_op jit(solution)/shard_map/back1_over_tp/ppermute | solution.py:823
  442.2 194.1 %reduce-scatter.8.cloned.1.call-start = ((), (), s32[]{:S(2)}) async-start(), calls=%async_computation.9 | async-start | bytes 5242880 | tf_op jit(solution)/shard_map/down_gate_two_over_dp/reduce_scatter | solution.py:946
  455.4 62.3 %collective-permute-start.24 = (bf16[512,2048]{1,0:T(8,128)(2,1)}, bf16[512,2048]{1,0:T(8,128)(2,1)}, u32[]{:S(2)}, u32[]{:S(2)}) collective-permute-start(bf16[512,2048]{1,0:T(8,128)(2,1)} %get-tuple-element.137), channel_id=1, source_target_pairs={{0,4},{4,0},{2,6},{6,2},{1,5},{5,1},{3,7},{7,3},{8,12},{12,8},{10,... | collective-permute-start | bytes 6291464 | tf_op jit(solution)/shard_map/gate_two_over_x/ppermute | solution.py:823
  480.8 76.5 %collective-permute-start.29 = (bf16[512,2048]{1,0:T(8,128)(2,1)}, bf16[512,2048]{1,0:T(8,128)(2,1)}, u32[]{:S(2)}, u32[]{:S(2)}) collective-permute-start(bf16[512,2048]{1,0:T(8,128)(2,1)} %nt_product.8.refs_11_.refs_1_), channel_id=1, source_target_pairs={{0,1},{1,0},{2,3},{3,2},{4,5},{5,4},{6,7},{7,6},{8,9},{9,8},{10,11... | collective-permute-start | bytes 6291464 | tf_op jit(solution)/shard_map/out0_over_tp/ppermute | solution.py:823
  527.1 43.4 %collective-permute-start.30 = (bf16[512,1024]{1,0:T(8,128)(2,1)}, bf16[512,1024]{1,0:T(8,128)(2,1)}, u32[]{:S(2)}, u32[]{:S(2)}) collective-permute-start(bf16[512,1024]{1,0:T(8,128)(2,1)} %add_rows.8.refs_4_), channel_id=1, source_target_pairs={{0,4},{4,0},{2,6},{6,2},{1,5},{5,1},{3,7},{7,3},{8,12},{12,8},{10,... | collective-permute-start | bytes 3145736 | tf_op jit(solution)/shard_map/kv_grad0_over_x/ppermute | solution.py:823
  534.1 150.6 %reduce-scatter.12.cloned.1.call-start = ((), (), s32[]{:S(2)}) async-start(), calls=%async_computation.11 | async-start | bytes 1310720 | tf_op jit(solution)/shard_map/output_over_dp/reduce_scatter | solution.py:946
  544.5 34.0 %collective-permute-start.31 = (bf16[512,1024]{1,0:T(8,128)(2,1)}, bf16[512,1024]{1,0:T(8,128)(2,1)}, u32[]{:S(2)}, u32[]{:S(2)}) collective-permute-start(bf16[512,1024]{1,0:T(8,128)(2,1)} %get-tuple-element.149), channel_id=1, source_target_pairs={{0,4},{4,0},{2,6},{6,2},{1,5},{5,1},{3,7},{7,3},{8,12},{12,8},{10,... | collective-permute-start | bytes 3145736 | tf_op jit(solution)/shard_map/output_over_x/ppermute | solution.py:823
  556.8 74.8 %collective-permute-start.28 = (bf16[512,2048]{1,0:T(8,128)(2,1)}, bf16[512,2048]{1,0:T(8,128)(2,1)}, u32[]{:S(2)}, u32[]{:S(2)}) collective-permute-start(bf16[512,2048]{1,0:T(8,128)(2,1)} %nt_product.9.refs_4_.refs_1_), channel_id=1, source_target_pairs={{0,1},{1,0},{2,3},{3,2},{4,5},{5,4},{6,7},{7,6},{8,9},{9,8},{10,11... | collective-permute-start | bytes 6291464 | tf_op jit(solution)/shard_map/out1_over_tp/ppermute | solution.py:823
  576.5 62.3 %collective-permute-start.35 = (bf16[512,2048]{1,0:T(8,128)(2,1)}, bf16[512,2048]{1,0:T(8,128)(2,1)}, u32[]{:S(2)}, u32[]{:S(2)}) collective-permute-start(bf16[512,2048]{1,0:T(8,128)(2,1)} %get-tuple-element.157), channel_id=1, source_target_pairs={{0,4},{4,0},{2,6},{6,2},{1,5},{5,1},{3,7},{7,3},{8,12},{12,8},{10,... | collective-permute-start | bytes 6291464 | tf_op jit(solution)/shard_map/up_two_over_x/ppermute | solution.py:823
  587.4 89.8 %collective-permute-start.37 = (bf16[512,2048]{1,0:T(8,128)(2,1)}, bf16[512,2048]{1,0:T(8,128)(2,1)}, u32[]{:S(2)}, u32[]{:S(2)}) collective-permute-start(bf16[512,2048]{1,0:T(8,128)(2,1)} %nt_product.10.refs_12_.refs_1_.refs_2_), channel_id=1, source_target_pairs={{0,1},{1,0},{2,3},{3,2},{4,5},{5,4},{6,7},{7,6},{8,9},{9,8},{10,11... | collective-permute-start | bytes 6291464 | tf_op jit(solution)/shard_map/one0_over_tp/ppermute | solution.py:823
  619.8 26.9 %collective-permute-start.34 = (bf16[512,1024]{1,0:T(8,128)(2,1)}, bf16[512,1024]{1,0:T(8,128)(2,1)}, u32[]{:S(2)}, u32[]{:S(2)}) collective-permute-start(bf16[512,1024]{1,0:T(8,128)(2,1)} %add_rows.10.refs_4_), channel_id=1, source_target_pairs={{0,4},{4,0},{2,6},{6,2},{1,5},{5,1},{3,7},{7,3},{8,12},{12,8},{10,... | collective-permute-start | bytes 3145736 | tf_op jit(solution)/shard_map/kv_grad1_over_x/ppermute | solution.py:823
  630.3 47.0 %collective-permute-start.39 = (bf16[512,1024]{1,0:T(8,128)(2,1)}, bf16[512,1024]{1,0:T(8,128)(2,1)}, u32[]{:S(2)}, u32[]{:S(2)}) collective-permute-start(bf16[512,1024]{1,0:T(8,128)(2,1)} %get-tuple-element.160), channel_id=1, source_target_pairs={{0,4},{4,0},{2,6},{6,2},{1,5},{5,1},{3,7},{7,3},{8,12},{12,8},{10,... | collective-permute-start | bytes 3145736 | tf_op jit(solution)/shard_map/query_over_x/ppermute | solution.py:823
  638.7 85.8 %reduce-scatter.14.cloned.1.call-start = ((), (), s32[]{:S(2)}) async-start(), calls=%async_computation.12 | async-start | bytes 2621440 | tf_op jit(solution)/shard_map/up_two_over_dp/reduce_scatter | solution.py:946
  662.9 92.9 %reduce-scatter.10.cloned.1.call-start = ((), (), s32[]{:S(2)}) async-start(), calls=%async_computation.10 | async-start | bytes 2621440 | tf_op jit(solution)/shard_map/query_key_over_dp/reduce_scatter | solution.py:946
  663.7 51.4 %collective-permute-start.36 = (bf16[512,2048]{1,0:T(8,128)(2,1)}, bf16[512,2048]{1,0:T(8,128)(2,1)}, u32[]{:S(2)}, u32[]{:S(2)}) collective-permute-start(bf16[512,2048]{1,0:T(8,128)(2,1)} %nt_product.11.refs_4_.refs_1_.refs_2_), channel_id=1, source_target_pairs={{0,1},{1,0},{2,3},{3,2},{4,5},{5,4},{6,7},{7,6},{8,9},{9,8},{10,11... | collective-permute-start | bytes 6291464 | tf_op jit(solution)/shard_map/one1_over_tp/ppermute | solution.py:823
  (48 other events, 462.0 us)
Sparse Core Ops, SparseCore 0:
  12.1 133.7 all-gather.2
  216.6 127.9 all-gather.4
  442.3 60.5 reduce-scatter.5
  534.3 75.9 reduce-scatter.7
  638.8 26.5 reduce-scatter.11
  667.6 42.5 reduce-scatter.13
  712.5 43.1 reduce-scatter.9

commit v5 on v4

--- a/solution.py
+++ b/solution.py
@@ -952,13 +952,13 @@
     starts = [3 * columns + at * third for at in range(3)]
     settled = (*attended_pair[1], one_turned[1])
     two_turned = turned(feed_two, "normed_two", after=settled)
-    acts = feed(feed_two, cot_rows, weights, starts, tile, third, 1, after=(two_turned[0],))
+    acts = feed(feed_two, cot_rows, weights, starts, min(256, third), third, 1, after=(two_turned[0],))
     firsts = [([a[0]], [core_swap(a[0], n + "_one")]) for a, n in zip(acts, names)]
     parts = [(cot_turned, firsts[0]), (two_turned, firsts[1]), (two_turned, firsts[2])]
     first_third = Gradient("first_third", parts)
     starts = [at * 2 * third for at in range(3)]
     acts = feed(
-        feed_two, cot_rows, weights_two, starts, tile, 2 * third, 1, after=(first_third.keep,)
+        feed_two, cot_rows, weights_two, starts, min(256, third), 2 * third, 1, after=(first_third.keep,)
     )
     seconds = [([a[0]], [core_swap(a[0], n + "_two")]) for a, n in zip(acts, names)]
 
@@ -1039,10 +1039,10 @@
     outputs = sum_rows(middle, out_started[0], 0, None, after=(held[0],))
     sent = send_keys(1, held, (outputs,))
     query_grad = Gradient("query", [(one_turned, q_pair)], after=(sent,))
-    outputs = sum_rows(middle, out_started[1], half_rows, outputs, after=(query_grad.keep,))
-    done, output_out = over_dp("output", [output_grad], after=(outputs, more_out))
+    done, output_out = over_dp("output", [output_grad], after=(query_grad.keep, more_out))
     done, up_out = over_dp("up_two", [up_two], after=(done,))
-    terms = gain_terms(input_rows, one[0][0], 0, after=(done,))
+    outputs = sum_rows(middle, out_started[1], half_rows, outputs, after=(done,))
+    terms = gain_terms(input_rows, one[0][0], 0, after=(outputs,))
     k_back = key_half(1, (terms,))
     part = one_half(1, ())
     k_pair = [k_back], [core_swap(k_back, "key_back")]

time: 774 us -> 771 us (level)
  transfers between devices with their start and end apart: 49 -> 49, of which waited for: 12 -> 14; matrix products, arithmetic and copies ran while one was open for 3% -> 3% of each run, Pallas kernels for 60% -> 60%
where the time goes in v5:
time: 771 us; the launch traced here: 763 us
  Pallas kernels  473 us (61%)
  waiting for transfers between devices  194 us (25%)
  starting transfers between devices  33.5 us (4%)
  local copies, waits for them, and re-layouts  29.2 us (4%)
  other arithmetic  18.2 us (2%)
  between operations  14.8 us (2%)
    pallas_call x50, Pallas kernels, call(): pl.pallas_call(body, grid_spec=pltpu.PrefetchScalarGridSpec(num_scalar_pr...  473 us
    all_gather x1, waiting for transfers between devices, shards(): weights = lax.all_gather(shard_one, ('dp', 'ctx'), axis=0, tiled=True)  115 us
    ppermute x41, waiting for transfers between devices, swap(): return lax.ppermute(value, axis, pairs)  47.2 us
    ppermute x41, starting transfers between devices, swap(): return lax.ppermute(value, axis, pairs)  28.8 us
    reduce_scatter x5, waiting for transfers between devices, over_dp(): lax.psum_scatter(summed, 'dp', scatter_dimension=0, tiled=True)  26.9 us
    unnamed x66, local copies, waits for them, and re-layouts  16.4 us
  transfers between devices with their start and end apart: 49, of which 14 were waited for; matrix products, arithmetic and copies ran while one was open for 3% of the time, Pallas kernels for 60%

profile of v5, /device:TPU:0, one launch (start us, length us, event | category | flops | bytes accessed | tf_op | source)
XLA Modules:
  0.0 763.3 jit_solution(433386267080493208)
XLA Ops:
  30.7 115.1 %all-gather.3.cloned.1.call-done.refs_1_.refs_4_.refs_2_.refs_3_.refs_6_ = bf16[2048,6272]{1,0:T(8,128)(2,1)} async-done(((bf16[128,6272]{1,0:T(8,128)(2,1)}), bf16[2048,6272]{1,0:T(8,128)(2,1)}) %all-gather.3.cloned.1.call-update) | async-done | bytes 25690128 | tf_op jit(solution)/shard_map/all_gather | solution.py:840
  154.2 6.8 project.3
  166.8 6.8 project.4
  188.9 9.9 %project.5 = (bf16[1024,1024]{1,0:T(8,128)(2,1)}, f32[1024,1024]{1,0:T(8,128)}) custom-call(bf16[1024,2048]{1,0:T(8,128)(2,1)} %norm_rows.1.refs_0_.refs_1_.refs_2_.refs_3_.refs_4_, bf16[2048,6272]{1,0:T(8,128)(2,1)} %all-gather.3.cloned.1.call-done.refs_1_.refs_4_.refs_2_.refs_3_.refs_6_, f32[1024,128]{1,0:T(8,128)} %get-tuple-element.97.refs_2_.refs_8_.refs_4_, ...), custom_call_target="tpu_custom_call" | custom-call | flops 99999997952 | tf_op jit(solution)/shard_map/project/pallas_call | solution.py:56
  199.8 13.6 %attend.2 = (bf16[512,1024]{1,0:T(8,128)(2,1)}, bf16[2,2048,1024]{2,1,0:T(8,128)(2,1)}) custom-call(s32[4,8]{1,0:T(4,128)} %copy-done.14, bf16[1024,1024]{1,0:T(8,128)(2,1)} %get-tuple-element.104.refs_1_.refs_0_, bf16[512,1024]{1,0:T(8,128)(2,1)} %get-tuple-element.100.refs_2_.refs_1_, bf16[512,1024]{1,0:T(8,128)(2,1)} %collective-permute-done.1.refs_6_.refs_3_.refs_2_, ...), custom_call_target="tpu_custom_call" | custom-call | flops 109999996928 | tf_op jit(solution)/shard_map/attend/pallas_call | solution.py:56
  223.4 13.5 %attend.3 = (bf16[512,1024]{1,0:T(8,128)(2,1)}, bf16[2,2048,1024]{2,1,0:T(8,128)(2,1)}) custom-call(s32[4,8]{1,0:T(4,128)} %copy-done.14, bf16[1024,1024]{1,0:T(8,128)(2,1)} %get-tuple-element.104.refs_1_.refs_0_, bf16[512,1024]{1,0:T(8,128)(2,1)} %get-tuple-element.105.refs_5_.refs_2_.refs_1_, bf16[512,1024]{1,0:T(8,128)(2,1)} %copy-done.27, ...), custom_call_target="tpu_custom_call" | custom-call | flops 109999996928 | tf_op jit(solution)/shard_map/attend/pallas_call | solution.py:56
  240.5 13.9 %output_join.2 = (f32[1024,2048]{1,0:T(8,128)}, bf16[1024,2048]{1,0:T(8,128)(2,1)}) custom-call(s32[2]{0:T(128)} %pad_add_fusion.1.refs_0_, bf16[1024,2048]{1,0:T(8,128)(2,1)} %bitcast.69, bf16[512,1024]{1,0:T(8,128)(2,1)} %get-tuple-element.106.refs_6_.refs_2_, bf16[512,1024]{1,0:T(8,128)(2,1)} %collective-permute-done.10.refs_3_, ...), custom_call_target="tpu_custom_call" | custom-call | flops 149999992832 | tf_op jit(solution)/shard_map/output_join/pallas_call | solution.py:56
  254.4 8.5 %collective-permute-done.9.refs_3_ = bf16[512,1024]{1,0:T(8,128)(2,1)} collective-permute-done((bf16[512,1024]{1,0:T(8,128)(2,1)}, bf16[512,1024]{1,0:T(8,128)(2,1)}, u32[]{:S(2)}, u32[]{:S(2)}) %collective-permute-start.9) | collective-permute-done | bytes 1048608 | tf_op jit(solution)/shard_map/attended1_over_tp/ppermute | solution.py:823
  262.9 13.7 %output_join.3 = (f32[1024,2048]{1,0:T(8,128)}, bf16[1024,2048]{1,0:T(8,128)(2,1)}) custom-call(s32[2]{0:T(128)} %pad_add_fusion.1.refs_0_, bf16[1024,2048]{1,0:T(8,128)(2,1)} %bitcast.70, bf16[512,1024]{1,0:T(8,128)(2,1)} %get-tuple-element.109.refs_2_.refs_3_, ...), custom_call_target="tpu_custom_call", output_to_operand_aliasing={{0}: (8, {}), {1}: (9, {})} | custom-call | flops 149999992832 | tf_op jit(solution)/shard_map/output_join/pallas_call | solution.py:56
  283.0 20.5 %feed.2 = (bf16[1024,1024]{1,0:T(8,128)(2,1)}, bf16[1024,1024]{1,0:T(8,128)(2,1)}, bf16[1024,1024]{1,0:T(8,128)(2,1)}) custom-call(bf16[1024,2048]{1,0:T(8,128)(2,1)} %get-tuple-element.113.refs_1_.refs_2_.refs_3_.refs_4_.refs_0_, bf16[1024,2048]{1,0:T(8,128)(2,1)} %bitcast.64, ...), custom_call_target="tpu_custom_call" | custom-call | flops 188959997952 | tf_op jit(solution)/shard_map/feed/pallas_call | solution.py:56
  316.3 22.8 %grad_product.7 = (bf16[512,3072]{1,0:T(8,128)(2,1)}, bf16[512,3072]{1,0:T(8,128)(2,1)}) custom-call(bf16[1024,1024]{1,0:T(8,128)(2,1)} %get-tuple-element.119.refs_0_, bf16[1024,1024]{1,0:T(8,128)(2,1)} %copy-done.19, bf16[1024,1024]{1,0:T(8,128)(2,1)} %get-tuple-element.116.refs_2_.refs_0_, bf16[1024,1024]{1,0:T(8,128)(2,1)} %copy-done.23, ...), custom_call_target="tpu_custom_call" | custom-call | flops 179383992320 | tf_op jit(solution)/shard_map/grad_product/pallas_call | solution.py:56
  344.3 34.1 %feed.3 = (bf16[1024,2048]{1,0:T(8,128)(2,1)}, bf16[1024,2048]{1,0:T(8,128)(2,1)}, bf16[1024,2048]{1,0:T(8,128)(2,1)}) custom-call(bf16[1024,2048]{1,0:T(8,128)(2,1)} %get-tuple-element.113.refs_1_.refs_2_.refs_3_.refs_4_.refs_0_, bf16[1024,2048]{1,0:T(8,128)(2,1)} %bitcast.65, ...), custom_call_target="tpu_custom_call" | custom-call | flops 357920014336 | tf_op jit(solution)/shard_map/feed/pallas_call | solution.py:56
  379.2 20.2 %nt_product.6.refs_4_.refs_2_ = bf16[512,2048]{1,0:T(8,128)(2,1)} custom-call(bf16[1024,1024]{1,0:T(8,128)(2,1)} %get-tuple-element.122.refs_6_.refs_0_, bf16[1024,2048]{1,0:T(8,128)(2,1)} %get-tuple-element.126.refs_1_.refs_2_, bf16[1024,1024]{1,0:T(8,128)(2,1)} %get-tuple-element.123.refs_10_.refs_2_, ...), custom_call_target="tpu_custom_call" | custom-call | flops 203743674368 | tf_op jit(solution)/shard_map/nt_product/pallas_call | solution.py:56
  400.9 13.2 %grad_product.8 = (bf16[512,2048]{1,0:T(8,128)(2,1)}, bf16[512,2048]{1,0:T(8,128)(2,1)}) custom-call(bf16[1024,1024]{1,0:T(8,128)(2,1)} %get-tuple-element.119.refs_0_, bf16[1024,1024]{1,0:T(8,128)(2,1)} %copy-done.19, bf16[1024,2048]{1,0:T(8,128)(2,1)} %get-tuple-element.125.refs_2_.refs_1_, bf16[1024,2048]{1,0:T(8,128)(2,1)} %collective-permute-done.18.refs_3_, ...), custom_call_target="tpu_custom_call" | custom-call | flops 131256000512 | tf_op jit(solution)/shard_map/grad_product/pallas_call | solution.py:56
  415.3 20.0 %nt_product.7.refs_2_ = bf16[512,2048]{1,0:T(8,128)(2,1)} custom-call(bf16[1024,1024]{1,0:T(8,128)(2,1)} %get-tuple-element.122.refs_6_.refs_0_, bf16[1024,2048]{1,0:T(8,128)(2,1)} %get-tuple-element.126.refs_1_.refs_2_, bf16[1024,1024]{1,0:T(8,128)(2,1)} %get-tuple-element.123.refs_10_.refs_2_, bf16[1024,2048]{1,0:T(8,128)(2,1)} %get-tuple-element.127.refs_3_.refs_2_, ...), custom_call_target="tpu_custom_call" | custom-call | flops 203743674368 | tf_op jit(solution)/shard_map/nt_product/pallas_call | solution.py:56
  440.3 13.2 %grad_product.9 = (bf16[512,2048]{1,0:T(8,128)(2,1)}, bf16[512,2048]{1,0:T(8,128)(2,1)}) custom-call(bf16[1024,1024]{1,0:T(8,128)(2,1)} %get-tuple-element.115.refs_5_.refs_4_.refs_8_.refs_0_, bf16[1024,1024]{1,0:T(8,128)(2,1)} %collective-permute-done.15.refs_5_.refs_9_.refs_1_, bf16[1024,2048]{1,0:T(8,128)(2,1)} %get-tuple-element.126.refs_1_.refs_2_, ...), custom_call_target="tpu_custom_call" | custom-call | flops 131256000512 | tf_op jit(solution)/shard_map/grad_product/pallas_call | solution.py:56
  454.3 7.5 norm_back.4
  467.4 11.5 %nt_product.8.refs_11_.refs_1_ = bf16[512,2048]{1,0:T(8,128)(2,1)} custom-call(bf16[1024,1024]{1,0:T(8,128)(2,1)} %get-tuple-element.116.refs_2_.refs_0_, bf16[1024,2048]{1,0:T(8,128)(2,1)} %get-tuple-element.125.refs_2_.refs_1_, bf16[2048,6272]{1,0:T(8,128)(2,1)} %all-gather.3.cloned.1.call-done.refs_1_.refs_4_.refs_2_.refs_3_.refs_6_, ...), custom_call_target="tpu_custom_call" | custom-call | flops 109371842560 | tf_op jit(solution)/shard_map/nt_product/pallas_call | solution.py:56
  480.4 20.8 %attend_back.2 = (bf16[1024,1024]{1,0:T(8,128)(2,1)}, bf16[512,1024]{1,0:T(8,128)(2,1)}, bf16[512,1024]{1,0:T(8,128)(2,1)}, bf16[2,512,1024]{2,1,0:T(8,128)(2,1)}, f32[8,128]{1,0:T(8,128)}) custom-call(bf16[1024,1024]{1,0:T(8,128)(2,1)} %get-tuple-element.104.refs_1_.refs_0_, bf16[512,1024]{1,0:T(8,128)(2,1)} %get-tuple-element.100.refs_2_.refs_1_, ...), custom_call_target="tpu_custom_call" | custom-call | flops 249999998976 | tf_op jit(solution)/shard_map/attend_back/pallas_call | solution.py:56
  503.0 7.5 norm_back.5
  533.9 8.8 %grad_product.10 = (bf16[512,1024]{1,0:T(8,128)(2,1)}, bf16[512,1024]{1,0:T(8,128)(2,1)}) custom-call(bf16[1024,1024]{1,0:T(8,128)(2,1)} %get-tuple-element.138.refs_2_.refs_0_, bf16[1024,1024]{1,0:T(8,128)(2,1)} %copy-done.22, bf16[512,1024]{1,0:T(8,128)(2,1)} %get-tuple-element.106.refs_6_.refs_2_, bf16[512,1024]{1,0:T(8,128)(2,1)} %get-tuple-element.109.refs_2_.refs_3_, ...), custom_call_target="tpu_custom_call" | custom-call | flops 83128000512 | tf_op jit(solution)/shard_map/grad_product/pallas_call | solution.py:56
  543.5 11.4 %nt_product.9.refs_4_.refs_1_ = bf16[512,2048]{1,0:T(8,128)(2,1)} custom-call(bf16[1024,1024]{1,0:T(8,128)(2,1)} %get-tuple-element.116.refs_2_.refs_0_, bf16[1024,2048]{1,0:T(8,128)(2,1)} %get-tuple-element.125.refs_2_.refs_1_, bf16[2048,6272]{1,0:T(8,128)(2,1)} %all-gather.3.cloned.1.call-done.refs_1_.refs_4_.refs_2_.refs_3_.refs_6_, ...), custom_call_target="tpu_custom_call" | custom-call | flops 109371842560 | tf_op jit(solution)/shard_map/nt_product/pallas_call | solution.py:56
  555.5 13.2 %grad_product.11 = (bf16[512,2048]{1,0:T(8,128)(2,1)}, bf16[512,2048]{1,0:T(8,128)(2,1)}) custom-call(bf16[1024,1024]{1,0:T(8,128)(2,1)} %get-tuple-element.115.refs_5_.refs_4_.refs_8_.refs_0_, bf16[1024,1024]{1,0:T(8,128)(2,1)} %collective-permute-done.15.refs_5_.refs_9_.refs_1_, bf16[1024,2048]{1,0:T(8,128)(2,1)} %get-tuple-element.127.refs_3_.refs_2_, ...), custom_call_target="tpu_custom_call" | custom-call | flops 131256000512 | tf_op jit(solution)/shard_map/grad_product/pallas_call | solution.py:56
  576.7 8.9 %nt_product.10.refs_12_.refs_1_.refs_2_ = bf16[512,2048]{1,0:T(8,128)(2,1)} custom-call(bf16[1024,1024]{1,0:T(8,128)(2,1)} %get-tuple-element.145.refs_0_.refs_11_, bf16[1024,1024]{1,0:T(8,128)(2,1)} %get-tuple-element.148.refs_1_.refs_7_, bf16[2048,6272]{1,0:T(8,128)(2,1)} %all-gather.3.cloned.1.call-done.refs_1_.refs_4_.refs_2_.refs_3_.refs_6_, ...), custom_call_target="tpu_custom_call" | custom-call | flops 77914562560 | tf_op jit(solution)/shard_map/nt_product/pallas_call | solution.py:56
  587.0 20.5 %attend_back.3 = (bf16[1024,1024]{1,0:T(8,128)(2,1)}, bf16[512,1024]{1,0:T(8,128)(2,1)}, bf16[512,1024]{1,0:T(8,128)(2,1)}, bf16[2,512,1024]{2,1,0:T(8,128)(2,1)}, f32[8,128]{1,0:T(8,128)}) custom-call(bf16[1024,1024]{1,0:T(8,128)(2,1)} %get-tuple-element.104.refs_1_.refs_0_, ...), custom_call_target="tpu_custom_call", output_to_operand_aliasing={{0}: (11, {})} | custom-call | flops 249999998976 | tf_op jit(solution)/shard_map/attend_back/pallas_call | solution.py:56
  620.0 8.4 %grad_product.12 = (bf16[512,1024]{1,0:T(8,128)(2,1)}, bf16[512,1024]{1,0:T(8,128)(2,1)}) custom-call(bf16[1024,1024]{1,0:T(8,128)(2,1)} %get-tuple-element.103.refs_5_.refs_0_, bf16[1024,1024]{1,0:T(8,128)(2,1)} %collective-permute-done.13.refs_7_.refs_1_, bf16[1024,1024]{1,0:T(8,128)(2,1)} %get-tuple-element.152.refs_2_.refs_0_, ...), custom_call_target="tpu_custom_call" | custom-call | flops 83128000512 | tf_op jit(solution)/shard_map/grad_product/pallas_call | solution.py:56
  649.5 8.8 %nt_product.11.refs_4_.refs_1_.refs_2_ = bf16[512,2048]{1,0:T(8,128)(2,1)} custom-call(bf16[1024,1024]{1,0:T(8,128)(2,1)} %get-tuple-element.152.refs_2_.refs_0_, bf16[1024,1024]{1,0:T(8,128)(2,1)} %get-tuple-element.158.refs_1_.refs_2_, bf16[2048,6272]{1,0:T(8,128)(2,1)} %all-gather.3.cloned.1.call-done.refs_1_.refs_4_.refs_2_.refs_3_.refs_6_, ...), custom_call_target="tpu_custom_call" | custom-call | flops 77914562560 | tf_op jit(solution)/shard_map/nt_product/pallas_call | solution.py:56
  665.6 8.5 %grad_product.13 = (bf16[512,1024]{1,0:T(8,128)(2,1)}, bf16[512,1024]{1,0:T(8,128)(2,1)}) custom-call(bf16[1024,1024]{1,0:T(8,128)(2,1)} %get-tuple-element.103.refs_5_.refs_0_, bf16[1024,1024]{1,0:T(8,128)(2,1)} %collective-permute-done.13.refs_7_.refs_1_, bf16[1024,1024]{1,0:T(8,128)(2,1)} %get-tuple-element.158.refs_1_.refs_2_, ...), custom_call_target="tpu_custom_call" | custom-call | flops 83128000512 | tf_op jit(solution)/shard_map/grad_product/pallas_call | solution.py:56
  675.3 7.5 norm_back.6
  684.8 14.6 %collective-permute-done.40.refs_3_ = bf16[512,1024]{1,0:T(8,128)(2,1)S(1)} collective-permute-done((bf16[512,1024]{1,0:T(8,128)(2,1)}, bf16[512,1024]{1,0:T(8,128)(2,1)S(1)}, u32[]{:S(2)}, u32[]{:S(2)}) %collective-permute-start.40) | collective-permute-done | bytes 1048608 | tf_op jit(solution)/shard_map/key_over_x/ppermute | solution.py:823
  713.6 7.5 norm_back.7
  726.0 26.9 %reduce-scatter.10.cloned.1.call-done = bf16[128,2048]{1,0:T(8,128)(2,1)} async-done(((bf16[512,2048]{1,0:T(8,128)(2,1)}), bf16[128,2048]{1,0:T(8,128)(2,1)}) %reduce-scatter.10.cloned.1.call-update) | async-done | bytes 524304 | tf_op jit(solution)/shard_map/query_key_over_dp/reduce_scatter | solution.py:946
  (246 shorter events, 210.4 us)
Async XLA Ops:
  7.2 138.7 %all-gather.3.cloned.1.call-start = ((), (), s32[]{:S(2)}) async-start(), calls=%async_computation.6 | async-start | bytes 27295744 | tf_op jit(solution)/shard_map/all_gather | solution.py:840
  12.0 332.4 %all-gather.5.cloned.1.call-start = ((), (), s32[]{:S(2)}) async-start(), calls=%async_computation.7 | async-start | bytes 26738688 | tf_op jit(solution)/shard_map/all_gather | solution.py:910
  161.1 25.6 %collective-permute-start.2 = (bf16[512,1024]{1,0:T(8,128)(2,1)}, bf16[512,1024]{1,0:T(8,128)(2,1)}, u32[]{:S(2)}, u32[]{:S(2)}) collective-permute-start(bf16[512,1024]{1,0:T(8,128)(2,1)} %get-tuple-element.100.refs_2_.refs_1_), channel_id=1, source_target_pairs={{0,4},{4,0},{2,6},{6,2},{1,5},{5,1},{3,7},{7,3},{8,12},{12,8},{10,... | collective-permute-start | bytes 3145736 | tf_op jit(solution)/shard_map/kv0_over_x/ppermute | solution.py:823
  162.3 25.6 %collective-permute-start.1 = (bf16[512,1024]{1,0:T(8,128)(2,1)}, bf16[512,1024]{1,0:T(8,128)(2,1)}, u32[]{:S(2)}, u32[]{:S(2)}) collective-permute-start(bf16[512,1024]{1,0:T(8,128)(2,1)} %get-tuple-element.100.refs_2_.refs_1_), channel_id=1, source_target_pairs={{0,2},{2,0},{4,6},{6,4},{1,3},{3,1},{5,7},{7,5},{8,10},{10,8},{12,... | collective-permute-start | bytes 3145736 | tf_op jit(solution)/shard_map/kv0_over_core/ppermute | solution.py:823
  165.4 48.4 %collective-permute-start.7 = (bf16[1024,1024]{1,0:T(8,128)(2,1)}, bf16[1024,1024]{1,0:T(8,128)(2,1)}, u32[]{:S(2)}, u32[]{:S(2)}) collective-permute-start(bf16[1024,1024]{1,0:T(8,128)(2,1)} %constant_dynamic-slice_fusion.refs_5_), channel_id=1, source_target_pairs={{0,1},{1,0},{2,3},{3,2},{4,5},{5,4},{6,7},{7,6},{8,9},{9,8},{10,11... | collective-permute-start | bytes 6291464 | tf_op jit(solution)/shard_map/output_proj_over_tp/ppermute | solution.py:823
  186.7 26.8 %collective-permute-start.4 = (bf16[512,1024]{1,0:T(8,128)(2,1)}, bf16[512,1024]{1,0:T(8,128)(2,1)}, u32[]{:S(2)}, u32[]{:S(2)}) collective-permute-start(bf16[512,1024]{1,0:T(8,128)(2,1)} %get-tuple-element.105.refs_5_.refs_2_.refs_1_), channel_id=1, source_target_pairs={{0,4},{4,0},{2,6},{6,2},{1,5},{5,1},{3,7},{7,3},{8,12},{12,8},{10,... | collective-permute-start | bytes 3145736 | tf_op jit(solution)/shard_map/kv1_over_x/ppermute | solution.py:823
  214.2 62.4 %collective-permute-start.13 = (bf16[1024,1024]{1,0:T(8,128)(2,1)}, bf16[1024,1024]{1,0:T(8,128)(2,1)}, u32[]{:S(2)}, u32[]{:S(2)}) collective-permute-start(bf16[1024,1024]{1,0:T(8,128)(2,1)} %get-tuple-element.114), channel_id=1, source_target_pairs={{0,2},{2,0},{4,6},{6,4},{1,3},{3,1},{5,7},{7,5},{8,10},{10,8},{12,... | collective-permute-start | bytes 6291464 | tf_op jit(solution)/shard_map/normed_one_over_core/ppermute | solution.py:823
  214.6 62.1 %collective-permute-start.11 = (bf16[512,1024]{1,0:T(8,128)(2,1)}, bf16[512,1024]{1,0:T(8,128)(2,1)}, u32[]{:S(2)}, u32[]{:S(2)}) collective-permute-start(bf16[512,1024]{1,0:T(8,128)(2,1)} %get-tuple-element.106.refs_6_.refs_2_), channel_id=1, source_target_pairs={{0,2},{2,0},{4,6},{6,4},{1,3},{3,1},{5,7},{7,5},{8,10},{10,8},{12,... | collective-permute-start | bytes 3145736 | tf_op jit(solution)/shard_map/attended_over_core/ppermute | solution.py:823
  214.7 25.8 %collective-permute-start.10 = (bf16[512,1024]{1,0:T(8,128)(2,1)}, bf16[512,1024]{1,0:T(8,128)(2,1)}, u32[]{:S(2)}, u32[]{:S(2)}) collective-permute-start(bf16[512,1024]{1,0:T(8,128)(2,1)} %get-tuple-element.106.refs_6_.refs_2_), channel_id=1, source_target_pairs={{0,1},{1,0},{2,3},{3,2},{4,5},{5,4},{6,7},{7,6},{8,9},{9,8},{10,11... | collective-permute-start | bytes 3145736 | tf_op jit(solution)/shard_map/attended0_over_tp/ppermute | solution.py:823
  216.2 311.1 %reduce-scatter.6.cloned.1.call-start = ((), (), s32[]{:S(2)}) async-start(), calls=%async_computation.8 | async-start | bytes 3932160 | tf_op jit(solution)/shard_map/first_third_over_dp/reduce_scatter | solution.py:946
  236.9 39.8 %collective-permute-start.12 = (bf16[512,1024]{1,0:T(8,128)(2,1)}, bf16[512,1024]{1,0:T(8,128)(2,1)}, u32[]{:S(2)}, u32[]{:S(2)}) collective-permute-start(bf16[512,1024]{1,0:T(8,128)(2,1)} %get-tuple-element.109.refs_2_.refs_3_), channel_id=1, source_target_pairs={{0,2},{2,0},{4,6},{6,4},{1,3},{3,1},{5,7},{7,5},{8,10},{10,8},{12,... | collective-permute-start | bytes 3145736 | tf_op jit(solution)/shard_map/attended_over_core/ppermute | solution.py:823
  237.2 25.7 %collective-permute-start.9 = (bf16[512,1024]{1,0:T(8,128)(2,1)}, bf16[512,1024]{1,0:T(8,128)(2,1)}, u32[]{:S(2)}, u32[]{:S(2)}) collective-permute-start(bf16[512,1024]{1,0:T(8,128)(2,1)} %get-tuple-element.109.refs_2_.refs_3_), channel_id=1, source_target_pairs={{0,1},{1,0},{2,3},{3,2},{4,5},{5,4},{6,7},{7,6},{8,9},{9,8},{10,11... | collective-permute-start | bytes 3145736 | tf_op jit(solution)/shard_map/attended1_over_tp/ppermute | solution.py:823
  339.1 96.7 %collective-permute-start.23 = (bf16[512,3072]{1,0:T(8,128)(2,1)}, bf16[512,3072]{1,0:T(8,128)(2,1)}, u32[]{:S(2)}, u32[]{:S(2)}) collective-permute-start(bf16[512,3072]{1,0:T(8,128)(2,1)} %get-tuple-element.129), channel_id=1, source_target_pairs={{0,4},{4,0},{2,6},{6,2},{1,5},{5,1},{3,7},{7,3},{8,12},{12,8},{10,... | collective-permute-start | bytes 9437192 | tf_op jit(solution)/shard_map/first_third_over_x/ppermute | solution.py:823
  378.7 36.6 %collective-permute-start.19 = (bf16[1024,2048]{1,0:T(8,128)(2,1)}, bf16[1024,2048]{1,0:T(8,128)(2,1)}, u32[]{:S(2)}, u32[]{:S(2)}) collective-permute-start(bf16[1024,2048]{1,0:T(8,128)(2,1)} %get-tuple-element.126.refs_1_.refs_2_), channel_id=1, source_target_pairs={{0,2},{2,0},{4,6},{6,4},{1,3},{3,1},{5,7},{7,5},{8,10},{10,8},{12,... | collective-permute-start | bytes 12582920 | tf_op jit(solution)/shard_map/gate_back_two_over_core/ppermute | solution.py:823
  379.0 36.3 %collective-permute-start.20 = (bf16[1024,2048]{1,0:T(8,128)(2,1)}, bf16[1024,2048]{1,0:T(8,128)(2,1)}, u32[]{:S(2)}, u32[]{:S(2)}) collective-permute-start(bf16[1024,2048]{1,0:T(8,128)(2,1)} %get-tuple-element.127.refs_3_.refs_2_), channel_id=1, source_target_pairs={{0,2},{2,0},{4,6},{6,4},{1,3},{3,1},{5,7},{7,5},{8,10},{10,8},{12,... | collective-permute-start | bytes 12582920 | tf_op jit(solution)/shard_map/up_back_two_over_core/ppermute | solution.py:823
  399.4 54.9 %collective-permute-start.22 = (bf16[512,2048]{1,0:T(8,128)(2,1)}, bf16[512,2048]{1,0:T(8,128)(2,1)}, u32[]{:S(2)}, u32[]{:S(2)}) collective-permute-start(bf16[512,2048]{1,0:T(8,128)(2,1)} %nt_product.6.refs_4_.refs_2_), channel_id=1, source_target_pairs={{0,1},{1,0},{2,3},{3,2},{4,5},{5,4},{6,7},{7,6},{8,9},{9,8},{10,11... | collective-permute-start | bytes 6291464 | tf_op jit(solution)/shard_map/back0_over_tp/ppermute | solution.py:823
  414.1 113.2 %collective-permute-start.26 = (bf16[512,2048]{1,0:T(8,128)(2,1)}, bf16[512,2048]{1,0:T(8,128)(2,1)}, u32[]{:S(2)}, u32[]{:S(2)}) collective-permute-start(bf16[512,2048]{1,0:T(8,128)(2,1)} %get-tuple-element.140), channel_id=1, source_target_pairs={{0,4},{4,0},{2,6},{6,2},{1,5},{5,1},{3,7},{7,3},{8,12},{12,8},{10,... | collective-permute-start | bytes 6291464 | tf_op jit(solution)/shard_map/down_two_over_x/ppermute | solution.py:823
  435.3 67.7 %collective-permute-start.21 = (bf16[512,2048]{1,0:T(8,128)(2,1)}, bf16[512,2048]{1,0:T(8,128)(2,1)}, u32[]{:S(2)}, u32[]{:S(2)}) collective-permute-start(bf16[512,2048]{1,0:T(8,128)(2,1)} %nt_product.7.refs_2_), channel_id=1, source_target_pairs={{0,1},{1,0},{2,3},{3,2},{4,5},{5,4},{6,7},{7,6},{8,9},{9,8},{10,11... | collective-permute-start | bytes 6291464 | tf_op jit(solution)/shard_map/back1_over_tp/ppermute | solution.py:823
  440.2 189.3 %reduce-scatter.8.cloned.1.call-start = ((), (), s32[]{:S(2)}) async-start(), calls=%async_computation.9 | async-start | bytes 5242880 | tf_op jit(solution)/shard_map/down_gate_two_over_dp/reduce_scatter | solution.py:946
  453.4 62.7 %collective-permute-start.24 = (bf16[512,2048]{1,0:T(8,128)(2,1)}, bf16[512,2048]{1,0:T(8,128)(2,1)}, u32[]{:S(2)}, u32[]{:S(2)}) collective-permute-start(bf16[512,2048]{1,0:T(8,128)(2,1)} %get-tuple-element.137), channel_id=1, source_target_pairs={{0,4},{4,0},{2,6},{6,2},{1,5},{5,1},{3,7},{7,3},{8,12},{12,8},{10,... | collective-permute-start | bytes 6291464 | tf_op jit(solution)/shard_map/gate_two_over_x/ppermute | solution.py:823
  478.9 76.6 %collective-permute-start.29 = (bf16[512,2048]{1,0:T(8,128)(2,1)}, bf16[512,2048]{1,0:T(8,128)(2,1)}, u32[]{:S(2)}, u32[]{:S(2)}) collective-permute-start(bf16[512,2048]{1,0:T(8,128)(2,1)} %nt_product.8.refs_11_.refs_1_), channel_id=1, source_target_pairs={{0,1},{1,0},{2,3},{3,2},{4,5},{5,4},{6,7},{7,6},{8,9},{9,8},{10,11... | collective-permute-start | bytes 6291464 | tf_op jit(solution)/shard_map/out0_over_tp/ppermute | solution.py:823
  525.5 43.1 %collective-permute-start.30 = (bf16[512,1024]{1,0:T(8,128)(2,1)}, bf16[512,1024]{1,0:T(8,128)(2,1)}, u32[]{:S(2)}, u32[]{:S(2)}) collective-permute-start(bf16[512,1024]{1,0:T(8,128)(2,1)} %add_rows.8.refs_4_), channel_id=1, source_target_pairs={{0,4},{4,0},{2,6},{6,2},{1,5},{5,1},{3,7},{7,3},{8,12},{12,8},{10,... | collective-permute-start | bytes 3145736 | tf_op jit(solution)/shard_map/kv_grad0_over_x/ppermute | solution.py:823
  532.5 150.2 %reduce-scatter.12.cloned.1.call-start = ((), (), s32[]{:S(2)}) async-start(), calls=%async_computation.11 | async-start | bytes 1310720 | tf_op jit(solution)/shard_map/output_over_dp/reduce_scatter | solution.py:946
  542.7 34.0 %collective-permute-start.31 = (bf16[512,1024]{1,0:T(8,128)(2,1)}, bf16[512,1024]{1,0:T(8,128)(2,1)}, u32[]{:S(2)}, u32[]{:S(2)}) collective-permute-start(bf16[512,1024]{1,0:T(8,128)(2,1)} %get-tuple-element.149), channel_id=1, source_target_pairs={{0,4},{4,0},{2,6},{6,2},{1,5},{5,1},{3,7},{7,3},{8,12},{12,8},{10,... | collective-permute-start | bytes 3145736 | tf_op jit(solution)/shard_map/output_over_x/ppermute | solution.py:823
  554.9 80.8 %collective-permute-start.28 = (bf16[512,2048]{1,0:T(8,128)(2,1)}, bf16[512,2048]{1,0:T(8,128)(2,1)}, u32[]{:S(2)}, u32[]{:S(2)}) collective-permute-start(bf16[512,2048]{1,0:T(8,128)(2,1)} %nt_product.9.refs_4_.refs_1_), channel_id=1, source_target_pairs={{0,1},{1,0},{2,3},{3,2},{4,5},{5,4},{6,7},{7,6},{8,9},{9,8},{10,11... | collective-permute-start | bytes 6291464 | tf_op jit(solution)/shard_map/out1_over_tp/ppermute | solution.py:823
  574.6 57.5 %collective-permute-start.32 = (bf16[512,2048]{1,0:T(8,128)(2,1)}, bf16[512,2048]{1,0:T(8,128)(2,1)}, u32[]{:S(2)}, u32[]{:S(2)}) collective-permute-start(bf16[512,2048]{1,0:T(8,128)(2,1)} %get-tuple-element.151), channel_id=1, source_target_pairs={{0,4},{4,0},{2,6},{6,2},{1,5},{5,1},{3,7},{7,3},{8,12},{12,8},{10,... | collective-permute-start | bytes 6291464 | tf_op jit(solution)/shard_map/up_two_over_x/ppermute | solution.py:823
  585.5 89.8 %collective-permute-start.37 = (bf16[512,2048]{1,0:T(8,128)(2,1)}, bf16[512,2048]{1,0:T(8,128)(2,1)}, u32[]{:S(2)}, u32[]{:S(2)}) collective-permute-start(bf16[512,2048]{1,0:T(8,128)(2,1)} %nt_product.10.refs_12_.refs_1_.refs_2_), channel_id=1, source_target_pairs={{0,1},{1,0},{2,3},{3,2},{4,5},{5,4},{6,7},{7,6},{8,9},{9,8},{10,11... | collective-permute-start | bytes 6291464 | tf_op jit(solution)/shard_map/one0_over_tp/ppermute | solution.py:823
  617.8 27.2 %collective-permute-start.35 = (bf16[512,1024]{1,0:T(8,128)(2,1)}, bf16[512,1024]{1,0:T(8,128)(2,1)}, u32[]{:S(2)}, u32[]{:S(2)}) collective-permute-start(bf16[512,1024]{1,0:T(8,128)(2,1)} %add_rows.10.refs_4_), channel_id=1, source_target_pairs={{0,4},{4,0},{2,6},{6,2},{1,5},{5,1},{3,7},{7,3},{8,12},{12,8},{10,... | collective-permute-start | bytes 3145736 | tf_op jit(solution)/shard_map/kv_grad1_over_x/ppermute | solution.py:823
  628.4 46.9 %collective-permute-start.39 = (bf16[512,1024]{1,0:T(8,128)(2,1)}, bf16[512,1024]{1,0:T(8,128)(2,1)}, u32[]{:S(2)}, u32[]{:S(2)}) collective-permute-start(bf16[512,1024]{1,0:T(8,128)(2,1)} %get-tuple-element.160), channel_id=1, source_target_pairs={{0,4},{4,0},{2,6},{6,2},{1,5},{5,1},{3,7},{7,3},{8,12},{12,8},{10,... | collective-permute-start | bytes 3145736 | tf_op jit(solution)/shard_map/query_over_x/ppermute | solution.py:823
  632.0 91.6 %reduce-scatter.14.cloned.1.call-start = ((), (), s32[]{:S(2)}) async-start(), calls=%async_computation.12 | async-start | bytes 2621440 | tf_op jit(solution)/shard_map/up_two_over_dp/reduce_scatter | solution.py:946
  661.1 91.7 %reduce-scatter.10.cloned.1.call-start = ((), (), s32[]{:S(2)}) async-start(), calls=%async_computation.10 | async-start | bytes 2621440 | tf_op jit(solution)/shard_map/query_key_over_dp/reduce_scatter | solution.py:946
  661.9 51.6 %collective-permute-start.36 = (bf16[512,2048]{1,0:T(8,128)(2,1)}, bf16[512,2048]{1,0:T(8,128)(2,1)}, u32[]{:S(2)}, u32[]{:S(2)}) collective-permute-start(bf16[512,2048]{1,0:T(8,128)(2,1)} %nt_product.11.refs_4_.refs_1_.refs_2_), channel_id=1, source_target_pairs={{0,1},{1,0},{2,3},{3,2},{4,5},{5,4},{6,7},{7,6},{8,9},{9,8},{10,11... | collective-permute-start | bytes 6291464 | tf_op jit(solution)/shard_map/one1_over_tp/ppermute | solution.py:823
  (48 other events, 462.4 us)
Sparse Core Ops, SparseCore 0:
  12.1 133.7 all-gather.2
  216.4 127.9 all-gather.4
  440.3 60.9 reduce-scatter.5
  532.7 76.5 reduce-scatter.7
  632.2 26.9 reduce-scatter.11
  661.3 45.2 reduce-scatter.13
  709.0 43.8 reduce-scatter.9

commit v6 on v5

--- a/solution.py
+++ b/solution.py
@@ -137,22 +137,27 @@
     )[0]
 
 
-def norm_kernel(x_ref, gain_ref, out_ref):
-    out_ref[...] = (unit_norm(x_ref[...].astype(F32))[0] * gain_ref[...]).astype(BF16)
-
-
-def norm_rows(x, gain, after=()):
+def norm_kernel(x_ref, gain_ref, *rest):
+    rest[-1][...] = (unit_norm(x_ref[...].astype(F32))[0] * gain_ref[...]).astype(BF16)
+
+
+def norm_rows(x, gain, row, rows, into, after=()):
     tokens, width = x.shape
-    tile = min(256, tokens)
+    tile = min(256, rows)
     block = (tile, width)
+    spot = lambda j: (row // tile + j, 0)
+    ins = [(x, block, spot), (gain, (1, width), lambda j: (0, 0))]
+    if into is not None:
+        ins.append((into, None, None))
     return call(
         norm_kernel,
-        (tokens // tile,),
-        [(x, block, lambda j: (j, 0)), (gain, (1, width), lambda j: (0, 0))],
-        [((tokens, width), BF16, block, lambda j: (j, 0))],
+        (rows // tile,),
+        ins,
+        [((tokens, width), BF16, block, spot)],
+        alias=None if into is None else {0: len(ins) - 1},
         after=after,
         name="norm_rows",
-        cost=5,
+        cost=3,
     )[0]
 
 
@@ -876,9 +881,10 @@
     gain_query = small[2, :, 0:head_shard].reshape(1, HEAD_DIM)
     gain_key = small[3, :, 0:head_shard].reshape(1, HEAD_DIM)
 
-    feed_one = norm_rows(input_rows, gain_first)
+    feed_one = None
     kv, raw_kv, latest = [], [], ()
     for h in range(2):
+        feed_one = norm_rows(input_rows, gain_first, h * half_rows, half_rows, feed_one, after=latest)
         part = project(
             feed_one, weights, cosine, sine, gain_key, groups, groups, 1, h * half_rows, half_rows, after=latest
         )
@@ -911,7 +917,7 @@
 
     settled = (attended[0],)
     if pair:
-        output_swapped = core_swap(behind(output_same, arrived), "output_proj")
+        output_swapped = core_swap(behind(output_same, others[1][2]), "output_proj")
         settled += (output_swapped,)
     found.append(attend(orders, q, kv[1], others[1], half_seqs, half_seqs, local, after=settled))
     attended, probs = [list(parts) for parts in zip(*found)]

time: 771 us -> 772 us (level)
    pallas_call x50 -> x51, Pallas kernels: 473 us -> 475 us  [call(): pl.pallas_call(body, grid_spec=pltpu.PrefetchScalarGridSpec(num_scalar_pr...]
  transfers between devices with their start and end apart: 49 -> 49, of which waited for: 14 -> 14; matrix products, arithmetic and copies ran while one was open for 3% -> 3% of each run, Pallas kernels for 60% -> 61%
where the time goes in v6:
time: 772 us; the launch traced here: 764 us
  Pallas kernels  475 us (62%)
  waiting for transfers between devices  195 us (25%)
  starting transfers between devices  33.1 us (4%)
  local copies, waits for them, and re-layouts  28.2 us (4%)
  other arithmetic  18.2 us (2%)
  between operations  14.9 us (2%)
    pallas_call x51, Pallas kernels, call(): pl.pallas_call(body, grid_spec=pltpu.PrefetchScalarGridSpec(num_scalar_pr...  475 us
    all_gather x1, waiting for transfers between devices, shards(): weights = lax.all_gather(shard_one, ('dp', 'ctx'), axis=0, tiled=True)  115 us
    ppermute x41, waiting for transfers between devices, swap(): return lax.ppermute(value, axis, pairs)  47.4 us
    ppermute x41, starting transfers between devices, swap(): return lax.ppermute(value, axis, pairs)  28.5 us
    reduce_scatter x5, waiting for transfers between devices, over_dp(): lax.psum_scatter(summed, 'dp', scatter_dimension=0, tiled=True)  27 us
  transfers between devices with their start and end apart: 49, of which 14 were waited for; matrix products, arithmetic and copies ran while one was open for 3% of the time, Pallas kernels for 61%

profile of v6, /device:TPU:0, one launch (start us, length us, event | category | flops | bytes accessed | tf_op | source)
XLA Modules:
  0.0 763.8 jit_solution(5252279544821812255)
XLA Ops:
  30.7 115.1 %all-gather.3.cloned.1.call-done.refs_1_.refs_4_.refs_2_.refs_3_.refs_6_ = bf16[2048,6272]{1,0:T(8,128)(2,1)} async-done(((bf16[128,6272]{1,0:T(8,128)(2,1)}), bf16[2048,6272]{1,0:T(8,128)(2,1)}) %all-gather.3.cloned.1.call-update) | async-done | bytes 25690128 | tf_op jit(solution)/shard_map/all_gather | solution.py:845
  151.8 6.8 project.3
  167.5 6.8 project.4
  186.5 9.9 %project.5 = (bf16[1024,1024]{1,0:T(8,128)(2,1)}, f32[1024,1024]{1,0:T(8,128)}) custom-call(bf16[1024,2048]{1,0:T(8,128)(2,1)} %norm_rows.3.refs_0_.refs_1_.refs_2_.refs_3_.refs_4_, bf16[2048,6272]{1,0:T(8,128)(2,1)} %all-gather.3.cloned.1.call-done.refs_1_.refs_4_.refs_2_.refs_3_.refs_6_, f32[1024,128]{1,0:T(8,128)} %get-tuple-element.97.refs_2_.refs_8_.refs_4_, ...), custom_call_target="tpu_custom_call" | custom-call | flops 99999997952 | tf_op jit(solution)/shard_map/project/pallas_call | solution.py:56
  197.4 13.7 %attend.2 = (bf16[512,1024]{1,0:T(8,128)(2,1)}, bf16[2,2048,1024]{2,1,0:T(8,128)(2,1)}) custom-call(s32[4,8]{1,0:T(4,128)} %copy-done.14, bf16[1024,1024]{1,0:T(8,128)(2,1)} %get-tuple-element.104.refs_1_.refs_0_, bf16[512,1024]{1,0:T(8,128)(2,1)} %get-tuple-element.99.refs_2_.refs_1_, bf16[512,1024]{1,0:T(8,128)(2,1)} %collective-permute-done.1.refs_6_.refs_3_.refs_2_, ...), custom_call_target="tpu_custom_call" | custom-call | flops 109999996928 | tf_op jit(solution)/shard_map/attend/pallas_call | solution.py:56
  221.0 14.2 %attend.3 = (bf16[512,1024]{1,0:T(8,128)(2,1)}, bf16[2,2048,1024]{2,1,0:T(8,128)(2,1)}) custom-call(s32[4,8]{1,0:T(4,128)} %copy-done.14, bf16[1024,1024]{1,0:T(8,128)(2,1)} %get-tuple-element.104.refs_1_.refs_0_, bf16[512,1024]{1,0:T(8,128)(2,1)} %get-tuple-element.105.refs_5_.refs_2_.refs_1_, bf16[512,1024]{1,0:T(8,128)(2,1)} %copy-done.27, ...), custom_call_target="tpu_custom_call" | custom-call | flops 109999996928 | tf_op jit(solution)/shard_map/attend/pallas_call | solution.py:56
  241.4 13.9 %output_join.2 = (f32[1024,2048]{1,0:T(8,128)}, bf16[1024,2048]{1,0:T(8,128)(2,1)}) custom-call(s32[2]{0:T(128)} %pad_add_fusion.1.refs_0_, bf16[1024,2048]{1,0:T(8,128)(2,1)} %bitcast.71, bf16[512,1024]{1,0:T(8,128)(2,1)} %get-tuple-element.106.refs_6_.refs_2_, bf16[512,1024]{1,0:T(8,128)(2,1)} %collective-permute-done.10.refs_3_, ...), custom_call_target="tpu_custom_call" | custom-call | flops 149999992832 | tf_op jit(solution)/shard_map/output_join/pallas_call | solution.py:56
  255.3 8.0 %collective-permute-done.9.refs_3_ = bf16[512,1024]{1,0:T(8,128)(2,1)} collective-permute-done((bf16[512,1024]{1,0:T(8,128)(2,1)}, bf16[512,1024]{1,0:T(8,128)(2,1)}, u32[]{:S(2)}, u32[]{:S(2)}) %collective-permute-start.9) | collective-permute-done | bytes 1048608 | tf_op jit(solution)/shard_map/attended1_over_tp/ppermute | solution.py:828
  263.2 13.7 %output_join.3 = (f32[1024,2048]{1,0:T(8,128)}, bf16[1024,2048]{1,0:T(8,128)(2,1)}) custom-call(s32[2]{0:T(128)} %pad_add_fusion.1.refs_0_, bf16[1024,2048]{1,0:T(8,128)(2,1)} %bitcast.72, bf16[512,1024]{1,0:T(8,128)(2,1)} %get-tuple-element.109.refs_2_.refs_3_, ...), custom_call_target="tpu_custom_call", output_to_operand_aliasing={{0}: (8, {}), {1}: (9, {})} | custom-call | flops 149999992832 | tf_op jit(solution)/shard_map/output_join/pallas_call | solution.py:56
  283.3 20.6 %feed.2 = (bf16[1024,1024]{1,0:T(8,128)(2,1)}, bf16[1024,1024]{1,0:T(8,128)(2,1)}, bf16[1024,1024]{1,0:T(8,128)(2,1)}) custom-call(bf16[1024,2048]{1,0:T(8,128)(2,1)} %get-tuple-element.113.refs_1_.refs_2_.refs_3_.refs_4_.refs_0_, bf16[1024,2048]{1,0:T(8,128)(2,1)} %bitcast.65, ...), custom_call_target="tpu_custom_call" | custom-call | flops 188959997952 | tf_op jit(solution)/shard_map/feed/pallas_call | solution.py:56
  316.7 22.8 %grad_product.7 = (bf16[512,3072]{1,0:T(8,128)(2,1)}, bf16[512,3072]{1,0:T(8,128)(2,1)}) custom-call(bf16[1024,1024]{1,0:T(8,128)(2,1)} %get-tuple-element.119.refs_0_, bf16[1024,1024]{1,0:T(8,128)(2,1)} %copy-done.19, bf16[1024,1024]{1,0:T(8,128)(2,1)} %get-tuple-element.116.refs_2_.refs_0_, bf16[1024,1024]{1,0:T(8,128)(2,1)} %copy-done.23, ...), custom_call_target="tpu_custom_call" | custom-call | flops 179383992320 | tf_op jit(solution)/shard_map/grad_product/pallas_call | solution.py:56
  344.7 34.1 %feed.3 = (bf16[1024,2048]{1,0:T(8,128)(2,1)}, bf16[1024,2048]{1,0:T(8,128)(2,1)}, bf16[1024,2048]{1,0:T(8,128)(2,1)}) custom-call(bf16[1024,2048]{1,0:T(8,128)(2,1)} %get-tuple-element.113.refs_1_.refs_2_.refs_3_.refs_4_.refs_0_, bf16[1024,2048]{1,0:T(8,128)(2,1)} %bitcast.66, ...), custom_call_target="tpu_custom_call" | custom-call | flops 357920014336 | tf_op jit(solution)/shard_map/feed/pallas_call | solution.py:56
  379.5 20.2 %nt_product.6.refs_4_.refs_2_ = bf16[512,2048]{1,0:T(8,128)(2,1)} custom-call(bf16[1024,1024]{1,0:T(8,128)(2,1)} %get-tuple-element.122.refs_6_.refs_0_, bf16[1024,2048]{1,0:T(8,128)(2,1)} %get-tuple-element.126.refs_1_.refs_2_, bf16[1024,1024]{1,0:T(8,128)(2,1)} %get-tuple-element.123.refs_10_.refs_2_, ...), custom_call_target="tpu_custom_call" | custom-call | flops 203743674368 | tf_op jit(solution)/shard_map/nt_product/pallas_call | solution.py:56
  401.2 13.2 %grad_product.8 = (bf16[512,2048]{1,0:T(8,128)(2,1)}, bf16[512,2048]{1,0:T(8,128)(2,1)}) custom-call(bf16[1024,1024]{1,0:T(8,128)(2,1)} %get-tuple-element.119.refs_0_, bf16[1024,1024]{1,0:T(8,128)(2,1)} %copy-done.19, bf16[1024,2048]{1,0:T(8,128)(2,1)} %get-tuple-element.125.refs_2_.refs_1_, bf16[1024,2048]{1,0:T(8,128)(2,1)} %collective-permute-done.18.refs_3_, ...), custom_call_target="tpu_custom_call" | custom-call | flops 131256000512 | tf_op jit(solution)/shard_map/grad_product/pallas_call | solution.py:56
  415.6 20.0 %nt_product.7.refs_2_ = bf16[512,2048]{1,0:T(8,128)(2,1)} custom-call(bf16[1024,1024]{1,0:T(8,128)(2,1)} %get-tuple-element.122.refs_6_.refs_0_, bf16[1024,2048]{1,0:T(8,128)(2,1)} %get-tuple-element.126.refs_1_.refs_2_, bf16[1024,1024]{1,0:T(8,128)(2,1)} %get-tuple-element.123.refs_10_.refs_2_, bf16[1024,2048]{1,0:T(8,128)(2,1)} %get-tuple-element.127.refs_3_.refs_2_, ...), custom_call_target="tpu_custom_call" | custom-call | flops 203743674368 | tf_op jit(solution)/shard_map/nt_product/pallas_call | solution.py:56
  440.6 13.2 %grad_product.9 = (bf16[512,2048]{1,0:T(8,128)(2,1)}, bf16[512,2048]{1,0:T(8,128)(2,1)}) custom-call(bf16[1024,1024]{1,0:T(8,128)(2,1)} %get-tuple-element.115.refs_5_.refs_4_.refs_8_.refs_0_, bf16[1024,1024]{1,0:T(8,128)(2,1)} %collective-permute-done.15.refs_5_.refs_9_.refs_1_, bf16[1024,2048]{1,0:T(8,128)(2,1)} %get-tuple-element.126.refs_1_.refs_2_, ...), custom_call_target="tpu_custom_call" | custom-call | flops 131256000512 | tf_op jit(solution)/shard_map/grad_product/pallas_call | solution.py:56
  454.6 7.5 norm_back.4
  467.8 11.5 %nt_product.8.refs_11_.refs_1_ = bf16[512,2048]{1,0:T(8,128)(2,1)} custom-call(bf16[1024,1024]{1,0:T(8,128)(2,1)} %get-tuple-element.116.refs_2_.refs_0_, bf16[1024,2048]{1,0:T(8,128)(2,1)} %get-tuple-element.125.refs_2_.refs_1_, bf16[2048,6272]{1,0:T(8,128)(2,1)} %all-gather.3.cloned.1.call-done.refs_1_.refs_4_.refs_2_.refs_3_.refs_6_, ...), custom_call_target="tpu_custom_call" | custom-call | flops 109371842560 | tf_op jit(solution)/shard_map/nt_product/pallas_call | solution.py:56
  480.7 20.9 %attend_back.2 = (bf16[1024,1024]{1,0:T(8,128)(2,1)}, bf16[512,1024]{1,0:T(8,128)(2,1)}, bf16[512,1024]{1,0:T(8,128)(2,1)}, bf16[2,512,1024]{2,1,0:T(8,128)(2,1)}, f32[8,128]{1,0:T(8,128)}) custom-call(bf16[1024,1024]{1,0:T(8,128)(2,1)} %get-tuple-element.104.refs_1_.refs_0_, bf16[512,1024]{1,0:T(8,128)(2,1)} %get-tuple-element.99.refs_2_.refs_1_, ...), custom_call_target="tpu_custom_call" | custom-call | flops 249999998976 | tf_op jit(solution)/shard_map/attend_back/pallas_call | solution.py:56
  503.4 7.5 norm_back.5
  534.3 8.8 %grad_product.10 = (bf16[512,1024]{1,0:T(8,128)(2,1)}, bf16[512,1024]{1,0:T(8,128)(2,1)}) custom-call(bf16[1024,1024]{1,0:T(8,128)(2,1)} %get-tuple-element.138.refs_2_.refs_0_, bf16[1024,1024]{1,0:T(8,128)(2,1)} %copy-done.22, bf16[512,1024]{1,0:T(8,128)(2,1)} %get-tuple-element.106.refs_6_.refs_2_, bf16[512,1024]{1,0:T(8,128)(2,1)} %get-tuple-element.109.refs_2_.refs_3_, ...), custom_call_target="tpu_custom_call" | custom-call | flops 83128000512 | tf_op jit(solution)/shard_map/grad_product/pallas_call | solution.py:56
  543.9 11.4 %nt_product.9.refs_4_.refs_1_ = bf16[512,2048]{1,0:T(8,128)(2,1)} custom-call(bf16[1024,1024]{1,0:T(8,128)(2,1)} %get-tuple-element.116.refs_2_.refs_0_, bf16[1024,2048]{1,0:T(8,128)(2,1)} %get-tuple-element.125.refs_2_.refs_1_, bf16[2048,6272]{1,0:T(8,128)(2,1)} %all-gather.3.cloned.1.call-done.refs_1_.refs_4_.refs_2_.refs_3_.refs_6_, ...), custom_call_target="tpu_custom_call" | custom-call | flops 109371842560 | tf_op jit(solution)/shard_map/nt_product/pallas_call | solution.py:56
  555.8 13.2 %grad_product.11 = (bf16[512,2048]{1,0:T(8,128)(2,1)}, bf16[512,2048]{1,0:T(8,128)(2,1)}) custom-call(bf16[1024,1024]{1,0:T(8,128)(2,1)} %get-tuple-element.115.refs_5_.refs_4_.refs_8_.refs_0_, bf16[1024,1024]{1,0:T(8,128)(2,1)} %collective-permute-done.15.refs_5_.refs_9_.refs_1_, bf16[1024,2048]{1,0:T(8,128)(2,1)} %get-tuple-element.127.refs_3_.refs_2_, ...), custom_call_target="tpu_custom_call" | custom-call | flops 131256000512 | tf_op jit(solution)/shard_map/grad_product/pallas_call | solution.py:56
  577.0 8.9 %nt_product.10.refs_12_.refs_1_.refs_2_ = bf16[512,2048]{1,0:T(8,128)(2,1)} custom-call(bf16[1024,1024]{1,0:T(8,128)(2,1)} %get-tuple-element.145.refs_0_.refs_11_, bf16[1024,1024]{1,0:T(8,128)(2,1)} %get-tuple-element.148.refs_1_.refs_7_, bf16[2048,6272]{1,0:T(8,128)(2,1)} %all-gather.3.cloned.1.call-done.refs_1_.refs_4_.refs_2_.refs_3_.refs_6_, ...), custom_call_target="tpu_custom_call" | custom-call | flops 77914562560 | tf_op jit(solution)/shard_map/nt_product/pallas_call | solution.py:56
  587.4 20.5 %attend_back.3 = (bf16[1024,1024]{1,0:T(8,128)(2,1)}, bf16[512,1024]{1,0:T(8,128)(2,1)}, bf16[512,1024]{1,0:T(8,128)(2,1)}, bf16[2,512,1024]{2,1,0:T(8,128)(2,1)}, f32[8,128]{1,0:T(8,128)}) custom-call(bf16[1024,1024]{1,0:T(8,128)(2,1)} %get-tuple-element.104.refs_1_.refs_0_, ...), custom_call_target="tpu_custom_call", output_to_operand_aliasing={{0}: (11, {})} | custom-call | flops 249999998976 | tf_op jit(solution)/shard_map/attend_back/pallas_call | solution.py:56
  620.3 8.4 %grad_product.12 = (bf16[512,1024]{1,0:T(8,128)(2,1)}, bf16[512,1024]{1,0:T(8,128)(2,1)}) custom-call(bf16[1024,1024]{1,0:T(8,128)(2,1)} %get-tuple-element.103.refs_5_.refs_0_, bf16[1024,1024]{1,0:T(8,128)(2,1)} %collective-permute-done.13.refs_7_.refs_1_, bf16[1024,1024]{1,0:T(8,128)(2,1)} %get-tuple-element.152.refs_2_.refs_0_, ...), custom_call_target="tpu_custom_call" | custom-call | flops 83128000512 | tf_op jit(solution)/shard_map/grad_product/pallas_call | solution.py:56
  649.9 8.8 %nt_product.11.refs_4_.refs_1_.refs_2_ = bf16[512,2048]{1,0:T(8,128)(2,1)} custom-call(bf16[1024,1024]{1,0:T(8,128)(2,1)} %get-tuple-element.152.refs_2_.refs_0_, bf16[1024,1024]{1,0:T(8,128)(2,1)} %get-tuple-element.158.refs_1_.refs_2_, bf16[2048,6272]{1,0:T(8,128)(2,1)} %all-gather.3.cloned.1.call-done.refs_1_.refs_4_.refs_2_.refs_3_.refs_6_, ...), custom_call_target="tpu_custom_call" | custom-call | flops 77914562560 | tf_op jit(solution)/shard_map/nt_product/pallas_call | solution.py:56
  665.9 8.5 %grad_product.13 = (bf16[512,1024]{1,0:T(8,128)(2,1)}, bf16[512,1024]{1,0:T(8,128)(2,1)}) custom-call(bf16[1024,1024]{1,0:T(8,128)(2,1)} %get-tuple-element.103.refs_5_.refs_0_, bf16[1024,1024]{1,0:T(8,128)(2,1)} %collective-permute-done.13.refs_7_.refs_1_, bf16[1024,1024]{1,0:T(8,128)(2,1)} %get-tuple-element.158.refs_1_.refs_2_, ...), custom_call_target="tpu_custom_call" | custom-call | flops 83128000512 | tf_op jit(solution)/shard_map/grad_product/pallas_call | solution.py:56
  675.7 7.5 norm_back.6
  685.2 14.6 %collective-permute-done.40.refs_3_ = bf16[512,1024]{1,0:T(8,128)(2,1)S(1)} collective-permute-done((bf16[512,1024]{1,0:T(8,128)(2,1)}, bf16[512,1024]{1,0:T(8,128)(2,1)S(1)}, u32[]{:S(2)}, u32[]{:S(2)}) %collective-permute-start.40) | collective-permute-done | bytes 1048608 | tf_op jit(solution)/shard_map/key_over_x/ppermute | solution.py:828
  713.8 7.5 norm_back.7
  726.2 26.9 %reduce-scatter.10.cloned.1.call-done = bf16[128,2048]{1,0:T(8,128)(2,1)} async-done(((bf16[512,2048]{1,0:T(8,128)(2,1)}), bf16[128,2048]{1,0:T(8,128)(2,1)}) %reduce-scatter.10.cloned.1.call-update) | async-done | bytes 524304 | tf_op jit(solution)/shard_map/query_key_over_dp/reduce_scatter | solution.py:952
  (247 shorter events, 210.4 us)
Async XLA Ops:
  7.2 138.7 %all-gather.3.cloned.1.call-start = ((), (), s32[]{:S(2)}) async-start(), calls=%async_computation.6 | async-start | bytes 27295744 | tf_op jit(solution)/shard_map/all_gather | solution.py:845
  12.0 332.7 %all-gather.5.cloned.1.call-start = ((), (), s32[]{:S(2)}) async-start(), calls=%async_computation.7 | async-start | bytes 26738688 | tf_op jit(solution)/shard_map/all_gather | solution.py:916
  158.7 25.6 %collective-permute-start.2 = (bf16[512,1024]{1,0:T(8,128)(2,1)}, bf16[512,1024]{1,0:T(8,128)(2,1)}, u32[]{:S(2)}, u32[]{:S(2)}) collective-permute-start(bf16[512,1024]{1,0:T(8,128)(2,1)} %get-tuple-element.99.refs_2_.refs_1_), channel_id=1, source_target_pairs={{0,4},{4,0},{2,6},{6,2},{1,5},{5,1},{3,7},{7,3},{8,12},{12,8},{10,... | collective-permute-start | bytes 3145736 | tf_op jit(solution)/shard_map/kv0_over_x/ppermute | solution.py:828
  159.9 25.6 %collective-permute-start.1 = (bf16[512,1024]{1,0:T(8,128)(2,1)}, bf16[512,1024]{1,0:T(8,128)(2,1)}, u32[]{:S(2)}, u32[]{:S(2)}) collective-permute-start(bf16[512,1024]{1,0:T(8,128)(2,1)} %get-tuple-element.99.refs_2_.refs_1_), channel_id=1, source_target_pairs={{0,2},{2,0},{4,6},{6,4},{1,3},{3,1},{5,7},{7,5},{8,10},{10,8},{12,... | collective-permute-start | bytes 3145736 | tf_op jit(solution)/shard_map/kv0_over_core/ppermute | solution.py:828
  166.0 48.4 %collective-permute-start.7 = (bf16[1024,1024]{1,0:T(8,128)(2,1)}, bf16[1024,1024]{1,0:T(8,128)(2,1)}, u32[]{:S(2)}, u32[]{:S(2)}) collective-permute-start(bf16[1024,1024]{1,0:T(8,128)(2,1)} %constant_dynamic-slice_fusion.refs_3_.refs_5_), channel_id=1, source_target_pairs={{0,1},{1,0},{2,3},{3,2},{4,5},{5,4},{6,7},{7,6},{8,9},{9,8},{10,11... | collective-permute-start | bytes 6291464 | tf_op jit(solution)/shard_map/output_proj_over_tp/ppermute | solution.py:828
  184.3 26.8 %collective-permute-start.4 = (bf16[512,1024]{1,0:T(8,128)(2,1)}, bf16[512,1024]{1,0:T(8,128)(2,1)}, u32[]{:S(2)}, u32[]{:S(2)}) collective-permute-start(bf16[512,1024]{1,0:T(8,128)(2,1)} %get-tuple-element.105.refs_5_.refs_2_.refs_1_), channel_id=1, source_target_pairs={{0,4},{4,0},{2,6},{6,2},{1,5},{5,1},{3,7},{7,3},{8,12},{12,8},{10,... | collective-permute-start | bytes 3145736 | tf_op jit(solution)/shard_map/kv1_over_x/ppermute | solution.py:828
  214.6 62.4 %collective-permute-start.13 = (bf16[1024,1024]{1,0:T(8,128)(2,1)}, bf16[1024,1024]{1,0:T(8,128)(2,1)}, u32[]{:S(2)}, u32[]{:S(2)}) collective-permute-start(bf16[1024,1024]{1,0:T(8,128)(2,1)} %get-tuple-element.114), channel_id=1, source_target_pairs={{0,2},{2,0},{4,6},{6,4},{1,3},{3,1},{5,7},{7,5},{8,10},{10,8},{12,... | collective-permute-start | bytes 6291464 | tf_op jit(solution)/shard_map/normed_one_over_core/ppermute | solution.py:828
  214.9 62.1 %collective-permute-start.11 = (bf16[512,1024]{1,0:T(8,128)(2,1)}, bf16[512,1024]{1,0:T(8,128)(2,1)}, u32[]{:S(2)}, u32[]{:S(2)}) collective-permute-start(bf16[512,1024]{1,0:T(8,128)(2,1)} %get-tuple-element.106.refs_6_.refs_2_), channel_id=1, source_target_pairs={{0,2},{2,0},{4,6},{6,4},{1,3},{3,1},{5,7},{7,5},{8,10},{10,8},{12,... | collective-permute-start | bytes 3145736 | tf_op jit(solution)/shard_map/attended_over_core/ppermute | solution.py:828
  215.1 26.3 %collective-permute-start.10 = (bf16[512,1024]{1,0:T(8,128)(2,1)}, bf16[512,1024]{1,0:T(8,128)(2,1)}, u32[]{:S(2)}, u32[]{:S(2)}) collective-permute-start(bf16[512,1024]{1,0:T(8,128)(2,1)} %get-tuple-element.106.refs_6_.refs_2_), channel_id=1, source_target_pairs={{0,1},{1,0},{2,3},{3,2},{4,5},{5,4},{6,7},{7,6},{8,9},{9,8},{10,11... | collective-permute-start | bytes 3145736 | tf_op jit(solution)/shard_map/attended0_over_tp/ppermute | solution.py:828
  216.6 311.1 %reduce-scatter.6.cloned.1.call-start = ((), (), s32[]{:S(2)}) async-start(), calls=%async_computation.8 | async-start | bytes 3932160 | tf_op jit(solution)/shard_map/first_third_over_dp/reduce_scatter | solution.py:952
  235.2 41.7 %collective-permute-start.12 = (bf16[512,1024]{1,0:T(8,128)(2,1)}, bf16[512,1024]{1,0:T(8,128)(2,1)}, u32[]{:S(2)}, u32[]{:S(2)}) collective-permute-start(bf16[512,1024]{1,0:T(8,128)(2,1)} %get-tuple-element.109.refs_2_.refs_3_), channel_id=1, source_target_pairs={{0,2},{2,0},{4,6},{6,4},{1,3},{3,1},{5,7},{7,5},{8,10},{10,8},{12,... | collective-permute-start | bytes 3145736 | tf_op jit(solution)/shard_map/attended_over_core/ppermute | solution.py:828
  235.2 28.0 %collective-permute-start.9 = (bf16[512,1024]{1,0:T(8,128)(2,1)}, bf16[512,1024]{1,0:T(8,128)(2,1)}, u32[]{:S(2)}, u32[]{:S(2)}) collective-permute-start(bf16[512,1024]{1,0:T(8,128)(2,1)} %get-tuple-element.109.refs_2_.refs_3_), channel_id=1, source_target_pairs={{0,1},{1,0},{2,3},{3,2},{4,5},{5,4},{6,7},{7,6},{8,9},{9,8},{10,11... | collective-permute-start | bytes 3145736 | tf_op jit(solution)/shard_map/attended1_over_tp/ppermute | solution.py:828
  339.5 96.7 %collective-permute-start.23 = (bf16[512,3072]{1,0:T(8,128)(2,1)}, bf16[512,3072]{1,0:T(8,128)(2,1)}, u32[]{:S(2)}, u32[]{:S(2)}) collective-permute-start(bf16[512,3072]{1,0:T(8,128)(2,1)} %get-tuple-element.129), channel_id=1, source_target_pairs={{0,4},{4,0},{2,6},{6,2},{1,5},{5,1},{3,7},{7,3},{8,12},{12,8},{10,... | collective-permute-start | bytes 9437192 | tf_op jit(solution)/shard_map/first_third_over_x/ppermute | solution.py:828
  379.0 36.6 %collective-permute-start.19 = (bf16[1024,2048]{1,0:T(8,128)(2,1)}, bf16[1024,2048]{1,0:T(8,128)(2,1)}, u32[]{:S(2)}, u32[]{:S(2)}) collective-permute-start(bf16[1024,2048]{1,0:T(8,128)(2,1)} %get-tuple-element.126.refs_1_.refs_2_), channel_id=1, source_target_pairs={{0,2},{2,0},{4,6},{6,4},{1,3},{3,1},{5,7},{7,5},{8,10},{10,8},{12,... | collective-permute-start | bytes 12582920 | tf_op jit(solution)/shard_map/gate_back_two_over_core/ppermute | solution.py:828
  379.3 36.3 %collective-permute-start.20 = (bf16[1024,2048]{1,0:T(8,128)(2,1)}, bf16[1024,2048]{1,0:T(8,128)(2,1)}, u32[]{:S(2)}, u32[]{:S(2)}) collective-permute-start(bf16[1024,2048]{1,0:T(8,128)(2,1)} %get-tuple-element.127.refs_3_.refs_2_), channel_id=1, source_target_pairs={{0,2},{2,0},{4,6},{6,4},{1,3},{3,1},{5,7},{7,5},{8,10},{10,8},{12,... | collective-permute-start | bytes 12582920 | tf_op jit(solution)/shard_map/up_back_two_over_core/ppermute | solution.py:828
  399.7 54.9 %collective-permute-start.22 = (bf16[512,2048]{1,0:T(8,128)(2,1)}, bf16[512,2048]{1,0:T(8,128)(2,1)}, u32[]{:S(2)}, u32[]{:S(2)}) collective-permute-start(bf16[512,2048]{1,0:T(8,128)(2,1)} %nt_product.6.refs_4_.refs_2_), channel_id=1, source_target_pairs={{0,1},{1,0},{2,3},{3,2},{4,5},{5,4},{6,7},{7,6},{8,9},{9,8},{10,11... | collective-permute-start | bytes 6291464 | tf_op jit(solution)/shard_map/back0_over_tp/ppermute | solution.py:828
  414.4 113.2 %collective-permute-start.26 = (bf16[512,2048]{1,0:T(8,128)(2,1)}, bf16[512,2048]{1,0:T(8,128)(2,1)}, u32[]{:S(2)}, u32[]{:S(2)}) collective-permute-start(bf16[512,2048]{1,0:T(8,128)(2,1)} %get-tuple-element.140), channel_id=1, source_target_pairs={{0,4},{4,0},{2,6},{6,2},{1,5},{5,1},{3,7},{7,3},{8,12},{12,8},{10,... | collective-permute-start | bytes 6291464 | tf_op jit(solution)/shard_map/down_two_over_x/ppermute | solution.py:828
  435.6 67.8 %collective-permute-start.21 = (bf16[512,2048]{1,0:T(8,128)(2,1)}, bf16[512,2048]{1,0:T(8,128)(2,1)}, u32[]{:S(2)}, u32[]{:S(2)}) collective-permute-start(bf16[512,2048]{1,0:T(8,128)(2,1)} %nt_product.7.refs_2_), channel_id=1, source_target_pairs={{0,1},{1,0},{2,3},{3,2},{4,5},{5,4},{6,7},{7,6},{8,9},{9,8},{10,11... | collective-permute-start | bytes 6291464 | tf_op jit(solution)/shard_map/back1_over_tp/ppermute | solution.py:828
  440.6 189.3 %reduce-scatter.8.cloned.1.call-start = ((), (), s32[]{:S(2)}) async-start(), calls=%async_computation.9 | async-start | bytes 5242880 | tf_op jit(solution)/shard_map/down_gate_two_over_dp/reduce_scatter | solution.py:952
  453.8 62.7 %collective-permute-start.24 = (bf16[512,2048]{1,0:T(8,128)(2,1)}, bf16[512,2048]{1,0:T(8,128)(2,1)}, u32[]{:S(2)}, u32[]{:S(2)}) collective-permute-start(bf16[512,2048]{1,0:T(8,128)(2,1)} %get-tuple-element.137), channel_id=1, source_target_pairs={{0,4},{4,0},{2,6},{6,2},{1,5},{5,1},{3,7},{7,3},{8,12},{12,8},{10,... | collective-permute-start | bytes 6291464 | tf_op jit(solution)/shard_map/gate_two_over_x/ppermute | solution.py:828
  479.2 76.6 %collective-permute-start.29 = (bf16[512,2048]{1,0:T(8,128)(2,1)}, bf16[512,2048]{1,0:T(8,128)(2,1)}, u32[]{:S(2)}, u32[]{:S(2)}) collective-permute-start(bf16[512,2048]{1,0:T(8,128)(2,1)} %nt_product.8.refs_11_.refs_1_), channel_id=1, source_target_pairs={{0,1},{1,0},{2,3},{3,2},{4,5},{5,4},{6,7},{7,6},{8,9},{9,8},{10,11... | collective-permute-start | bytes 6291464 | tf_op jit(solution)/shard_map/out0_over_tp/ppermute | solution.py:828
  525.9 43.1 %collective-permute-start.30 = (bf16[512,1024]{1,0:T(8,128)(2,1)}, bf16[512,1024]{1,0:T(8,128)(2,1)}, u32[]{:S(2)}, u32[]{:S(2)}) collective-permute-start(bf16[512,1024]{1,0:T(8,128)(2,1)} %add_rows.8.refs_4_), channel_id=1, source_target_pairs={{0,4},{4,0},{2,6},{6,2},{1,5},{5,1},{3,7},{7,3},{8,12},{12,8},{10,... | collective-permute-start | bytes 3145736 | tf_op jit(solution)/shard_map/kv_grad0_over_x/ppermute | solution.py:828
  532.9 150.3 %reduce-scatter.12.cloned.1.call-start = ((), (), s32[]{:S(2)}) async-start(), calls=%async_computation.11 | async-start | bytes 1310720 | tf_op jit(solution)/shard_map/output_over_dp/reduce_scatter | solution.py:952
  543.0 34.0 %collective-permute-start.31 = (bf16[512,1024]{1,0:T(8,128)(2,1)}, bf16[512,1024]{1,0:T(8,128)(2,1)}, u32[]{:S(2)}, u32[]{:S(2)}) collective-permute-start(bf16[512,1024]{1,0:T(8,128)(2,1)} %get-tuple-element.149), channel_id=1, source_target_pairs={{0,4},{4,0},{2,6},{6,2},{1,5},{5,1},{3,7},{7,3},{8,12},{12,8},{10,... | collective-permute-start | bytes 3145736 | tf_op jit(solution)/shard_map/output_over_x/ppermute | solution.py:828
  555.2 80.8 %collective-permute-start.28 = (bf16[512,2048]{1,0:T(8,128)(2,1)}, bf16[512,2048]{1,0:T(8,128)(2,1)}, u32[]{:S(2)}, u32[]{:S(2)}) collective-permute-start(bf16[512,2048]{1,0:T(8,128)(2,1)} %nt_product.9.refs_4_.refs_1_), channel_id=1, source_target_pairs={{0,1},{1,0},{2,3},{3,2},{4,5},{5,4},{6,7},{7,6},{8,9},{9,8},{10,11... | collective-permute-start | bytes 6291464 | tf_op jit(solution)/shard_map/out1_over_tp/ppermute | solution.py:828
  575.0 57.5 %collective-permute-start.32 = (bf16[512,2048]{1,0:T(8,128)(2,1)}, bf16[512,2048]{1,0:T(8,128)(2,1)}, u32[]{:S(2)}, u32[]{:S(2)}) collective-permute-start(bf16[512,2048]{1,0:T(8,128)(2,1)} %get-tuple-element.151), channel_id=1, source_target_pairs={{0,4},{4,0},{2,6},{6,2},{1,5},{5,1},{3,7},{7,3},{8,12},{12,8},{10,... | collective-permute-start | bytes 6291464 | tf_op jit(solution)/shard_map/up_two_over_x/ppermute | solution.py:828
  585.9 89.8 %collective-permute-start.37 = (bf16[512,2048]{1,0:T(8,128)(2,1)}, bf16[512,2048]{1,0:T(8,128)(2,1)}, u32[]{:S(2)}, u32[]{:S(2)}) collective-permute-start(bf16[512,2048]{1,0:T(8,128)(2,1)} %nt_product.10.refs_12_.refs_1_.refs_2_), channel_id=1, source_target_pairs={{0,1},{1,0},{2,3},{3,2},{4,5},{5,4},{6,7},{7,6},{8,9},{9,8},{10,11... | collective-permute-start | bytes 6291464 | tf_op jit(solution)/shard_map/one0_over_tp/ppermute | solution.py:828
  618.2 27.2 %collective-permute-start.35 = (bf16[512,1024]{1,0:T(8,128)(2,1)}, bf16[512,1024]{1,0:T(8,128)(2,1)}, u32[]{:S(2)}, u32[]{:S(2)}) collective-permute-start(bf16[512,1024]{1,0:T(8,128)(2,1)} %add_rows.10.refs_4_), channel_id=1, source_target_pairs={{0,4},{4,0},{2,6},{6,2},{1,5},{5,1},{3,7},{7,3},{8,12},{12,8},{10,... | collective-permute-start | bytes 3145736 | tf_op jit(solution)/shard_map/kv_grad1_over_x/ppermute | solution.py:828
  628.7 47.0 %collective-permute-start.39 = (bf16[512,1024]{1,0:T(8,128)(2,1)}, bf16[512,1024]{1,0:T(8,128)(2,1)}, u32[]{:S(2)}, u32[]{:S(2)}) collective-permute-start(bf16[512,1024]{1,0:T(8,128)(2,1)} %get-tuple-element.160), channel_id=1, source_target_pairs={{0,4},{4,0},{2,6},{6,2},{1,5},{5,1},{3,7},{7,3},{8,12},{12,8},{10,... | collective-permute-start | bytes 3145736 | tf_op jit(solution)/shard_map/query_over_x/ppermute | solution.py:828
  632.4 91.5 %reduce-scatter.14.cloned.1.call-start = ((), (), s32[]{:S(2)}) async-start(), calls=%async_computation.12 | async-start | bytes 2621440 | tf_op jit(solution)/shard_map/up_two_over_dp/reduce_scatter | solution.py:952
  661.5 91.7 %reduce-scatter.10.cloned.1.call-start = ((), (), s32[]{:S(2)}) async-start(), calls=%async_computation.10 | async-start | bytes 2621440 | tf_op jit(solution)/shard_map/query_key_over_dp/reduce_scatter | solution.py:952
  662.3 51.5 %collective-permute-start.36 = (bf16[512,2048]{1,0:T(8,128)(2,1)}, bf16[512,2048]{1,0:T(8,128)(2,1)}, u32[]{:S(2)}, u32[]{:S(2)}) collective-permute-start(bf16[512,2048]{1,0:T(8,128)(2,1)} %nt_product.11.refs_4_.refs_1_.refs_2_), channel_id=1, source_target_pairs={{0,1},{1,0},{2,3},{3,2},{4,5},{5,4},{6,7},{7,6},{8,9},{9,8},{10,11... | collective-permute-start | bytes 6291464 | tf_op jit(solution)/shard_map/one1_over_tp/ppermute | solution.py:828
  (48 other events, 455.4 us)
Sparse Core Ops, SparseCore 0:
  12.1 133.7 all-gather.2
  216.7 127.9 all-gather.4
  440.7 60.8 reduce-scatter.5
  533.0 76.4 reduce-scatter.7
  632.5 26.9 reduce-scatter.11
  661.6 45.2 reduce-scatter.13
  709.3 43.8 reduce-scatter.9
